TPU v7x, 768 devices: a whole 4x8x12 slice. The times are simulated.
768 devices in a mesh: dp: 24 (over z, x_lo), blk: 16 (over x_hi, y), tensor: 2 (over core).
Axes of the slice: x: 4 (x_hi: 2, x_lo: 2; x = x_hi * 2 + x_lo), y: 8, z: 12, core: 2. Of those that a mesh axis runs over, the one named last changes fastest.
Arguments:
- activations: bfloat16 [98304, 8192], P(('dp', 'blk')), may hold values from -6 to 6
- norm_gain: float32 [8192], replicated, may hold values from 0.5 to 1.5
- key_weight: bfloat16 [8192, 512], P('blk', 'tensor'), may hold values from -0.0625 to 0.0625
- key_grad: bfloat16 [98304, 512], P(('dp', 'blk'), 'tensor'), may hold values from -6 to 6
- doc_lengths: int32 [384, 4], P(('dp', 'blk')), may hold values from 1 to 128, 256 in all within a row
Outputs:
- weight_grad: float32 [8192, 512], P('blk', 'tensor')
- normed_grad: bfloat16 [98304, 8192], P(('dp', 'blk'), 'tensor')
Inputs may be any that keep to these rules, and one draw needn't show every extreme that they name: `doc_lengths`: each row sums to 256, and its longest document has exactly 128 tokens.
All inputs are finite; a program needn't handle non-finite values.
Results may differ from a plain program's by a relative error of at most 0.0057.
Values may be sent and summed in bfloat16 or wider, within the bound.
No kernel may reach another device: no remote copies, remote signals or barrier semaphores. Data moves between devices by JAX's collectives and lax.ppermute only.
A program may use at most 64 MiB of HBM per device.

v0:
```python
import math

import jax
import jax.numpy as jnp
from jax import lax
from jax.sharding import PartitionSpec as P

HS = 128


def positions(length_row, tok_rows):
    starts = jnp.cumsum(length_row) - length_row
    token_index = jnp.arange(tok_rows, dtype=jnp.int32)
    doc_first = jnp.max(
        jnp.where(starts[None, :] <= token_index[:, None], starts[None, :], 0), axis=1
    )
    return token_index - doc_first


def normalize(act_block, norm_gain):
    widened = act_block.astype(jnp.float32)
    mean_square = jnp.mean(widened * widened, axis=-1, keepdims=True)
    return (widened * lax.rsqrt(mean_square + 1e-06) * norm_gain).astype(jnp.bfloat16)


def rope_back(grad_block, token_pos, head_count, head_size):
    half_size = head_size // 2
    frequency = jnp.exp(
        jnp.arange(half_size, dtype=jnp.float32) * (-2.0 * math.log(1000000.0) / head_size)
    )
    angles = token_pos.astype(jnp.float32)[:, None] * frequency[None, :]
    cosine = jnp.cos(angles)[:, None, :]
    sine_part = jnp.sin(angles)[:, None, :]
    grad_heads = grad_block.astype(jnp.float32).reshape(grad_block.shape[0], head_count, head_size)
    first_half = grad_heads[..., :half_size]
    second_half = grad_heads[..., half_size:]
    rotated = jnp.concatenate(
        [
            first_half * cosine + second_half * sine_part,
            second_half * cosine - first_half * sine_part,
        ],
        axis=-1,
    )
    return rotated.reshape(grad_block.shape[0], head_count * head_size).astype(jnp.bfloat16)


def per_device(activations, norm_gain, key_weight, key_grad, doc_lengths):
    tok_rows = activations.shape[0]
    head_count = key_grad.shape[1] // HS
    normed = normalize(activations, norm_gain)
    rotated = rope_back(key_grad, positions(doc_lengths[0], tok_rows), head_count, HS)
    contract_rows = (((0,), (0,)), ((), ()))
    contract_cols = (((1,), (1,)), ((), ()))
    grad_term = lax.dot_general(normed, rotated, contract_rows, preferred_element_type=jnp.float32)
    grad_shard = lax.psum_scatter(grad_term, "blk", scatter_dimension=0, tiled=True)
    weight_grad = lax.psum(grad_shard, "dp") / lax.axis_size("dp")
    gathered = lax.all_gather(key_weight, "blk", axis=0, tiled=True)
    partial_value = lax.dot_general(
        rotated, gathered, contract_cols, preferred_element_type=jnp.float32
    )
    normed_grad = lax.psum_scatter(
        partial_value.astype(jnp.bfloat16), "tensor", scatter_dimension=1, tiled=True
    )
    return (weight_grad, normed_grad)


def solution(mesh):
    placed = (
        P(("dp", "blk"), None),
        P(),
        P("blk", "tensor"),
        P(("dp", "blk"), "tensor"),
        P(("dp", "blk"), None),
    )
    return jax.shard_map(
        per_device,
        mesh=mesh,
        in_specs=placed,
        out_specs=(P("blk", "tensor"), P(("dp", "blk"), "tensor")),
        check_vma=False,
    )
```

profile of v0, /device:TPU:1, one launch (start us, length us, event | category | flops | bytes accessed | tf_op | source)
XLA Modules:
  0.0 612.9 jit_solution(14415078808331574014)
XLA Ops:
  7.2 0.0 copy-start.1
  7.2 0.0 reduce-scatter.3.cloned.1.call-start
  7.2 0.8 reduce-window_clone.1
  8.1 0.7 subtract_bitcast_fusion
  8.7 0.1 select_reduce_fusion
  8.8 1.0 reshape.89
  9.9 0.0 copy-start
  9.9 3.3 fusion
  13.1 0.5 multiply_cosine_fusion
  13.7 0.5 add_convert_fusion
  14.2 0.4 pad_maximum_fusion
  14.5 0.0 copy-done.1
  14.5 0.0 copy-done
  14.5 4.9 fusion.3
  19.4 0.0 reduce-scatter.3.cloned.1.call-update
  19.5 0.0 all-gather.2.cloned.1.call-start
  19.5 0.7 all-gather.2.cloned.1.call-update
  20.2 0.0 all-reduce.2.cloned.1.call-start
  20.3 236.5 %reduce-scatter.3.cloned.1.call-done = f32[512,256]{1,0:T(8,128)} async-done(((f32[8192,256]{1,0:T(8,128)}), f32[512,256]{1,0:T(8,128)}) %reduce-scatter.3.cloned.1.call-update) | async-done | bytes 524304 | tf_op jit(solution)/shard_map/reduce_scatter | solution.py:55
  256.8 0.0 all-reduce.2.cloned.1.call-update
  256.8 0.0 reduce-scatter.5.cloned.1.call-start
  256.9 114.1 %all-gather.2.cloned.1.call-done = bf16[8192,256]{1,0:T(8,128)(2,1)} async-done(((bf16[512,256]{1,0:T(8,128)(2,1)}), bf16[8192,256]{1,0:T(8,128)(2,1)}) %all-gather.2.cloned.1.call-update) | async-done | bytes 4194320 | tf_op jit(solution)/shard_map/all_gather | solution.py:57
  371.0 5.4 convolution_convert_fusion
  376.4 0.0 reduce-scatter.5.cloned.1.call-update
  376.4 188.8 %all-reduce.2.cloned.1.call-done = f32[512,256]{1,0:T(8,128)} async-done(((f32[512,256]{1,0:T(8,128)}), f32[512,256]{1,0:T(8,128)}) %all-reduce.2.cloned.1.call-update) | async-done | bytes 524304 | tf_op jit(solution)/shard_map/psum | solution.py:56
  565.2 1.9 broadcast_multiply_fusion
  567.0 39.4 %reduce-scatter.5.cloned.1.call-done = bf16[256,4096]{1,0:T(8,128)(2,1)} async-done(((bf16[256,8192]{1,0:T(8,128)(2,1)}), bf16[256,4096]{1,0:T(8,128)(2,1)}) %reduce-scatter.5.cloned.1.call-update) | async-done | bytes 2097168 | tf_op jit(solution)/shard_map/reduce_scatter | solution.py:61
  (3 shorter events, 0.0 us)
Async XLA Ops:
  7.2 7.4 %copy-start.1 = (f32[8192]{0:T(1024)S(1)}, f32[8192]{0:T(1024)}, u32[]{:S(2)}) copy-start(f32[8192]{0:T(1024)} %param.6) | copy-start | bytes 98308
  7.2 249.6 %reduce-scatter.3.cloned.1.call-start = ((), (), s32[]{:S(2)}) async-start(), calls=%async_computation.2 | async-start | bytes 8912896 | tf_op jit(solution)/shard_map/reduce_scatter | solution.py:55
  9.9 4.7 copy-start
  19.5 351.5 %all-gather.2.cloned.1.call-start = ((), (), s32[]{:S(2)}) async-start(), calls=%async_computation.4 | async-start | bytes 4456448 | tf_op jit(solution)/shard_map/all_gather | solution.py:57
  20.2 544.9 %all-reduce.2.cloned.1.call-start = ((), (), s32[]{:S(2)}) async-start(), calls=%async_computation.3 | async-start | bytes 1048576 | tf_op jit(solution)/shard_map/psum | solution.py:56
  256.8 349.6 %reduce-scatter.5.cloned.1.call-start = ((), (), s32[]{:S(2)}) async-start(), calls=%async_computation.5 | async-start | bytes 6291456 | tf_op jit(solution)/shard_map/reduce_scatter | solution.py:61
Sparse Core Ops, SparseCore 0:
  19.6 237.1 reduce-scatter.2
  260.5 110.3 all-gather.1
  374.2 190.9 all-reduce.1
  569.0 37.3 reduce-scatter.4
where the time goes:
time: 613 us
  waiting for transfers between devices  579 us (94%)
  between operations  13.8 us (2%)
  matrix products  10.3 us (2%)
  other arithmetic  8.1 us (1%)
    reduce_scatter x1, waiting for transfers between devices, per_device(): lax.psum_scatter(grad_term, 'blk', scatter_dimension=0, tiled=True)  237 us
    psum x1, waiting for transfers between devices, per_device(): weight_grad = lax.psum(grad_shard, 'dp') / lax.axis_size('dp')  189 us
    all_gather x1, waiting for transfers between devices, per_device(): gathered = lax.all_gather(key_weight, 'blk', axis=0, tiled=True)  114 us
    reduce_scatter x1, waiting for transfers between devices, per_device(): lax.psum_scatter(partial_value.astype(jnp.bfloat16), 'tensor', scatter_di...  39.4 us
  transfers between devices with their start and end apart: 4, of which 4 were waited for; matrix products, arithmetic and copies ran while one was open for 1% of the time, Pallas kernels for 0%

commit v1 on v0

v1 whole, which is shorter than its diff:
```python
import functools
import math

import jax
import jax.numpy as jnp
from jax import lax
from jax.experimental import pallas as pl
from jax.experimental.pallas import tpu as pltpu
from jax.sharding import Mesh, PartitionSpec as P

NZ, NX, NY, NT = 12, 2, 8, 2
TOK, D, HS, COLS = 256, 8192, 128, 256
QUART = 128
FEAT = NY * QUART
KV = NT * COLS
ZROWS = 48
VMEM = 48 * 1024 * 1024
BF16, F32 = jnp.bfloat16, jnp.float32


def prep_kernel(place, doc, act, gain, key_grad, freq, *outs):
    xl, xh, t = place[0], place[1], place[2]
    rows = act.shape[0]
    square = jnp.zeros((rows, 128), F32)
    for j in range(D // 128):
        v = act[:, j * 128 : (j + 1) * 128].astype(F32)
        square = square + v * v
    scale = lax.rsqrt(jnp.sum(square, axis=1, keepdims=True) * (1.0 / D) + 1e-06)

    token = pl.program_id(0) * rows + lax.broadcasted_iota(jnp.int32, (rows, 128), 0)
    second = doc[0, 0]
    third = second + doc[0, 1]
    fourth = third + doc[0, 2]
    first = jnp.where(
        token >= fourth,
        fourth,
        jnp.where(token >= third, third, jnp.where(token >= second, second, 0)),
    )
    angle = (token - first).astype(F32) * freq[...]
    cosine = jnp.cos(angle)
    lane = lax.broadcasted_iota(jnp.int32, (rows, 128), 1)
    sine = jnp.sin(angle)
    sine = jnp.where(lane < HS // 2, sine, -sine)
    rotated = []
    for h in range(COLS // HS):
        v = key_grad[:, h * HS : (h + 1) * HS].astype(F32)
        rotated.append((v * cosine + pltpu.roll(v, HS // 2, 1) * sine).astype(BF16))

    for k, out in enumerate(outs):
        a, b = k & 1, k >> 1
        base = (xh ^ a) * (D // 2) + (2 * (xl ^ b) + t) * QUART
        for j in range(NY):
            at = pl.ds(pl.multiple_of(base + j * 4 * QUART, 128), QUART)
            v = act[:, at].astype(F32) * scale * gain[:, at]
            out[:, j * QUART : (j + 1) * QUART] = v.astype(BF16)
        for h, v in enumerate(rotated):
            out[:, FEAT + h * HS : FEAT + (h + 1) * HS] = v


def grad_kernel(place, b0, b1, b2, b3, other, out):
    t = place[2]
    blocks = (b0, b1, b2, b3)
    normed = jnp.concatenate([b[:, :FEAT] for b in blocks], axis=0)
    own = jnp.concatenate([b[:, FEAT:] for b in blocks], axis=0)
    for half, rot in ((t, own), (1 - t, other[...])):
        g = lax.dot_general(rot, normed, (((0,), (0,)), ((), ())), preferred_element_type=F32)
        g = g.astype(BF16)
        for y in range(NY):
            out[y, pl.ds(pl.multiple_of(half * COLS, COLS), COLS), :] = g[
                :, y * QUART : (y + 1) * QUART
            ]


def input_kernel(place, b0, b1, b2, b3, other, weight, *outs):
    t, swap = place[2], (place[1] ^ place[2]) == 1
    blocks = (b0, b1, b2, b3)
    lhs = []
    for r in range(4):
        own = jnp.where(swap, blocks[r ^ 1][:, FEAT:], blocks[r][:, FEAT:])
        oth = jnp.where(
            swap, other[(r ^ 1) * TOK : ((r ^ 1) + 1) * TOK, :], other[r * TOK : (r + 1) * TOK, :]
        )
        lhs.append(jnp.concatenate([own, oth], axis=1))
    lhs = jnp.concatenate(lhs, axis=0)
    for j in range(NY // 2):
        rhs = jnp.concatenate(
            [
                jnp.concatenate([weight[y, t], weight[y, 1 - t]], axis=1)
                for y in (2 * j, 2 * j + 1)
            ],
            axis=0,
        )
        p = lax.dot_general(lhs, rhs, (((1,), (1,)), ((), ())), preferred_element_type=F32)
        p = p.astype(BF16)
        for r, out in enumerate(outs):
            out[:, j * 2 * QUART : (j + 1) * 2 * QUART] = p[r * TOK : (r + 1) * TOK, :]


def place_kernel(place, r0, r1, r2, r3, out):
    mine = 2 * place[0] + place[1]
    for r, got in enumerate((r0, r1, r2, r3)):
        q = mine ^ r
        for y in range(NY):
            at = pl.ds(pl.multiple_of(y * 4 * QUART + q * QUART, QUART), QUART)
            out[:, at] = got[:, y * QUART : (y + 1) * QUART]


def whole(count):
    return [pl.BlockSpec(memory_space=pltpu.VMEM)] * count


SCALARS = pl.BlockSpec(memory_space=pltpu.SMEM)
PARAMS = pltpu.CompilerParams(vmem_limit_bytes=VMEM)


def per_device(activations, norm_gain, key_weight, key_grad, doc_lengths):
    xl, xh, t = lax.axis_index("xl"), lax.axis_index("xh"), lax.axis_index("t")
    place = jnp.stack([xl, xh, t]).astype(jnp.int32)
    half = jnp.arange(HS, dtype=jnp.int32) % (HS // 2)
    freq = jnp.exp(half.astype(F32) * (-2.0 * math.log(1000000.0) / HS))[None, :]

    rows = 64
    sent = jax.ShapeDtypeStruct((TOK, FEAT + COLS), BF16)
    blocks = pl.pallas_call(
        prep_kernel,
        grid=(TOK // rows,),
        in_specs=[
            SCALARS,
            SCALARS,
            pl.BlockSpec((rows, D), lambda i: (i, 0)),
            pl.BlockSpec((1, D), lambda i: (0, 0)),
            pl.BlockSpec((rows, COLS), lambda i: (i, 0)),
            pl.BlockSpec((1, HS), lambda i: (0, 0)),
        ],
        out_specs=[pl.BlockSpec((rows, FEAT + COLS), lambda i: (i, 0))] * 4,
        out_shape=[sent] * 4,
        compiler_params=PARAMS,
        name="prep",
    )(place, doc_lengths, activations, norm_gain[None, :], key_grad, freq)

    got = [blocks[0]] + [
        lax.ppermute(blocks[k], ("xl", "xh"), [(i, i ^ k) for i in range(4)]) for k in (1, 2, 3)
    ]

    shard = lax.dynamic_slice_in_dim(key_weight, xl * 2 * QUART, 2 * QUART, 0)
    shard = shard.reshape(1, NT, QUART, COLS)
    shard = jnp.broadcast_to(shard, (NY, NT, QUART, COLS)).reshape(NY * NT, QUART, COLS)
    weight = lax.all_to_all(shard, ("y", "t"), 0, 0, tiled=True).reshape(NY, NT, QUART, COLS)

    mine = jnp.concatenate([b[:, FEAT:] for b in got], axis=0)
    other = lax.ppermute(mine, "t", [(0, 1), (1, 0)])

    products = pl.pallas_call(
        input_kernel,
        in_specs=[SCALARS] + whole(6),
        out_specs=whole(4),
        out_shape=[jax.ShapeDtypeStruct((TOK, FEAT), BF16)] * 4,
        compiler_params=PARAMS,
        name="input_grad",
    )(place, *got, other, weight)

    returned = []
    for r in range(4):
        r0, r1 = r >> 1, r & 1
        pairs = [
            (4 * i + 2 * j + k, 4 * (i ^ r0) + 2 * (k ^ r1) + j)
            for i in range(2)
            for j in range(2)
            for k in range(2)
        ]
        returned.append(lax.ppermute(products[r], ("xl", "xh", "t"), pairs))

    term = pl.pallas_call(
        grad_kernel,
        in_specs=[SCALARS] + whole(5),
        out_specs=whole(1)[0],
        out_shape=jax.ShapeDtypeStruct((NY, KV, QUART), BF16),
        compiler_params=PARAMS,
        name="weight_grad",
    )(place, *got, other)

    term = lax.all_to_all(term, "y", 0, 0, tiled=True)
    term = jnp.sum(term.astype(F32), axis=0)
    term = jnp.pad(term, ((0, NZ * ZROWS - KV), (0, 0))).astype(BF16).reshape(NZ, ZROWS, QUART)
    term = lax.all_to_all(term, "z", 0, 0, tiled=True)
    term = jnp.sum(term.astype(F32), axis=0) * (1.0 / (NZ * NX))
    term = lax.all_gather(term, "z", axis=0, tiled=True)[:KV]
    term = jnp.broadcast_to(term.reshape(1, NT, COLS, QUART), (NX, NT, COLS, QUART))
    term = lax.all_to_all(term.reshape(NX * NT, COLS, QUART), ("xl", "t"), 0, 0, tiled=True)
    weight_grad = jnp.swapaxes(term, 1, 2).reshape(NX * NT * QUART, COLS)

    normed_grad = pl.pallas_call(
        place_kernel,
        grid=(TOK // rows,),
        in_specs=[SCALARS] + [pl.BlockSpec((rows, FEAT), lambda i: (i, 0))] * 4,
        out_specs=pl.BlockSpec((rows, 4 * FEAT), lambda i: (i, 0)),
        out_shape=jax.ShapeDtypeStruct((TOK, 4 * FEAT), BF16),
        compiler_params=PARAMS,
        name="placed",
    )(place, *returned)
    return (weight_grad, normed_grad)


def solution(mesh):
    fine = Mesh(mesh.devices.reshape(NZ, NX, 2, NY, NT), ("z", "xl", "xh", "y", "t"))
    tokens = ("z", "xl", "xh", "y")
    return jax.shard_map(
        per_device,
        mesh=fine,
        in_specs=(
            P(tokens, None),
            P(),
            P(("xh", "y"), "t"),
            P(tokens, "t"),
            P(tokens, None),
        ),
        out_specs=(P(("xh", "y"), "t"), P(tokens, "t")),
        check_vma=False,
    )
```

time: 613 us -> 192 us (0.31)
  waiting for transfers between devices: 579 us -> 80.2 us
  starting transfers between devices: 0.16 us -> 68.3 us
  blocking collectives: 0 us -> 20.3 us
  Pallas kernels: 0 us -> 13.4 us
  between operations: 13.8 us -> 0.82 us
  matrix products: 10.3 us -> 0 us
    reduce_scatter x2 -> x0, waiting for transfers between devices: 276 us -> none  [the longest x1 237 us: per_device(): lax.psum_scatter(grad_term, 'blk', scatter_dimension=0, tiled=True)]
    psum x1 -> x0, waiting for transfers between devices: 189 us -> none  [per_device(): weight_grad = lax.psum(grad_shard, 'dp') / lax.axis_size('dp')]
    all_gather x1 -> x0, waiting for transfers between devices: 114 us -> none  [per_device(): gathered = lax.all_gather(key_weight, 'blk', axis=0, tiled=True)]
    all_to_all x0 -> x4, waiting for transfers between devices: none -> 60.7 us  [the longest x1 29.3 us: per_device(): term = lax.all_to_all(term, 'y', 0, 0, tiled=True)]
    ppermute x0 -> x8, starting transfers between devices: none -> 34.9 us  [the longest x4 12.9 us: per_device(): returned.append(lax.ppermute(products[r], ('xl', 'xh', 't'), pairs))]
    all_to_all x0 -> x4, starting transfers between devices: none -> 33.5 us  [the longest x1 14.9 us: per_device(): term = lax.all_to_all(term, 'z', 0, 0, tiled=True)]
    all_gather x0 -> x1, blocking collectives: none -> 20.3 us  [per_device(): term = lax.all_gather(term, 'z', axis=0, tiled=True)[:KV]]
    ppermute x0 -> x8, waiting for transfers between devices: none -> 19.5 us  [the longest x3 18 us: per_device(): lax.ppermute(blocks[k], ('xl', 'xh'), [(i, i ^ k) for i in range(4)])]
  transfers between devices with their start and end apart: 4 -> 12, of which waited for: 4 -> 7; matrix products, arithmetic and copies ran while one was open for 1% -> 2% of each run, Pallas kernels for 0% -> 3%
where the time goes in v1:
time: 192 us; the launch traced here: 191 us
  waiting for transfers between devices  80.2 us (42%)
  starting transfers between devices  68.3 us (36%)
  blocking collectives  20.3 us (11%)
  Pallas kernels  13.4 us (7%)
  local copies, waits for them, and re-layouts  5.9 us (3%)
  other arithmetic  2.44 us (1%)
    all_to_all x1, waiting for transfers between devices, per_device(): term = lax.all_to_all(term, 'y', 0, 0, tiled=True)  29.3 us
    all_to_all x1, waiting for transfers between devices, per_device(): lax.all_to_all(shard, ('y', 't'), 0, 0, tiled=True)  26 us
    all_gather x1, blocking collectives, per_device(): term = lax.all_gather(term, 'z', axis=0, tiled=True)[:KV]  20.3 us
    ppermute x3, waiting for transfers between devices, per_device(): lax.ppermute(blocks[k], ('xl', 'xh'), [(i, i ^ k) for i in range(4)])  18 us
    all_to_all x1, starting transfers between devices, per_device(): term = lax.all_to_all(term, 'z', 0, 0, tiled=True)  14.9 us
    ppermute x4, starting transfers between devices, per_device(): returned.append(lax.ppermute(products[r], ('xl', 'xh', 't'), pairs))  12.9 us
    ppermute x1, starting transfers between devices, per_device(): other = lax.ppermute(mine, 't', [(0, 1), (1, 0)])  11.7 us
    ppermute x3, starting transfers between devices, per_device(): lax.ppermute(blocks[k], ('xl', 'xh'), [(i, i ^ k) for i in range(4)])  10.2 us
  transfers between devices with their start and end apart: 12, of which 7 were waited for; matrix products, arithmetic and copies ran while one was open for 2% of the time, Pallas kernels for 3%

profile of v1, /device:TPU:1, one launch (start us, length us, event | category | flops | bytes accessed | tf_op | source)
XLA Modules:
  0.0 191.3 jit_solution(7395070160613210158)
XLA Ops:
  0.6 0.0 copy-start
  0.7 0.1 pad_add_fusion.place
  0.7 0.0 copy-start.1
  0.7 0.9 copy-done.1
  1.7 0.0 copy-start.2
  1.7 0.8 copy-done.2
  2.4 0.0 copy-start.3
  2.4 0.7 copy-done.3
  3.1 4.3 %prep.1 = (bf16[256,1280]{1,0:T(8,128)(2,1)S(1)}, bf16[256,1280]{1,0:T(8,128)(2,1)S(1)}, bf16[256,1280]{1,0:T(8,128)(2,1)S(1)}, bf16[256,1280]{1,0:T(8,128)(2,1)S(1)}) custom-call(s32[3]{0:T(128)S(1)} %pad_add_fusion.place, s32[1,4]{1,0:T(1,128)S(1)} %copy-done.3, bf16[256,8192]{1,0:T(8,128)(2,1)} %act.1, f32[1,8192]{1,0:T(1,128)S(1)} %bitcast.13, ...), custom_call_target="tpu_custom_call" | custom-call | tf_op jit(solution)/shard_map/prep/pallas_call | solution.py:124
  7.4 5.2 %collective-permute-start.2 = (bf16[256,1280]{1,0:T(8,128)(2,1)S(1)}, bf16[256,1280]{1,0:T(8,128)(2,1)S(1)}, u32[]{:S(2)}, u32[]{:S(2)}) collective-permute-start(bf16[256,1280]{1,0:T(8,128)(2,1)S(1)} %get-tuple-element.13), channel_id=1, source_target_pairs={{0,48},{16,32},{32,16},{48,0},{1,49},{17,33},{33,17},{49,1},{2,50}... | collective-permute-start | bytes 1966088 | tf_op jit(solution)/shard_map/ppermute | solution.py:142
  12.6 1.9 %collective-permute-start.1 = (bf16[256,1280]{1,0:T(8,128)(2,1)S(1)}, bf16[256,1280]{1,0:T(8,128)(2,1)S(1)}, u32[]{:S(2)}, u32[]{:S(2)}) collective-permute-start(bf16[256,1280]{1,0:T(8,128)(2,1)S(1)} %get-tuple-element.12), channel_id=1, source_target_pairs={{0,32},{16,48},{32,0},{48,16},{1,33},{17,49},{33,1},{49,17},{2,34}... | collective-permute-start | bytes 1966088 | tf_op jit(solution)/shard_map/ppermute | solution.py:142
  14.5 3.1 %collective-permute-start = (bf16[256,1280]{1,0:T(8,128)(2,1)S(1)}, bf16[256,1280]{1,0:T(8,128)(2,1)S(1)}, u32[]{:S(2)}, u32[]{:S(2)}) collective-permute-start(bf16[256,1280]{1,0:T(8,128)(2,1)S(1)} %get-tuple-element.11), channel_id=1, source_target_pairs={{0,16},{16,0},{32,48},{48,32},{1,17},{17,1},{33,49},{49,33},{2,18}... | collective-permute-start | bytes 1966088 | tf_op jit(solution)/shard_map/ppermute | solution.py:142
  17.7 2.9 %collective-permute-done.2.b3 = bf16[256,1280]{1,0:T(8,128)(2,1)S(1)} collective-permute-done((bf16[256,1280]{1,0:T(8,128)(2,1)S(1)}, bf16[256,1280]{1,0:T(8,128)(2,1)S(1)}, u32[]{:S(2)}, u32[]{:S(2)}) %collective-permute-start.2) | collective-permute-done | bytes 655392 | tf_op jit(solution)/shard_map/ppermute | solution.py:142
  20.6 3.7 %collective-permute-done.1.b2 = bf16[256,1280]{1,0:T(8,128)(2,1)S(1)} collective-permute-done((bf16[256,1280]{1,0:T(8,128)(2,1)S(1)}, bf16[256,1280]{1,0:T(8,128)(2,1)S(1)}, u32[]{:S(2)}, u32[]{:S(2)}) %collective-permute-start.1) | collective-permute-done | bytes 655392 | tf_op jit(solution)/shard_map/ppermute | solution.py:142
  24.3 11.4 %collective-permute-done.b1 = bf16[256,1280]{1,0:T(8,128)(2,1)S(1)} collective-permute-done((bf16[256,1280]{1,0:T(8,128)(2,1)S(1)}, bf16[256,1280]{1,0:T(8,128)(2,1)S(1)}, u32[]{:S(2)}, u32[]{:S(2)}) %collective-permute-start) | collective-permute-done | bytes 655392 | tf_op jit(solution)/shard_map/ppermute | solution.py:142
  35.7 11.7 %collective-permute-start.3 = (bf16[1024,256]{1,0:T(8,128)(2,1)S(1)}, bf16[1024,256]{1,0:T(8,128)(2,1)S(1)}, u32[]{:S(2)}, u32[]{:S(2)}) collective-permute-start(bf16[1024,256]{1,0:T(8,128)(2,1)S(1)} %pad_maximum_fusion), channel_id=1, source_target_pairs={{0,1},{1,0},{2,3},{3,2},{4,5},{5,4},{6,7},{7,6},{8,9},{9,8},{10,11... | collective-permute-start | bytes 1572872 | tf_op jit(solution)/shard_map/ppermute | solution.py:151
  47.5 1.5 collective-permute-done.3.other
  49.0 2.8 %weight_grad.1 = bf16[8,512,128]{2,1,0:T(8,128)(2,1)} custom-call(s32[3]{0:T(128)S(1)} %pad_add_fusion.place, bf16[256,1280]{1,0:T(8,128)(2,1)S(1)} %get-tuple-element.10.b0, bf16[256,1280]{1,0:T(8,128)(2,1)S(1)} %collective-permute-done.b1, bf16[256,1280]{1,0:T(8,128)(2,1)S(1)} %collective-permute-done.1.b2, ...), custom_call_target="tpu_custom_call" | custom-call | tf_op jit(solution)/shard_map/weight_grad/pallas_call | solution.py:173
  51.8 7.0 %all-to-all-start = ((bf16[8,512,128]{2,1,0:T(8,128)(2,1)}), bf16[8,512,128]{2,1,0:T(8,128)(2,1)}, u32[]{:S(2)}, u32[]{:S(2)}) async-start(bf16[8,512,128]{2,1,0:T(8,128)(2,1)} %weight_grad.1), calls=%async_computation | async-start | bytes 2097152 | tf_op jit(solution)/shard_map/all_to_all | solution.py:182
  58.7 0.0 copy-done
  58.8 29.3 %all-to-all-done = bf16[8,512,128]{2,1,0:T(8,128)(2,1)} async-done(((bf16[8,512,128]{2,1,0:T(8,128)(2,1)}), bf16[8,512,128]{2,1,0:T(8,128)(2,1)}, u32[]{:S(2)}, u32[]{:S(2)}) %all-to-all-start) | async-done | bytes 1048608 | tf_op jit(solution)/shard_map/all_to_all | solution.py:182
  88.1 1.1 broadcast_in_dim.22
  89.1 4.6 %all-to-all-start.3 = ((bf16[16,128,256]{2,1,0:T(8,128)(2,1)}), bf16[16,128,256]{2,1,0:T(8,128)(2,1)}, u32[]{:S(2)}, u32[]{:S(2)}) async-start(bf16[16,128,256]{2,1,0:T(8,128)(2,1)} %bitcast.14), calls=%async_computation.3 | async-start | bytes 2097152 | tf_op jit(solution)/shard_map/all_to_all | solution.py:148
  93.7 1.4 reduce
  95.1 0.7 pad.5
  95.8 26.0 %all-to-all-done.3 = bf16[16,128,256]{2,1,0:T(8,128)(2,1)} async-done(((bf16[16,128,256]{2,1,0:T(8,128)(2,1)}), bf16[16,128,256]{2,1,0:T(8,128)(2,1)}, u32[]{:S(2)}, u32[]{:S(2)}) %all-to-all-start.3) | async-done | bytes 1048608 | tf_op jit(solution)/shard_map/all_to_all | solution.py:148
  121.8 14.9 %all-to-all-start.1 = ((bf16[12,48,128]{2,1,0:T(8,128)(2,1)}), bf16[12,48,128]{2,1,0:T(8,128)(2,1)}, u32[]{:S(2)}, u32[]{:S(2)}) async-start(bf16[12,48,128]{2,1,0:T(8,128)(2,1)} %bitcast.17), calls=%async_computation.1 | async-start | bytes 294912 | tf_op jit(solution)/shard_map/all_to_all | solution.py:185
  136.7 3.7 %input_grad.1 = (bf16[256,1024]{1,0:T(8,128)(2,1)}, bf16[256,1024]{1,0:T(8,128)(2,1)}, bf16[256,1024]{1,0:T(8,128)(2,1)}, bf16[256,1024]{1,0:T(8,128)(2,1)}) custom-call(s32[3]{0:T(128)S(1)} %pad_add_fusion.place, bf16[256,1280]{1,0:T(8,128)(2,1)S(1)} %get-tuple-element.10.b0, bf16[256,1280]{1,0:T(8,128)(2,1)S(1)} %collective-permute-done.b1, ...), custom_call_target="tpu_custom_call" | custom-call | tf_op jit(solution)/shard_map/input_grad/pallas_call | solution.py:153
  140.4 2.5 %collective-permute-start.4 = (bf16[256,1024]{1,0:T(8,128)(2,1)}, bf16[256,1024]{1,0:T(8,128)(2,1)S(1)}, u32[]{:S(2)}, u32[]{:S(2)}) collective-permute-start(bf16[256,1024]{1,0:T(8,128)(2,1)} %get-tuple-element.14), channel_id=1, source_target_pairs={{0,0},{1,16},{16,1},{17,17},{32,32},{33,48},{48,33},{49,49},{2,2},... | collective-permute-start | bytes 1572872 | tf_op jit(solution)/shard_map/ppermute | solution.py:171
  142.9 1.9 %collective-permute-start.5 = (bf16[256,1024]{1,0:T(8,128)(2,1)}, bf16[256,1024]{1,0:T(8,128)(2,1)S(1)}, u32[]{:S(2)}, u32[]{:S(2)}) collective-permute-start(bf16[256,1024]{1,0:T(8,128)(2,1)} %get-tuple-element.15), channel_id=1, source_target_pairs={{0,16},{1,0},{16,17},{17,1},{32,48},{33,32},{48,49},{49,33},{2,18}... | collective-permute-start | bytes 1572872 | tf_op jit(solution)/shard_map/ppermute | solution.py:171
  144.8 4.0 %collective-permute-start.6 = (bf16[256,1024]{1,0:T(8,128)(2,1)}, bf16[256,1024]{1,0:T(8,128)(2,1)S(1)}, u32[]{:S(2)}, u32[]{:S(2)}) collective-permute-start(bf16[256,1024]{1,0:T(8,128)(2,1)} %get-tuple-element.16), channel_id=1, source_target_pairs={{0,32},{1,48},{16,33},{17,49},{32,0},{33,16},{48,1},{49,17},{2,34}... | collective-permute-start | bytes 1572872 | tf_op jit(solution)/shard_map/ppermute | solution.py:171
  148.8 4.5 %collective-permute-start.7 = (bf16[256,1024]{1,0:T(8,128)(2,1)}, bf16[256,1024]{1,0:T(8,128)(2,1)S(1)}, u32[]{:S(2)}, u32[]{:S(2)}) collective-permute-start(bf16[256,1024]{1,0:T(8,128)(2,1)} %get-tuple-element.17), channel_id=1, source_target_pairs={{0,48},{1,32},{16,49},{17,33},{32,16},{33,0},{48,17},{49,1},{2,50}... | collective-permute-start | bytes 1572872 | tf_op jit(solution)/shard_map/ppermute | solution.py:171
  153.3 0.0 all-to-all-done.1
  153.3 0.9 convert_reduce_fusion
  154.2 20.3 %all_gather.3 = f32[576,128]{1,0:T(8,128)S(1)} all-gather(f32[48,128]{1,0:T(8,128)S(1)} %broadcast_multiply_fusion), channel_id=1, replica_groups=mesh['z'=12,'xl'=2,'xh'=2,'y'=8,'t'=2] {'z'}, dimensions={0}, use_global_device_ids=true | all-gather | bytes 319488 | tf_op jit(solution)/shard_map/all_gather | solution.py:187
  174.5 0.1 copy.8
  174.7 0.8 broadcast_in_dim.20
  175.5 7.1 %all-to-all-start.2 = ((f32[4,256,128]{1,2,0:T(8,128)}), f32[4,256,128]{1,2,0:T(8,128)S(1)}, u32[]{:S(2)}, u32[]{:S(2)}) async-start(f32[4,256,128]{1,2,0:T(8,128)} %bitcast.6), calls=%async_computation.2 | async-start | bytes 1048576 | tf_op jit(solution)/shard_map/all_to_all | solution.py:189
  182.6 0.0 collective-permute-done.4.r0
  182.6 0.0 collective-permute-done.5.r1
  182.6 0.0 collective-permute-done.6.r2
  182.6 0.0 collective-permute-done.7.r3
  182.6 2.6 %placed.1 = bf16[256,4096]{1,0:T(8,128)(2,1)} custom-call(s32[3]{0:T(128)S(1)} %pad_add_fusion.place, bf16[256,1024]{1,0:T(8,128)(2,1)S(1)} %collective-permute-done.4.r0, bf16[256,1024]{1,0:T(8,128)(2,1)S(1)} %collective-permute-done.5.r1, bf16[256,1024]{1,0:T(8,128)(2,1)S(1)} %collective-permute-done.6.r2, bf16[256,1024]{1,0:T(8,128)(2,1)S(1)} %collective-permute-done.7.r3), custom_call_target="tpu_custom_call" | custom-call | tf_op jit(solution)/shard_map/placed/pallas_call | solution.py:192
  185.2 5.3 %all-to-all-done.2 = f32[4,256,128]{1,2,0:T(8,128)S(1)} async-done(((f32[4,256,128]{1,2,0:T(8,128)}), f32[4,256,128]{1,2,0:T(8,128)S(1)}, u32[]{:S(2)}, u32[]{:S(2)}) %all-to-all-start.2) | async-done | bytes 524320 | tf_op jit(solution)/shard_map/all_to_all | solution.py:189
  190.6 0.8 copy.10
  (9 shorter events, 0.1 us)
Async XLA Ops:
  0.6 58.1 %copy-start = (bf16[512,256]{1,0:T(8,128)(2,1)S(1)}, bf16[512,256]{1,0:T(8,128)(2,1)}, u32[]{:S(2)}) copy-start(bf16[512,256]{1,0:T(8,128)(2,1)} %param.7) | copy-start | bytes 786436
  0.7 0.9 copy-start.1
  1.7 0.8 copy-start.2
  2.4 0.7 copy-start.3
  7.4 13.2 %collective-permute-start.2 = (bf16[256,1280]{1,0:T(8,128)(2,1)S(1)}, bf16[256,1280]{1,0:T(8,128)(2,1)S(1)}, u32[]{:S(2)}, u32[]{:S(2)}) collective-permute-start(bf16[256,1280]{1,0:T(8,128)(2,1)S(1)} %get-tuple-element.13), channel_id=1, source_target_pairs={{0,48},{16,32},{32,16},{48,0},{1,49},{17,33},{33,17},{49,1},{2,50}... | collective-permute-start | bytes 1966088 | tf_op jit(solution)/shard_map/ppermute | solution.py:142
  12.6 11.6 %collective-permute-start.1 = (bf16[256,1280]{1,0:T(8,128)(2,1)S(1)}, bf16[256,1280]{1,0:T(8,128)(2,1)S(1)}, u32[]{:S(2)}, u32[]{:S(2)}) collective-permute-start(bf16[256,1280]{1,0:T(8,128)(2,1)S(1)} %get-tuple-element.12), channel_id=1, source_target_pairs={{0,32},{16,48},{32,0},{48,16},{1,33},{17,49},{33,1},{49,17},{2,34}... | collective-permute-start | bytes 1966088 | tf_op jit(solution)/shard_map/ppermute | solution.py:142
  14.5 21.1 %collective-permute-start = (bf16[256,1280]{1,0:T(8,128)(2,1)S(1)}, bf16[256,1280]{1,0:T(8,128)(2,1)S(1)}, u32[]{:S(2)}, u32[]{:S(2)}) collective-permute-start(bf16[256,1280]{1,0:T(8,128)(2,1)S(1)} %get-tuple-element.11), channel_id=1, source_target_pairs={{0,16},{16,0},{32,48},{48,32},{1,17},{17,1},{33,49},{49,33},{2,18}... | collective-permute-start | bytes 1966088 | tf_op jit(solution)/shard_map/ppermute | solution.py:142
  35.7 13.3 %collective-permute-start.3 = (bf16[1024,256]{1,0:T(8,128)(2,1)S(1)}, bf16[1024,256]{1,0:T(8,128)(2,1)S(1)}, u32[]{:S(2)}, u32[]{:S(2)}) collective-permute-start(bf16[1024,256]{1,0:T(8,128)(2,1)S(1)} %pad_maximum_fusion), channel_id=1, source_target_pairs={{0,1},{1,0},{2,3},{3,2},{4,5},{5,4},{6,7},{7,6},{8,9},{9,8},{10,11... | collective-permute-start | bytes 1572872 | tf_op jit(solution)/shard_map/ppermute | solution.py:151
  51.8 36.3 %all-to-all-start = ((bf16[8,512,128]{2,1,0:T(8,128)(2,1)}), bf16[8,512,128]{2,1,0:T(8,128)(2,1)}, u32[]{:S(2)}, u32[]{:S(2)}) async-start(bf16[8,512,128]{2,1,0:T(8,128)(2,1)} %weight_grad.1), calls=%async_computation | async-start | bytes 2097152 | tf_op jit(solution)/shard_map/all_to_all | solution.py:182
  89.1 32.6 %all-to-all-start.3 = ((bf16[16,128,256]{2,1,0:T(8,128)(2,1)}), bf16[16,128,256]{2,1,0:T(8,128)(2,1)}, u32[]{:S(2)}, u32[]{:S(2)}) async-start(bf16[16,128,256]{2,1,0:T(8,128)(2,1)} %bitcast.14), calls=%async_computation.3 | async-start | bytes 2097152 | tf_op jit(solution)/shard_map/all_to_all | solution.py:148
  121.8 31.5 %all-to-all-start.1 = ((bf16[12,48,128]{2,1,0:T(8,128)(2,1)}), bf16[12,48,128]{2,1,0:T(8,128)(2,1)}, u32[]{:S(2)}, u32[]{:S(2)}) async-start(bf16[12,48,128]{2,1,0:T(8,128)(2,1)} %bitcast.17), calls=%async_computation.1 | async-start | bytes 294912 | tf_op jit(solution)/shard_map/all_to_all | solution.py:185
  140.4 42.2 %collective-permute-start.4 = (bf16[256,1024]{1,0:T(8,128)(2,1)}, bf16[256,1024]{1,0:T(8,128)(2,1)S(1)}, u32[]{:S(2)}, u32[]{:S(2)}) collective-permute-start(bf16[256,1024]{1,0:T(8,128)(2,1)} %get-tuple-element.14), channel_id=1, source_target_pairs={{0,0},{1,16},{16,1},{17,17},{32,32},{33,48},{48,33},{49,49},{2,2},... | collective-permute-start | bytes 1572872 | tf_op jit(solution)/shard_map/ppermute | solution.py:171
  142.9 39.7 %collective-permute-start.5 = (bf16[256,1024]{1,0:T(8,128)(2,1)}, bf16[256,1024]{1,0:T(8,128)(2,1)S(1)}, u32[]{:S(2)}, u32[]{:S(2)}) collective-permute-start(bf16[256,1024]{1,0:T(8,128)(2,1)} %get-tuple-element.15), channel_id=1, source_target_pairs={{0,16},{1,0},{16,17},{17,1},{32,48},{33,32},{48,49},{49,33},{2,18}... | collective-permute-start | bytes 1572872 | tf_op jit(solution)/shard_map/ppermute | solution.py:171
  144.8 37.8 %collective-permute-start.6 = (bf16[256,1024]{1,0:T(8,128)(2,1)}, bf16[256,1024]{1,0:T(8,128)(2,1)S(1)}, u32[]{:S(2)}, u32[]{:S(2)}) collective-permute-start(bf16[256,1024]{1,0:T(8,128)(2,1)} %get-tuple-element.16), channel_id=1, source_target_pairs={{0,32},{1,48},{16,33},{17,49},{32,0},{33,16},{48,1},{49,17},{2,34}... | collective-permute-start | bytes 1572872 | tf_op jit(solution)/shard_map/ppermute | solution.py:171
  148.8 33.8 %collective-permute-start.7 = (bf16[256,1024]{1,0:T(8,128)(2,1)}, bf16[256,1024]{1,0:T(8,128)(2,1)S(1)}, u32[]{:S(2)}, u32[]{:S(2)}) collective-permute-start(bf16[256,1024]{1,0:T(8,128)(2,1)} %get-tuple-element.17), channel_id=1, source_target_pairs={{0,48},{1,32},{16,49},{17,33},{32,16},{33,0},{48,17},{49,1},{2,50}... | collective-permute-start | bytes 1572872 | tf_op jit(solution)/shard_map/ppermute | solution.py:171
  175.5 15.0 %all-to-all-start.2 = ((f32[4,256,128]{1,2,0:T(8,128)}), f32[4,256,128]{1,2,0:T(8,128)S(1)}, u32[]{:S(2)}, u32[]{:S(2)}) async-start(f32[4,256,128]{1,2,0:T(8,128)} %bitcast.6), calls=%async_computation.2 | async-start | bytes 1048576 | tf_op jit(solution)/shard_map/all_to_all | solution.py:189

commit v2 on v1

v2 whole, which is shorter than its diff:
```python
import functools
import math

import jax
import jax.numpy as jnp
from jax import lax
from jax.experimental import pallas as pl
from jax.experimental.pallas import tpu as pltpu
from jax.sharding import Mesh, PartitionSpec as P

NZ, NX, NY, NT = 12, 2, 8, 2
TOK, D, HS, COLS = 256, 8192, 128, 256
QUART = 128
FEAT = NY * QUART
KV = NT * COLS
ZCOLS = 24
VMEM = 48 * 1024 * 1024
BF16, F32 = jnp.bfloat16, jnp.float32


def prep_kernel(place, act, gain, first, *outs):
    del first
    xl, xh, t = place[0], place[1], place[2]
    rows = act.shape[0]
    square = jnp.zeros((rows, 128), F32)
    for j in range(D // 128):
        v = act[:, j * 128 : (j + 1) * 128].astype(F32)
        square = square + v * v
    scale = lax.rsqrt(jnp.sum(square, axis=1, keepdims=True) * (1.0 / D) + 1e-06)

    for k, out in enumerate(outs):
        a, b = k & 1, k >> 1
        base = (xh ^ a) * (D // 2) + (2 * (xl ^ b) + t) * QUART
        for j in range(NY):
            at = pl.ds(pl.multiple_of(base + j * 4 * QUART, 128), QUART)
            v = act[:, at].astype(F32) * scale * gain[:, at]
            out[:, j * QUART : (j + 1) * QUART] = v.astype(BF16)


def rope_kernel(doc, key_grad, freq, first, rot):
    del first
    rows = key_grad.shape[0]
    token = lax.broadcasted_iota(jnp.int32, (rows, 128), 0)
    second = doc[0, 0]
    third = second + doc[0, 1]
    fourth = third + doc[0, 2]
    first = jnp.where(
        token >= fourth,
        fourth,
        jnp.where(token >= third, third, jnp.where(token >= second, second, 0)),
    )
    angle = (token - first).astype(F32) * freq[...]
    cosine = jnp.cos(angle)
    lane = lax.broadcasted_iota(jnp.int32, (rows, 128), 1)
    sine = jnp.sin(angle)
    sine = jnp.where(lane < HS // 2, sine, -sine)
    for h in range(COLS // HS):
        v = key_grad[:, h * HS : (h + 1) * HS].astype(F32)
        v = (v * cosine + pltpu.roll(v, HS // 2, 1) * sine).astype(BF16)
        for copy in range(4):
            rot[copy, :, h * HS : (h + 1) * HS] = v


def grad_kernel(place, b0, b1, b2, b3, mine, other, out):
    t, me = place[2], 2 * place[0] + place[1]
    normed = jnp.concatenate([b[...] for b in (b0, b1, b2, b3)], axis=0)
    for half, rot in ((t, mine), (1 - t, other)):
        rot = jnp.concatenate([rot[me ^ k] for k in range(4)], axis=0)
        g = lax.dot_general(rot, normed, (((0,), (0,)), ((), ())), preferred_element_type=F32)
        g = g.astype(BF16)
        for y in range(NY):
            out[y, pl.ds(pl.multiple_of(half * COLS, COLS), COLS), :] = g[
                :, y * QUART : (y + 1) * QUART
            ]


def input_kernel(place, mine, other, w_mine, w_other, *outs):
    xl, t = place[0], place[2]
    lhs = []
    for r in range(4):
        i = 2 * (xl ^ (r >> 1)) + (t ^ (r & 1))
        lhs.append(jnp.concatenate([mine[i], other[i]], axis=1))
    lhs = jnp.concatenate(lhs, axis=0)
    for j in range(NY // 2):
        rhs = jnp.concatenate(
            [
                jnp.concatenate([w_mine[y, t], w_other[y]], axis=1)
                for y in (2 * j, 2 * j + 1)
            ],
            axis=0,
        )
        p = lax.dot_general(lhs, rhs, (((1,), (1,)), ((), ())), preferred_element_type=F32)
        p = p.astype(BF16)
        for r, out in enumerate(outs):
            out[:, j * 2 * QUART : (j + 1) * 2 * QUART] = p[r * TOK : (r + 1) * TOK, :]


def sum_y_kernel(term, after, out):
    del after
    total = term[0].astype(F32)
    for y in range(1, NY):
        total = total + term[y].astype(F32)
    zero = jnp.zeros((NZ * ZCOLS - COLS, QUART), F32)
    for t in range(NT):
        padded = jnp.concatenate([total[t * COLS : (t + 1) * COLS, :], zero], axis=0)
        for z in range(NZ):
            out[z, t] = padded[z * ZCOLS : (z + 1) * ZCOLS, :].astype(BF16)


def sum_z_kernel(term, after0, after1, after2, after3, out):
    del after0, after1, after2, after3
    for t in range(NT):
        total = term[0, t].astype(F32)
        for z in range(1, NZ):
            total = total + term[z, t].astype(F32)
        total = (total * (1.0 / (NZ * NX))).astype(BF16)
        for z in range(NZ):
            out[z, t] = total


def split_kernel(term, out):
    for z in range(NZ):
        for t in range(NT):
            for xl in range(NX):
                out[NT * xl + t, z] = term[z, t]


def turn_kernel(term, out):
    for q in range(NX * NT):
        piece = jnp.concatenate([term[q, z].astype(F32) for z in range(NZ)], axis=0)
        out[q * QUART : (q + 1) * QUART, :] = piece[:COLS, :].T


def place_kernel(place, r0, r1, r2, r3, out):
    mine = 2 * place[0] + place[1]
    for r, got in enumerate((r0, r1, r2, r3)):
        q = mine ^ r
        for y in range(NY):
            at = pl.ds(pl.multiple_of(y * 4 * QUART + q * QUART, QUART), QUART)
            out[:, at] = got[:, y * QUART : (y + 1) * QUART]


def whole(count):
    return [pl.BlockSpec(memory_space=pltpu.VMEM)] * count


SCALARS = pl.BlockSpec(memory_space=pltpu.SMEM)
PARAMS = pltpu.CompilerParams(vmem_limit_bytes=VMEM)


def per_device(activations, norm_gain, key_weight, key_grad, doc_lengths):
    xl, xh, t = lax.axis_index("xl"), lax.axis_index("xh"), lax.axis_index("t")
    place = jnp.stack([xl, xh, t]).astype(jnp.int32)
    half = jnp.arange(HS, dtype=jnp.int32) % (HS // 2)
    freq = jnp.exp(half.astype(F32) * (-2.0 * math.log(1000000.0) / HS))[None, :]

    half_shard = lax.dynamic_slice_in_dim(key_weight, xl * NT * QUART, NT * QUART, 0)
    shard = lax.all_gather(half_shard, "y", axis=0, tiled=True).reshape(NY, NT, QUART, COLS)

    rotated = pl.pallas_call(
        rope_kernel,
        in_specs=[SCALARS] + whole(2) + [pl.BlockSpec(memory_space=pl.ANY)],
        out_specs=whole(1)[0],
        out_shape=jax.ShapeDtypeStruct((4, TOK, COLS), BF16),
        compiler_params=PARAMS,
        name="rope",
    )(doc_lengths, key_grad, freq, half_shard)
    rows = 64
    blocks = pl.pallas_call(
        prep_kernel,
        grid=(TOK // rows,),
        in_specs=[
            SCALARS,
            pl.BlockSpec((rows, D), lambda i: (i, 0)),
            pl.BlockSpec((1, D), lambda i: (0, 0)),
            pl.BlockSpec(memory_space=pl.ANY),
        ],
        out_specs=[pl.BlockSpec((rows, FEAT), lambda i: (i, 0))] * 4,
        out_shape=[jax.ShapeDtypeStruct((TOK, FEAT), BF16)] * 4,
        compiler_params=PARAMS,
        name="prep",
    )(place, activations, norm_gain[None, :], rotated)

    got = [blocks[0]] + [
        lax.ppermute(blocks[k], ("xl", "xh"), [(i, i ^ k) for i in range(4)]) for k in (1, 2, 3)
    ]
    mine = lax.all_to_all(rotated, ("xl", "xh"), 0, 0, tiled=True)
    other = lax.ppermute(mine, "t", [(0, 1), (1, 0)])

    term = pl.pallas_call(
        grad_kernel,
        in_specs=[SCALARS] + whole(6),
        out_specs=whole(1)[0],
        out_shape=jax.ShapeDtypeStruct((NY, KV, QUART), BF16),
        compiler_params=PARAMS,
        name="weight_grad",
    )(place, *got, mine, other)

    w_other = lax.dynamic_index_in_dim(shard, 1 - t, 1, keepdims=False)
    w_other = lax.ppermute(w_other, "t", [(0, 1), (1, 0)])
    products = pl.pallas_call(
        input_kernel,
        in_specs=[SCALARS] + whole(4),
        out_specs=whole(4),
        out_shape=[jax.ShapeDtypeStruct((TOK, FEAT), BF16)] * 4,
        compiler_params=PARAMS,
        name="input_grad",
    )(place, mine, other, shard, w_other)

    returned = []
    for r in range(4):
        r0, r1 = r >> 1, r & 1
        pairs = [
            (4 * i + 2 * j + k, 4 * (i ^ r0) + 2 * (k ^ r1) + j)
            for i in range(2)
            for j in range(2)
            for k in range(2)
        ]
        returned.append(lax.ppermute(products[r], ("xl", "xh", "t"), pairs))

    term = lax.all_to_all(term, "y", 0, 0, tiled=True)
    term = pl.pallas_call(
        sum_y_kernel,
        in_specs=whole(1) + [pl.BlockSpec(memory_space=pl.ANY)],
        out_specs=whole(1)[0],
        out_shape=jax.ShapeDtypeStruct((NZ, NT, ZCOLS, QUART), BF16),
        compiler_params=PARAMS,
        name="sum_y",
    )(term, products[0])
    term = lax.all_to_all(term, "z", 0, 0, tiled=True)
    pieces = jax.ShapeDtypeStruct((NZ, NT, ZCOLS, QUART), BF16)
    term = pl.pallas_call(
        sum_z_kernel,
        in_specs=whole(1) + [pl.BlockSpec(memory_space=pl.ANY)] * 4,
        out_specs=whole(1)[0],
        out_shape=pieces,
        compiler_params=PARAMS,
        name="sum_z",
    )(term, *returned)
    term = lax.all_to_all(term, "z", 0, 0, tiled=True)
    term = pl.pallas_call(
        split_kernel,
        in_specs=whole(1),
        out_specs=whole(1)[0],
        out_shape=jax.ShapeDtypeStruct((NX * NT, NZ, ZCOLS, QUART), BF16),
        compiler_params=PARAMS,
        name="split",
    )(term)
    term = lax.all_to_all(term, ("xl", "t"), 0, 0, tiled=True)
    weight_grad = pl.pallas_call(
        turn_kernel,
        in_specs=whole(1),
        out_specs=whole(1)[0],
        out_shape=jax.ShapeDtypeStruct((NX * NT * QUART, COLS), F32),
        compiler_params=PARAMS,
        name="turn",
    )(term)

    normed_grad = pl.pallas_call(
        place_kernel,
        grid=(TOK // rows,),
        in_specs=[SCALARS] + [pl.BlockSpec((rows, FEAT), lambda i: (i, 0))] * 4,
        out_specs=pl.BlockSpec((rows, 4 * FEAT), lambda i: (i, 0)),
        out_shape=jax.ShapeDtypeStruct((TOK, 4 * FEAT), BF16),
        compiler_params=PARAMS,
        name="placed",
    )(place, *returned)
    return (weight_grad, normed_grad)


def solution(mesh):
    fine = Mesh(mesh.devices.reshape(NZ, NX, 2, NY, NT), ("z", "xl", "xh", "y", "t"))
    tokens = ("z", "xl", "xh", "y")
    return jax.shard_map(
        per_device,
        mesh=fine,
        in_specs=(
            P(tokens, None),
            P(),
            P(("xh", "y"), "t"),
            P(tokens, "t"),
            P(tokens, None),
        ),
        out_specs=(P(("xh", "y"), "t"), P(tokens, "t")),
        check_vma=False,
    )
```

time: 192 us -> 154 us (0.80)
  waiting for transfers between devices: 80.2 us -> 29.8 us
  between operations: 0.82 us -> 14.2 us
  blocking collectives: 20.3 us -> 15.2 us
  Pallas kernels: 13.4 us -> 17.5 us
  starting transfers between devices: 68.3 us -> 71 us
  other arithmetic: 2.44 us -> 0.09 us
    all_to_all x1, waiting for transfers between devices: 29.3 us -> 0.01 us  [per_device(): term = lax.all_to_all(term, 'y', 0, 0, tiled=True)]
    all_to_all x2, waiting for transfers between devices: 31.4 us -> 2.89 us  [the longest x1 2.89 us: per_device(): term = lax.all_to_all(term, ('xl', 't'), 0, 0, tiled=True)]
    all_gather x1 -> x0, blocking collectives: 20.3 us -> none  [per_device(): term = lax.all_gather(term, 'z', axis=0, tiled=True)[:KV]]
    all_to_all x0 -> x1, blocking collectives: none -> 15.2 us  [per_device(): term = lax.all_to_all(term, 'z', 0, 0, tiled=True)]
    ppermute x3, waiting for transfers between devices: 18 us -> 5.01 us  [per_device(): lax.ppermute(blocks[k], ('xl', 'xh'), [(i, i ^ k) for i in range(4)])]
    all_gather x0 -> x1, waiting for transfers between devices: none -> 9 us  [per_device(): lax.all_gather(half_shard, 'y', axis=0, tiled=True)]
    ppermute x0 -> x1, starting transfers between devices: none -> 8.81 us  [per_device(): w_other = lax.ppermute(w_other, 't', [(0, 1), (1, 0)])]
    ppermute x4, waiting for transfers between devices: 0.01 us -> 7.75 us  [per_device(): returned.append(lax.ppermute(products[r], ('xl', 'xh', 't'), pairs))]
  transfers between devices with their start and end apart: 12 -> 14, of which waited for: 7 -> 8; matrix products, arithmetic and copies ran while one was open for 2% -> 1% of each run, Pallas kernels for 3% -> 9%
where the time goes in v2:
time: 154 us; the launch traced here: 153 us
  starting transfers between devices  71 us (46%)
  waiting for transfers between devices  29.8 us (19%)
  Pallas kernels  17.5 us (11%)
  blocking collectives  15.2 us (10%)
  between operations  14.2 us (9%)
  local copies, waits for them, and re-layouts  5.6 us (4%)
    all_to_all x1, blocking collectives, per_device(): term = lax.all_to_all(term, 'z', 0, 0, tiled=True)  15.2 us
    ppermute x4, starting transfers between devices, per_device(): returned.append(lax.ppermute(products[r], ('xl', 'xh', 't'), pairs))  12.9 us
    ppermute x1, starting transfers between devices, per_device(): other = lax.ppermute(mine, 't', [(0, 1), (1, 0)])  11.9 us
    ppermute x3, starting transfers between devices, per_device(): lax.ppermute(blocks[k], ('xl', 'xh'), [(i, i ^ k) for i in range(4)])  9.58 us
    all_to_all x1, starting transfers between devices, per_device(): term = lax.all_to_all(term, 'y', 0, 0, tiled=True)  9 us
    all_gather x1, waiting for transfers between devices, per_device(): lax.all_gather(half_shard, 'y', axis=0, tiled=True)  9 us
    ppermute x1, starting transfers between devices, per_device(): w_other = lax.ppermute(w_other, 't', [(0, 1), (1, 0)])  8.81 us
    all_to_all x1, starting transfers between devices, per_device(): term = lax.all_to_all(term, 'z', 0, 0, tiled=True)  7.84 us
  transfers between devices with their start and end apart: 14, of which 8 were waited for; matrix products, arithmetic and copies ran while one was open for 1% of the time, Pallas kernels for 9%

profile of v2, /device:TPU:1, one launch (start us, length us, event | category | flops | bytes accessed | tf_op | source)
XLA Modules:
  0.0 153.4 jit_solution(905569260472765437)
XLA Ops:
  7.2 0.0 copy-start
  7.2 0.9 copy-done
  8.1 0.0 copy-start.2
  8.1 0.0 copy-start.3
  8.2 0.9 copy-done.3
  9.1 0.7 copy-done.5
  9.8 2.0 %rope.1.first = bf16[4,256,256]{2,1,0:T(8,128)(2,1)} custom-call(s32[1,4]{1,0:T(1,128)S(1)} %copy-done.5, bf16[256,256]{1,0:T(8,128)(2,1)S(1)} %copy-done.3, f32[1,128]{1,0:T(1,128)S(1)} %fusion.2.freq, bf16[256,256]{1,0:T(8,128)(2,1)S(1)} %constant_dynamic-slice_fusion.first), custom_call_target="tpu_custom_call" | custom-call | tf_op jit(solution)/shard_map/rope/pallas_call | solution.py:160
  11.8 4.8 %all-to-all-start = ((bf16[4,256,256]{2,1,0:T(8,128)(2,1)}), bf16[4,256,256]{2,1,0:T(8,128)(2,1)S(1)}, u32[]{:S(2)}, u32[]{:S(2)}) async-start(bf16[4,256,256]{2,1,0:T(8,128)(2,1)} %rope.1.first), calls=%async_computation | async-start | bytes 1048576 | tf_op jit(solution)/shard_map/all_to_all | solution.py:187
  16.6 0.0 all-gather.2.cloned.1.call-start
  16.6 0.7 all-gather.2.cloned.1.call-update
  17.3 0.1 pad_add_fusion.place
  17.4 0.8 copy-done.4
  18.2 4.7 %prep.1 = (bf16[256,1024]{1,0:T(8,128)(2,1)S(1)}, bf16[256,1024]{1,0:T(8,128)(2,1)}, bf16[256,1024]{1,0:T(8,128)(2,1)}, bf16[256,1024]{1,0:T(8,128)(2,1)}) custom-call(s32[3]{0:T(128)S(1)} %pad_add_fusion.place, bf16[256,8192]{1,0:T(8,128)(2,1)} %act.1, f32[1,8192]{1,0:T(1,128)S(1)} %bitcast.9, bf16[4,256,256]{2,1,0:T(8,128)(2,1)} %rope.1.first), custom_call_target="tpu_custom_call" | custom-call | tf_op jit(solution)/shard_map/prep/pallas_call | solution.py:169
  22.9 4.9 %collective-permute-start = (bf16[256,1024]{1,0:T(8,128)(2,1)}, bf16[256,1024]{1,0:T(8,128)(2,1)S(1)}, u32[]{:S(2)}, u32[]{:S(2)}) collective-permute-start(bf16[256,1024]{1,0:T(8,128)(2,1)} %get-tuple-element.11), channel_id=1, source_target_pairs={{0,16},{16,0},{32,48},{48,32},{1,17},{17,1},{33,49},{49,33},{2,18}... | collective-permute-start | bytes 1572872 | tf_op jit(solution)/shard_map/ppermute | solution.py:185
  27.7 2.2 %collective-permute-start.1 = (bf16[256,1024]{1,0:T(8,128)(2,1)}, bf16[256,1024]{1,0:T(8,128)(2,1)S(1)}, u32[]{:S(2)}, u32[]{:S(2)}) collective-permute-start(bf16[256,1024]{1,0:T(8,128)(2,1)} %get-tuple-element.12), channel_id=1, source_target_pairs={{0,32},{16,48},{32,0},{48,16},{1,33},{17,49},{33,1},{49,17},{2,34}... | collective-permute-start | bytes 1572872 | tf_op jit(solution)/shard_map/ppermute | solution.py:185
  29.9 2.5 %collective-permute-start.2 = (bf16[256,1024]{1,0:T(8,128)(2,1)}, bf16[256,1024]{1,0:T(8,128)(2,1)S(1)}, u32[]{:S(2)}, u32[]{:S(2)}) collective-permute-start(bf16[256,1024]{1,0:T(8,128)(2,1)} %get-tuple-element.13), channel_id=1, source_target_pairs={{0,48},{16,32},{32,16},{48,0},{1,49},{17,33},{33,17},{49,1},{2,50}... | collective-permute-start | bytes 1572872 | tf_op jit(solution)/shard_map/ppermute | solution.py:185
  32.5 0.0 all-to-all-done.mine
  32.5 11.9 %collective-permute-start.3 = (bf16[4,256,256]{2,1,0:T(8,128)(2,1)S(1)}, bf16[4,256,256]{2,1,0:T(8,128)(2,1)S(1)}, u32[]{:S(2)}, u32[]{:S(2)}) collective-permute-start(bf16[4,256,256]{2,1,0:T(8,128)(2,1)S(1)} %all-to-all-done.mine), channel_id=1, source_target_pairs={{0,1},{1,0},{2,3},{3,2},{4,5},{5,4},{6,7},{7,6},{8,9},{9,8},{10,11... | collective-permute-start | bytes 1572872 | tf_op jit(solution)/shard_map/ppermute | solution.py:188
  44.3 0.0 collective-permute-done.b1
  44.4 2.8 %collective-permute-done.1.b2 = bf16[256,1024]{1,0:T(8,128)(2,1)S(1)} collective-permute-done((bf16[256,1024]{1,0:T(8,128)(2,1)}, bf16[256,1024]{1,0:T(8,128)(2,1)S(1)}, u32[]{:S(2)}, u32[]{:S(2)}) %collective-permute-start.1) | collective-permute-done | bytes 524320 | tf_op jit(solution)/shard_map/ppermute | solution.py:185
  47.2 2.2 %collective-permute-done.2.b3 = bf16[256,1024]{1,0:T(8,128)(2,1)S(1)} collective-permute-done((bf16[256,1024]{1,0:T(8,128)(2,1)}, bf16[256,1024]{1,0:T(8,128)(2,1)S(1)}, u32[]{:S(2)}, u32[]{:S(2)}) %collective-permute-start.2) | collective-permute-done | bytes 524320 | tf_op jit(solution)/shard_map/ppermute | solution.py:185
  49.4 0.0 collective-permute-done.3.other
  49.4 2.8 %weight_grad.1 = bf16[8,512,128]{2,1,0:T(8,128)(2,1)} custom-call(s32[3]{0:T(128)S(1)} %pad_add_fusion.place, bf16[256,1024]{1,0:T(8,128)(2,1)S(1)} %get-tuple-element.10.b0, bf16[256,1024]{1,0:T(8,128)(2,1)S(1)} %collective-permute-done.b1, bf16[256,1024]{1,0:T(8,128)(2,1)S(1)} %collective-permute-done.1.b2, ...), custom_call_target="tpu_custom_call" | custom-call | tf_op jit(solution)/shard_map/weight_grad/pallas_call | solution.py:190
  52.2 9.0 %all-to-all-start.1 = ((bf16[8,512,128]{2,1,0:T(8,128)(2,1)}), bf16[8,512,128]{2,1,0:T(8,128)(2,1)S(1)}, u32[]{:S(2)}, u32[]{:S(2)}) async-start(bf16[8,512,128]{2,1,0:T(8,128)(2,1)} %weight_grad.1), calls=%async_computation.1 | async-start | bytes 2097152 | tf_op jit(solution)/shard_map/all_to_all | solution.py:221
  61.2 9.0 %all-gather.2.cloned.1.call-done = bf16[2048,256]{1,0:T(8,128)(2,1)} async-done(((bf16[256,256]{1,0:T(8,128)(2,1)}), bf16[2048,256]{1,0:T(8,128)(2,1)}) %all-gather.2.cloned.1.call-update) | async-done | bytes 1048592 | tf_op jit(solution)/shard_map/all_gather | solution.py:158
  70.2 1.1 dynamic-slice_bitcast_fusion
  71.2 8.8 %collective-permute-start.4 = (bf16[8,128,256]{2,1,0:T(8,128)(2,1)S(1)}, bf16[8,128,256]{2,1,0:T(8,128)(2,1)S(1)}, u32[]{:S(2)}, u32[]{:S(2)}) collective-permute-start(bf16[8,128,256]{2,1,0:T(8,128)(2,1)S(1)} %dynamic-slice_bitcast_fusion), channel_id=1, source_target_pairs={{0,1},{1,0},{2,3},{3,2},{4,5},{5,4},{6,7},{7,6},{8,9},{9,8},{10,11... | collective-permute-start | bytes 1572872 | tf_op jit(solution)/shard_map/ppermute | solution.py:200
  80.1 1.5 collective-permute-done.4.w_other
  81.6 1.2 copy-done.1
  82.8 2.9 %input_grad.1 = (bf16[256,1024]{1,0:T(8,128)(2,1)}, bf16[256,1024]{1,0:T(8,128)(2,1)}, bf16[256,1024]{1,0:T(8,128)(2,1)}, bf16[256,1024]{1,0:T(8,128)(2,1)}) custom-call(s32[3]{0:T(128)S(1)} %pad_add_fusion.place, bf16[4,256,256]{2,1,0:T(8,128)(2,1)S(1)} %all-to-all-done.mine, bf16[4,256,256]{2,1,0:T(8,128)(2,1)S(1)} %collective-permute-done.3.other, ...), custom_call_target="tpu_custom_call" | custom-call | tf_op jit(solution)/shard_map/input_grad/pallas_call | solution.py:201
  85.7 4.2 %collective-permute-start.5 = (bf16[256,1024]{1,0:T(8,128)(2,1)}, bf16[256,1024]{1,0:T(8,128)(2,1)S(1)}, u32[]{:S(2)}, u32[]{:S(2)}) collective-permute-start(bf16[256,1024]{1,0:T(8,128)(2,1)} %get-tuple-element.14.after), channel_id=1, source_target_pairs={{0,0},{1,16},{16,1},{17,17},{32,32},{33,48},{48,33},{49,49},{2,2},... | collective-permute-start | bytes 1572872 | tf_op jit(solution)/shard_map/ppermute | solution.py:219
  90.0 1.9 %collective-permute-start.6 = (bf16[256,1024]{1,0:T(8,128)(2,1)}, bf16[256,1024]{1,0:T(8,128)(2,1)S(1)}, u32[]{:S(2)}, u32[]{:S(2)}) collective-permute-start(bf16[256,1024]{1,0:T(8,128)(2,1)} %get-tuple-element.15), channel_id=1, source_target_pairs={{0,16},{1,0},{16,17},{17,1},{32,48},{33,32},{48,49},{49,33},{2,18}... | collective-permute-start | bytes 1572872 | tf_op jit(solution)/shard_map/ppermute | solution.py:219
  91.9 2.4 %collective-permute-start.7 = (bf16[256,1024]{1,0:T(8,128)(2,1)}, bf16[256,1024]{1,0:T(8,128)(2,1)S(1)}, u32[]{:S(2)}, u32[]{:S(2)}) collective-permute-start(bf16[256,1024]{1,0:T(8,128)(2,1)} %get-tuple-element.16), channel_id=1, source_target_pairs={{0,32},{1,48},{16,33},{17,49},{32,0},{33,16},{48,1},{49,17},{2,34}... | collective-permute-start | bytes 1572872 | tf_op jit(solution)/shard_map/ppermute | solution.py:219
  94.3 4.4 %collective-permute-start.8 = (bf16[256,1024]{1,0:T(8,128)(2,1)}, bf16[256,1024]{1,0:T(8,128)(2,1)S(1)}, u32[]{:S(2)}, u32[]{:S(2)}) collective-permute-start(bf16[256,1024]{1,0:T(8,128)(2,1)} %get-tuple-element.17), channel_id=1, source_target_pairs={{0,48},{1,32},{16,49},{17,33},{32,16},{33,0},{48,17},{49,1},{2,50}... | collective-permute-start | bytes 1572872 | tf_op jit(solution)/shard_map/ppermute | solution.py:219
  98.7 0.0 all-to-all-done.1.term
  98.7 0.8 sum_y.1
  99.5 7.8 %all-to-all-start.2 = ((bf16[12,2,24,128]{3,2,1,0:T(8,128)(2,1)}), bf16[12,2,24,128]{3,2,1,0:T(8,128)(2,1)S(1)}, u32[]{:S(2)}, u32[]{:S(2)}) async-start(bf16[12,2,24,128]{3,2,1,0:T(8,128)(2,1)} %sum_y.1), calls=%async_computation.2 | async-start | bytes 294912 | tf_op jit(solution)/shard_map/all_to_all | solution.py:230
  107.3 0.0 collective-permute-done.5.after0.r0
  107.3 0.0 collective-permute-done.6.after1.r1
  107.4 7.6 %collective-permute-done.7.after2.r2 = bf16[256,1024]{1,0:T(8,128)(2,1)S(1)} collective-permute-done((bf16[256,1024]{1,0:T(8,128)(2,1)}, bf16[256,1024]{1,0:T(8,128)(2,1)S(1)}, u32[]{:S(2)}, u32[]{:S(2)}) %collective-permute-start.7) | collective-permute-done | bytes 524320 | tf_op jit(solution)/shard_map/ppermute | solution.py:219
  115.0 0.1 collective-permute-done.8.after3.r3
  115.1 2.9 %all-to-all-done.2.term = bf16[12,2,24,128]{3,2,1,0:T(8,128)(2,1)S(1)} async-done(((bf16[12,2,24,128]{3,2,1,0:T(8,128)(2,1)}), bf16[12,2,24,128]{3,2,1,0:T(8,128)(2,1)S(1)}, u32[]{:S(2)}, u32[]{:S(2)}) %all-to-all-start.2) | async-done | bytes 147488 | tf_op jit(solution)/shard_map/all_to_all | solution.py:230
  118.1 15.2 %all_to_all.25.term = bf16[12,2,24,128]{3,2,1,0:T(8,128)(2,1)S(1)} all-to-all(bf16[12,2,24,128]{3,2,1,0:T(8,128)(2,1)S(1)} %sum_z.1), channel_id=1, replica_groups=mesh['z'=12,'xl'=2,'xh'=2,'y'=8,'t'=2] {'z'}, dimensions={0} | all-to-all | bytes 294912 | tf_op jit(solution)/shard_map/all_to_all | solution.py:240
  133.2 0.8 split.1
  134.0 6.2 %all-to-all-start.4 = ((bf16[4,12,24,128]{3,2,1,0:T(8,128)(2,1)}), bf16[4,12,24,128]{3,2,1,0:T(8,128)(2,1)S(1)}, u32[]{:S(2)}, u32[]{:S(2)}) async-start(bf16[4,12,24,128]{3,2,1,0:T(8,128)(2,1)} %split.1), calls=%async_computation.4 | async-start | bytes 589824 | tf_op jit(solution)/shard_map/all_to_all | solution.py:249
  140.2 2.6 %placed.1 = bf16[256,4096]{1,0:T(8,128)(2,1)} custom-call(s32[3]{0:T(128)S(1)} %pad_add_fusion.place, bf16[256,1024]{1,0:T(8,128)(2,1)S(1)} %collective-permute-done.5.after0.r0, bf16[256,1024]{1,0:T(8,128)(2,1)S(1)} %collective-permute-done.6.after1.r1, bf16[256,1024]{1,0:T(8,128)(2,1)S(1)} %collective-permute-done.7.after2.r2, ...), custom_call_target="tpu_custom_call" | custom-call | tf_op jit(solution)/shard_map/placed/pallas_call | solution.py:259
  142.7 2.9 %all-to-all-done.4.term = bf16[4,12,24,128]{3,2,1,0:T(8,128)(2,1)S(1)} async-done(((bf16[4,12,24,128]{3,2,1,0:T(8,128)(2,1)}), bf16[4,12,24,128]{3,2,1,0:T(8,128)(2,1)S(1)}, u32[]{:S(2)}, u32[]{:S(2)}) %all-to-all-start.4) | async-done | bytes 294944 | tf_op jit(solution)/shard_map/all_to_all | solution.py:249
  145.6 0.9 turn.1
  (7 shorter events, 0.1 us)
Async XLA Ops:
  7.2 1.0 copy-start
  8.1 8.5 %copy-start.2 = (bf16[256,256]{1,0:T(8,128)(2,1)}, bf16[256,256]{1,0:T(8,128)(2,1)S(1)}, u32[]{:S(2)}) copy-start(bf16[256,256]{1,0:T(8,128)(2,1)S(1)} %constant_dynamic-slice_fusion.first) | copy-start | bytes 393220
  8.1 1.0 copy-start.3
  9.1 0.7 copy-start.5
  11.8 20.7 %all-to-all-start = ((bf16[4,256,256]{2,1,0:T(8,128)(2,1)}), bf16[4,256,256]{2,1,0:T(8,128)(2,1)S(1)}, u32[]{:S(2)}, u32[]{:S(2)}) async-start(bf16[4,256,256]{2,1,0:T(8,128)(2,1)} %rope.1.first), calls=%async_computation | async-start | bytes 1048576 | tf_op jit(solution)/shard_map/all_to_all | solution.py:187
  16.6 53.5 %all-gather.2.cloned.1.call-start = ((), (), s32[]{:S(2)}) async-start(), calls=%async_computation.5 | async-start | bytes 1179648 | tf_op jit(solution)/shard_map/all_gather | solution.py:158
  17.4 0.8 copy-start.4
  22.9 21.5 %collective-permute-start = (bf16[256,1024]{1,0:T(8,128)(2,1)}, bf16[256,1024]{1,0:T(8,128)(2,1)S(1)}, u32[]{:S(2)}, u32[]{:S(2)}) collective-permute-start(bf16[256,1024]{1,0:T(8,128)(2,1)} %get-tuple-element.11), channel_id=1, source_target_pairs={{0,16},{16,0},{32,48},{48,32},{1,17},{17,1},{33,49},{49,33},{2,18}... | collective-permute-start | bytes 1572872 | tf_op jit(solution)/shard_map/ppermute | solution.py:185
  27.7 19.4 %collective-permute-start.1 = (bf16[256,1024]{1,0:T(8,128)(2,1)}, bf16[256,1024]{1,0:T(8,128)(2,1)S(1)}, u32[]{:S(2)}, u32[]{:S(2)}) collective-permute-start(bf16[256,1024]{1,0:T(8,128)(2,1)} %get-tuple-element.12), channel_id=1, source_target_pairs={{0,32},{16,48},{32,0},{48,16},{1,33},{17,49},{33,1},{49,17},{2,34}... | collective-permute-start | bytes 1572872 | tf_op jit(solution)/shard_map/ppermute | solution.py:185
  29.9 19.4 %collective-permute-start.2 = (bf16[256,1024]{1,0:T(8,128)(2,1)}, bf16[256,1024]{1,0:T(8,128)(2,1)S(1)}, u32[]{:S(2)}, u32[]{:S(2)}) collective-permute-start(bf16[256,1024]{1,0:T(8,128)(2,1)} %get-tuple-element.13), channel_id=1, source_target_pairs={{0,48},{16,32},{32,16},{48,0},{1,49},{17,33},{33,17},{49,1},{2,50}... | collective-permute-start | bytes 1572872 | tf_op jit(solution)/shard_map/ppermute | solution.py:185
  32.5 16.9 %collective-permute-start.3 = (bf16[4,256,256]{2,1,0:T(8,128)(2,1)S(1)}, bf16[4,256,256]{2,1,0:T(8,128)(2,1)S(1)}, u32[]{:S(2)}, u32[]{:S(2)}) collective-permute-start(bf16[4,256,256]{2,1,0:T(8,128)(2,1)S(1)} %all-to-all-done.mine), channel_id=1, source_target_pairs={{0,1},{1,0},{2,3},{3,2},{4,5},{5,4},{6,7},{7,6},{8,9},{9,8},{10,11... | collective-permute-start | bytes 1572872 | tf_op jit(solution)/shard_map/ppermute | solution.py:188
  52.2 46.5 %all-to-all-start.1 = ((bf16[8,512,128]{2,1,0:T(8,128)(2,1)}), bf16[8,512,128]{2,1,0:T(8,128)(2,1)S(1)}, u32[]{:S(2)}, u32[]{:S(2)}) async-start(bf16[8,512,128]{2,1,0:T(8,128)(2,1)} %weight_grad.1), calls=%async_computation.1 | async-start | bytes 2097152 | tf_op jit(solution)/shard_map/all_to_all | solution.py:221
  71.2 10.3 %collective-permute-start.4 = (bf16[8,128,256]{2,1,0:T(8,128)(2,1)S(1)}, bf16[8,128,256]{2,1,0:T(8,128)(2,1)S(1)}, u32[]{:S(2)}, u32[]{:S(2)}) collective-permute-start(bf16[8,128,256]{2,1,0:T(8,128)(2,1)S(1)} %dynamic-slice_bitcast_fusion), channel_id=1, source_target_pairs={{0,1},{1,0},{2,3},{3,2},{4,5},{5,4},{6,7},{7,6},{8,9},{9,8},{10,11... | collective-permute-start | bytes 1572872 | tf_op jit(solution)/shard_map/ppermute | solution.py:200
  81.6 1.2 copy-start.1
  85.7 21.6 %collective-permute-start.5 = (bf16[256,1024]{1,0:T(8,128)(2,1)}, bf16[256,1024]{1,0:T(8,128)(2,1)S(1)}, u32[]{:S(2)}, u32[]{:S(2)}) collective-permute-start(bf16[256,1024]{1,0:T(8,128)(2,1)} %get-tuple-element.14.after), channel_id=1, source_target_pairs={{0,0},{1,16},{16,1},{17,17},{32,32},{33,48},{48,33},{49,49},{2,2},... | collective-permute-start | bytes 1572872 | tf_op jit(solution)/shard_map/ppermute | solution.py:219
  90.0 17.4 %collective-permute-start.6 = (bf16[256,1024]{1,0:T(8,128)(2,1)}, bf16[256,1024]{1,0:T(8,128)(2,1)S(1)}, u32[]{:S(2)}, u32[]{:S(2)}) collective-permute-start(bf16[256,1024]{1,0:T(8,128)(2,1)} %get-tuple-element.15), channel_id=1, source_target_pairs={{0,16},{1,0},{16,17},{17,1},{32,48},{33,32},{48,49},{49,33},{2,18}... | collective-permute-start | bytes 1572872 | tf_op jit(solution)/shard_map/ppermute | solution.py:219
  91.9 23.1 %collective-permute-start.7 = (bf16[256,1024]{1,0:T(8,128)(2,1)}, bf16[256,1024]{1,0:T(8,128)(2,1)S(1)}, u32[]{:S(2)}, u32[]{:S(2)}) collective-permute-start(bf16[256,1024]{1,0:T(8,128)(2,1)} %get-tuple-element.16), channel_id=1, source_target_pairs={{0,32},{1,48},{16,33},{17,49},{32,0},{33,16},{48,1},{49,17},{2,34}... | collective-permute-start | bytes 1572872 | tf_op jit(solution)/shard_map/ppermute | solution.py:219
  94.3 20.8 %collective-permute-start.8 = (bf16[256,1024]{1,0:T(8,128)(2,1)}, bf16[256,1024]{1,0:T(8,128)(2,1)S(1)}, u32[]{:S(2)}, u32[]{:S(2)}) collective-permute-start(bf16[256,1024]{1,0:T(8,128)(2,1)} %get-tuple-element.17), channel_id=1, source_target_pairs={{0,48},{1,32},{16,49},{17,33},{32,16},{33,0},{48,17},{49,1},{2,50}... | collective-permute-start | bytes 1572872 | tf_op jit(solution)/shard_map/ppermute | solution.py:219
  99.5 18.5 %all-to-all-start.2 = ((bf16[12,2,24,128]{3,2,1,0:T(8,128)(2,1)}), bf16[12,2,24,128]{3,2,1,0:T(8,128)(2,1)S(1)}, u32[]{:S(2)}, u32[]{:S(2)}) async-start(bf16[12,2,24,128]{3,2,1,0:T(8,128)(2,1)} %sum_y.1), calls=%async_computation.2 | async-start | bytes 294912 | tf_op jit(solution)/shard_map/all_to_all | solution.py:230
  134.0 11.7 %all-to-all-start.4 = ((bf16[4,12,24,128]{3,2,1,0:T(8,128)(2,1)}), bf16[4,12,24,128]{3,2,1,0:T(8,128)(2,1)S(1)}, u32[]{:S(2)}, u32[]{:S(2)}) async-start(bf16[4,12,24,128]{3,2,1,0:T(8,128)(2,1)} %split.1), calls=%async_computation.4 | async-start | bytes 589824 | tf_op jit(solution)/shard_map/all_to_all | solution.py:249
Sparse Core Ops, SparseCore 0:
  19.8 50.3 all-gather.1

commit v3 on v2

v3 whole, which is shorter than its diff:
```python
import functools
import math

import jax
import jax.numpy as jnp
from jax import lax
from jax.experimental import pallas as pl
from jax.experimental.pallas import tpu as pltpu
from jax.sharding import Mesh, PartitionSpec as P

NZ, NX, NY, NT = 12, 2, 8, 2
TOK, D, HS, COLS = 256, 8192, 128, 256
QUART = 128
HALF = NY // 2
STEPS = (0, 4, 2, 6)
TOKEN = jax.ShapeDtypeStruct((8, 128), jnp.float32)
FEAT = NY * QUART
KV = NT * COLS
ZCOLS = 24
BF16, F32 = jnp.bfloat16, jnp.float32


def prep_kernel(doc, act, gain, key_grad, out, token_out):
    t = lax.axis_index("t")
    token_out[...] = jnp.zeros(TOKEN.shape, TOKEN.dtype)
    rows = act.shape[0]
    token = pl.program_id(0) * rows + lax.broadcasted_iota(jnp.int32, (rows, HS), 0)
    second = doc[0, 0]
    third = second + doc[0, 1]
    fourth = third + doc[0, 2]
    start = jnp.where(
        token >= fourth,
        fourth,
        jnp.where(token >= third, third, jnp.where(token >= second, second, 0)),
    )
    lane = lax.broadcasted_iota(jnp.int32, (rows, HS), 1)
    half = (lane[:1] % (HS // 2)).astype(F32)
    freq = jnp.exp(half * (-2.0 * math.log(1000000.0) / HS))
    angle = (token - start).astype(F32) * freq
    cosine = jnp.cos(angle)
    sine = jnp.sin(angle)
    sine = jnp.where(lane < HS // 2, sine, -sine)
    for h in range(COLS // HS):
        v = key_grad[:, h * HS : (h + 1) * HS].astype(F32)
        v = (v * cosine + pltpu.roll(v, HS // 2, 1) * sine).astype(BF16)
        for i in range(4):
            out[i, :, FEAT + h * HS : FEAT + (h + 1) * HS] = v

    square = jnp.zeros((rows, 128), F32)
    for j in range(D // 128):
        v = act[:, j * 128 : (j + 1) * 128].astype(F32)
        square = square + v * v
    scale = lax.rsqrt(jnp.sum(square, axis=1, keepdims=True) * (1.0 / D) + 1e-06)
    for i in range(4):
        base = (i & 1) * (D // 2) + (2 * (i >> 1) + t) * QUART
        for j in range(NY):
            at = pl.ds(pl.multiple_of(base + j * 4 * QUART, 128), QUART)
            v = act[:, at].astype(F32) * scale * gain[:, at]
            out[i, :, j * QUART : (j + 1) * QUART] = v.astype(BF16)


def half_kernel(weight, after, out):
    del after
    half = NT * QUART
    out[...] = weight[pl.ds(pl.multiple_of(lax.axis_index("xl") * half, half), half), :]


def pack_kernel(got, after, out):
    del after
    out[...] = got[...]


def product(rot, got):
    rot = rot.reshape(4 * TOK, COLS)
    normed = got[:, :, :FEAT].reshape(4 * TOK, FEAT)
    g = lax.dot_general(rot, normed, (((0,), (0,)), ((), ())), preferred_element_type=F32)
    return g.astype(BF16)


def own_kernel(got, out):
    g = product(got[:, :, FEAT:], got)
    for y in range(NY):
        out[y] = g[:, y * QUART : (y + 1) * QUART]


def grad_kernel(got, other, own, after, out):
    del after
    t = lax.axis_index("t")
    mine = pl.ds(pl.multiple_of(t * COLS, COLS), COLS)
    rest = pl.ds(pl.multiple_of((1 - t) * COLS, COLS), COLS)
    g = product(other[...], got)
    for y in range(NY):
        out[y, mine, :] = own[y]
        out[y, rest, :] = g[:, y * QUART : (y + 1) * QUART]


def other_kernel(near, far, out):
    rows = pl.ds(pl.multiple_of((1 - lax.axis_index("t")) * QUART, QUART), QUART)
    for k in range(HALF):
        out[k] = near[k, rows, :]
        out[HALF + k] = far[k, rows, :]


def input_kernel(mine, other, near, far, w_other, *outs):
    outs, token = outs[:4], outs[4]
    token[...] = jnp.zeros(TOKEN.shape, TOKEN.dtype)
    xl, t, y = lax.axis_index("xl"), lax.axis_index("t"), lax.axis_index("y")
    lhs = []
    for r in range(4):
        i = 2 * (xl ^ (r >> 1)) + (t ^ (r & 1))
        lhs.append(jnp.concatenate([mine[i], other[i]], axis=1))
    lhs = jnp.concatenate(lhs, axis=0)
    own = pl.ds(pl.multiple_of(t * QUART, QUART), QUART)
    for half, weight in enumerate((near, far)):
        for j in range(0, HALF, 2):
            rhs = jnp.concatenate(
                [
                    jnp.concatenate([weight[k, own, :], w_other[HALF * half + k]], axis=1)
                    for k in (j, j + 1)
                ],
                axis=0,
            )
            p = lax.dot_general(lhs, rhs, (((1,), (1,)), ((), ())), preferred_element_type=F32)
            p = p.astype(BF16)
            for k in (j, j + 1):
                at = pl.ds(pl.multiple_of((y ^ STEPS[k] ^ half) * QUART, QUART), QUART)
                for r, out in enumerate(outs):
                    out[:, at] = p[r * TOK : (r + 1) * TOK, (k - j) * QUART : (k - j + 1) * QUART]


def sum_y_kernel(term, after, out):
    del after
    total = term[0].astype(F32)
    for y in range(1, NY):
        total = total + term[y].astype(F32)
    zero = jnp.zeros((NZ * ZCOLS - COLS, QUART), F32)
    for t in range(NT):
        padded = jnp.concatenate([total[t * COLS : (t + 1) * COLS, :], zero], axis=0)
        for z in range(NZ):
            out[z, t] = padded[z * ZCOLS : (z + 1) * ZCOLS, :].astype(BF16)


def sum_z_kernel(term, after0, after1, after2, after3, out):
    del after0, after1, after2, after3
    for t in range(NT):
        total = term[0, t].astype(F32)
        for z in range(1, NZ):
            total = total + term[z, t].astype(F32)
        total = (total * (1.0 / (NZ * NX))).astype(BF16)
        for z in range(NZ):
            out[z, t] = total


def split_kernel(term, after, out):
    del after
    for z in range(NZ):
        for t in range(NT):
            for xl in range(NX):
                out[NT * xl + t, z] = term[z, t]


def turn_kernel(term, out):
    for q in range(NX * NT):
        piece = jnp.concatenate([term[q, z].astype(F32) for z in range(NZ)], axis=0)
        out[q * QUART : (q + 1) * QUART, :] = piece[:COLS, :].T


def place_kernel(r0, r1, r2, r3, out, token):
    token[...] = jnp.zeros(TOKEN.shape, TOKEN.dtype)
    mine = 2 * lax.axis_index("xl") + lax.axis_index("xh")
    for r, got in enumerate((r0, r1, r2, r3)):
        q = mine ^ r
        for y in range(NY):
            at = pl.ds(pl.multiple_of(y * 4 * QUART + q * QUART, QUART), QUART)
            out[:, at] = got[:, y * QUART : (y + 1) * QUART]


def whole(count):
    return [pl.BlockSpec(memory_space=pltpu.VMEM)] * count


UNUSED = [pl.BlockSpec(memory_space=pl.ANY)]
SCALARS = pl.BlockSpec(memory_space=pltpu.SMEM)
PARAMS = pltpu.CompilerParams(vmem_limit_bytes=48 * 1024 * 1024)
LARGE = pltpu.CompilerParams(vmem_limit_bytes=60 * 1024 * 1024)


def per_device(activations, norm_gain, key_weight, key_grad, doc_lengths):
    rows = 64
    blocks, prepared = pl.pallas_call(
        prep_kernel,
        grid=(TOK // rows,),
        in_specs=[
            SCALARS,
            pl.BlockSpec((rows, D), lambda i: (i, 0)),
            pl.BlockSpec((1, D), lambda i: (0, 0)),
            pl.BlockSpec((rows, COLS), lambda i: (i, 0)),
        ],
        out_specs=[
            pl.BlockSpec((4, rows, FEAT + COLS), lambda i: (0, i, 0)),
            pl.BlockSpec(TOKEN.shape, lambda i: (0, 0)),
        ],
        out_shape=[jax.ShapeDtypeStruct((4, TOK, FEAT + COLS), BF16), TOKEN],
        compiler_params=LARGE,
        name="prep",
    )(doc_lengths, activations, norm_gain[None, :], key_grad)

    got = lax.all_to_all(blocks, ("xl", "xh"), 0, 0, tiled=True)

    half_weight = pl.pallas_call(
        half_kernel,
        in_specs=whole(1) + UNUSED,
        out_specs=whole(1)[0],
        out_shape=jax.ShapeDtypeStruct((NT * QUART, COLS), BF16),
        compiler_params=PARAMS,
        name="half_weight",
    )(key_weight, prepared)
    near = jnp.stack(
        [half_weight]
        + [lax.ppermute(half_weight, "y", [(i, i ^ e) for i in range(NY)]) for e in STEPS[1:]]
    )
    far = lax.ppermute(near, "y", [(i, i ^ 1) for i in range(NY)])

    mine = pl.pallas_call(
        pack_kernel,
        grid=(1,),
        in_specs=[pl.BlockSpec((4, TOK, COLS), lambda i: (0, 0, FEAT // COLS))] + UNUSED,
        out_specs=pl.BlockSpec((4, TOK, COLS), lambda i: (0, 0, 0)),
        out_shape=jax.ShapeDtypeStruct((4, TOK, COLS), BF16),
        compiler_params=PARAMS,
        name="pack",
    )(got, near)
    other = lax.ppermute(mine, "t", [(0, 1), (1, 0)])

    term = pl.pallas_call(
        own_kernel,
        in_specs=whole(1),
        out_specs=whole(1)[0],
        out_shape=jax.ShapeDtypeStruct((NY, COLS, QUART), BF16),
        compiler_params=PARAMS,
        name="own_grad",
    )(got)
    term = pl.pallas_call(
        grad_kernel,
        in_specs=whole(3) + UNUSED,
        out_specs=whole(1)[0],
        out_shape=jax.ShapeDtypeStruct((NY, KV, QUART), BF16),
        compiler_params=PARAMS,
        name="weight_grad",
    )(got, other, term, far)

    w_other = pl.pallas_call(
        other_kernel,
        in_specs=whole(2),
        out_specs=whole(1)[0],
        out_shape=jax.ShapeDtypeStruct((NY, QUART, COLS), BF16),
        compiler_params=PARAMS,
        name="w_other",
    )(near, far)
    w_other = lax.ppermute(w_other, "t", [(0, 1), (1, 0)])
    *products, multiplied = pl.pallas_call(
        input_kernel,
        in_specs=whole(5),
        out_specs=whole(5),
        out_shape=[jax.ShapeDtypeStruct((TOK, FEAT), BF16)] * 4 + [TOKEN],
        compiler_params=PARAMS,
        name="input_grad",
    )(mine, other, near, far, w_other)

    returned = []
    for r in range(4):
        r0, r1 = r >> 1, r & 1
        pairs = [
            (4 * i + 2 * j + k, 4 * (i ^ r0) + 2 * (k ^ r1) + j)
            for i in range(2)
            for j in range(2)
            for k in range(2)
        ]
        returned.append(lax.ppermute(products[r], ("xl", "xh", "t"), pairs))

    term = lax.all_to_all(term, "y", 0, 0, tiled=True)
    term = pl.pallas_call(
        sum_y_kernel,
        in_specs=whole(1) + [pl.BlockSpec(memory_space=pl.ANY)],
        out_specs=whole(1)[0],
        out_shape=jax.ShapeDtypeStruct((NZ, NT, ZCOLS, QUART), BF16),
        compiler_params=PARAMS,
        name="sum_y",
    )(term, multiplied)
    term = lax.all_to_all(term, "z", 0, 0, tiled=True)
    normed_grad, placed = pl.pallas_call(
        place_kernel,
        grid=(TOK // rows,),
        in_specs=[pl.BlockSpec((rows, FEAT), lambda i: (i, 0))] * 4,
        out_specs=[
            pl.BlockSpec((rows, 4 * FEAT), lambda i: (i, 0)),
            pl.BlockSpec(TOKEN.shape, lambda i: (0, 0)),
        ],
        out_shape=[jax.ShapeDtypeStruct((TOK, 4 * FEAT), BF16), TOKEN],
        compiler_params=PARAMS,
        name="placed",
    )(*returned)
    pieces = jax.ShapeDtypeStruct((NZ, NT, ZCOLS, QUART), BF16)
    term = pl.pallas_call(
        sum_z_kernel,
        in_specs=whole(1) + [pl.BlockSpec(memory_space=pl.ANY)] * 4,
        out_specs=whole(1)[0],
        out_shape=pieces,
        compiler_params=PARAMS,
        name="sum_z",
    )(term, *returned)
    term = lax.all_to_all(term, "z", 0, 0, tiled=True)
    term = pl.pallas_call(
        split_kernel,
        in_specs=whole(1) + UNUSED,
        out_specs=whole(1)[0],
        out_shape=jax.ShapeDtypeStruct((NX * NT, NZ, ZCOLS, QUART), BF16),
        compiler_params=PARAMS,
        name="split",
    )(term, placed)
    term = lax.all_to_all(term, ("xl", "t"), 0, 0, tiled=True)
    weight_grad = pl.pallas_call(
        turn_kernel,
        in_specs=whole(1),
        out_specs=whole(1)[0],
        out_shape=jax.ShapeDtypeStruct((NX * NT * QUART, COLS), F32),
        compiler_params=PARAMS,
        name="turn",
    )(term)

    return (weight_grad, normed_grad)


def solution(mesh):
    fine = Mesh(mesh.devices.reshape(NZ, NX, 2, NY, NT), ("z", "xl", "xh", "y", "t"))
    tokens = ("z", "xl", "xh", "y")
    return jax.shard_map(
        per_device,
        mesh=fine,
        in_specs=(
            P(tokens, None),
            P(),
            P(("xh", "y"), "t"),
            P(tokens, "t"),
            P(tokens, None),
        ),
        out_specs=(P(("xh", "y"), "t"), P(tokens, "t")),
        check_vma=False,
    )
```

time: 154 us -> 142 us (0.922)
  between operations: 14.2 us -> 0.85 us
  waiting for transfers between devices: 29.8 us -> 39.3 us
  blocking collectives: 15.2 us -> 12.1 us
  local copies, waits for them, and re-layouts: 5.6 us -> 2.83 us
    all_to_all x1 -> x2, waiting for transfers between devices: 2.92 us -> 20 us  [per_device(): term = lax.all_to_all(term, 'z', 0, 0, tiled=True)]
    all_to_all x1 -> x2, starting transfers between devices: 7.84 us -> 20.6 us  [per_device(): term = lax.all_to_all(term, 'z', 0, 0, tiled=True)]
    all_gather x1 -> x0, waiting for transfers between devices: 9 us -> none  [per_device(): lax.all_gather(half_shard, 'y', axis=0, tiled=True)]
    ppermute x4, waiting for transfers between devices: 7.75 us -> 0.01 us  [per_device(): returned.append(lax.ppermute(products[r], ('xl', 'xh', 't'), pairs))]
    ppermute x1, starting transfers between devices: 11.9 us -> 5.11 us  [per_device(): other = lax.ppermute(mine, 't', [(0, 1), (1, 0)])]
    all_to_all x2 -> x1, starting transfers between devices: 11 us -> 4.99 us  [per_device(): got = lax.all_to_all(blocks, ('xl', 'xh'), 0, 0, tiled=True)]
    all_to_all x2 -> x1, waiting for transfers between devices: 2.89 us -> 7.6 us  [per_device(): got = lax.all_to_all(blocks, ('xl', 'xh'), 0, 0, tiled=True)]
    ppermute x3 -> x4, starting transfers between devices: 9.58 us -> 14.1 us  [the longest x3 11.8 us: per_device(): lax.ppermute(half_weight, 'y', [(i, i ^ e) for i in range(NY)])]
  transfers between devices with their start and end apart: 14 -> 14, of which waited for: 8 -> 8; matrix products, arithmetic and copies ran while one was open for 1% -> 0% of each run, Pallas kernels for 9% -> 6%
where the time goes in v3:
time: 142 us; the launch traced here: 141 us
  starting transfers between devices  69.6 us (49%)
  waiting for transfers between devices  39.3 us (28%)
  Pallas kernels  16.1 us (11%)
  blocking collectives  12.1 us (9%)
  local copies, waits for them, and re-layouts  2.83 us (2%)
    all_to_all x2, starting transfers between devices, per_device(): term = lax.all_to_all(term, 'z', 0, 0, tiled=True)  20.6 us
    all_to_all x2, waiting for transfers between devices, per_device(): term = lax.all_to_all(term, 'z', 0, 0, tiled=True)  20 us
    ppermute x4, starting transfers between devices, per_device(): returned.append(lax.ppermute(products[r], ('xl', 'xh', 't'), pairs))  13.1 us
    all_to_all x1, blocking collectives, per_device(): term = lax.all_to_all(term, ('xl', 't'), 0, 0, tiled=True)  12.1 us
    ppermute x3, starting transfers between devices, per_device(): lax.ppermute(half_weight, 'y', [(i, i ^ e) for i in range(NY)])  11.8 us
    all_to_all x1, waiting for transfers between devices, per_device(): got = lax.all_to_all(blocks, ('xl', 'xh'), 0, 0, tiled=True)  7.6 us
    ppermute x3, waiting for transfers between devices, per_device(): lax.ppermute(half_weight, 'y', [(i, i ^ e) for i in range(NY)])  7.56 us
    all_to_all x1, starting transfers between devices, per_device(): term = lax.all_to_all(term, 'y', 0, 0, tiled=True)  6.95 us
  transfers between devices with their start and end apart: 14, of which 8 were waited for; matrix products, arithmetic and copies ran while one was open for 0% of the time, Pallas kernels for 6%

profile of v3, /device:TPU:1, one launch (start us, length us, event | category | flops | bytes accessed | tf_op | source)
XLA Modules:
  0.0 140.9 jit_solution(72170462079228689)
XLA Ops:
  0.6 5.3 %prep.1 = (bf16[4,256,1280]{2,1,0:T(8,128)(2,1)}, f32[8,128]{1,0:T(8,128)}) custom-call(s32[1,4]{1,0:T(1,128)} %doc.1, bf16[256,8192]{1,0:T(8,128)(2,1)} %act.1, f32[1,8192]{1,0:T(1,128)} %bitcast.9, bf16[256,256]{1,0:T(8,128)(2,1)} %key_grad.1), custom_call_target="tpu_custom_call" | custom-call | tf_op jit(solution)/shard_map/prep/pallas_call | solution.py:190
  5.9 5.0 %all-to-all-start = ((bf16[4,256,1280]{2,1,0:T(8,128)(2,1)}), bf16[4,256,1280]{2,1,0:T(8,128)(2,1)S(1)}, u32[]{:S(2)}, u32[]{:S(2)}) async-start(bf16[4,256,1280]{2,1,0:T(8,128)(2,1)} %get-tuple-element.11), calls=%async_computation | async-start | bytes 5242880 | tf_op jit(solution)/shard_map/all_to_all | solution.py:208
  10.9 0.0 copy-done.5
  10.9 0.0 copy-done.6
  10.9 5.9 %collective-permute-start.2 = (bf16[256,256]{1,0:T(8,128)(2,1)S(1)}, bf16[256,256]{1,0:T(8,128)(2,1)S(1)}, u32[]{:S(2)}, u32[]{:S(2)}) collective-permute-start(bf16[256,256]{1,0:T(8,128)(2,1)S(1)} %half_weight.1), channel_id=1, source_target_pairs={{0,12},{2,14},{4,8},{6,10},{8,4},{10,6},{12,0},{14,2},{1,13},{3,15... | collective-permute-start | bytes 393224 | tf_op jit(solution)/shard_map/ppermute | solution.py:220
  16.8 3.8 %collective-permute-start.1 = (bf16[256,256]{1,0:T(8,128)(2,1)S(1)}, bf16[256,256]{1,0:T(8,128)(2,1)S(1)}, u32[]{:S(2)}, u32[]{:S(2)}) collective-permute-start(bf16[256,256]{1,0:T(8,128)(2,1)S(1)} %half_weight.1), channel_id=1, source_target_pairs={{0,4},{2,6},{4,0},{6,2},{8,12},{10,14},{12,8},{14,10},{1,5},{3,7},... | collective-permute-start | bytes 393224 | tf_op jit(solution)/shard_map/ppermute | solution.py:220
  20.6 2.1 %collective-permute-start = (bf16[256,256]{1,0:T(8,128)(2,1)S(1)}, bf16[256,256]{1,0:T(8,128)(2,1)S(1)}, u32[]{:S(2)}, u32[]{:S(2)}) collective-permute-start(bf16[256,256]{1,0:T(8,128)(2,1)S(1)} %half_weight.1), channel_id=1, source_target_pairs={{0,8},{2,10},{4,12},{6,14},{8,0},{10,2},{12,4},{14,6},{1,9},{3,11}... | collective-permute-start | bytes 393224 | tf_op jit(solution)/shard_map/ppermute | solution.py:220
  22.8 0.0 collective-permute-done.2
  22.8 2.2 %collective-permute-done.1 = bf16[256,256]{1,0:T(8,128)(2,1)S(1)} collective-permute-done((bf16[256,256]{1,0:T(8,128)(2,1)S(1)}, bf16[256,256]{1,0:T(8,128)(2,1)S(1)}, u32[]{:S(2)}, u32[]{:S(2)}) %collective-permute-start.1) | collective-permute-done | bytes 131104 | tf_op jit(solution)/shard_map/ppermute | solution.py:220
  24.9 5.4 %collective-permute-done = bf16[256,256]{1,0:T(8,128)(2,1)S(1)} collective-permute-done((bf16[256,256]{1,0:T(8,128)(2,1)S(1)}, bf16[256,256]{1,0:T(8,128)(2,1)S(1)}, u32[]{:S(2)}, u32[]{:S(2)}) %collective-permute-start) | collective-permute-done | bytes 131104 | tf_op jit(solution)/shard_map/ppermute | solution.py:220
  30.3 0.1 pad_maximum_fusion.after.near
  30.4 2.3 %collective-permute-start.4 = (bf16[4,256,256]{2,1,0:T(8,128)(2,1)S(1)}, bf16[4,256,256]{2,1,0:T(8,128)(2,1)}, u32[]{:S(2)}, u32[]{:S(2)}) collective-permute-start(bf16[4,256,256]{2,1,0:T(8,128)(2,1)S(1)} %pad_maximum_fusion.after.near), channel_id=1, source_target_pairs={{0,2},{2,0},{4,6},{6,4},{8,10},{10,8},{12,14},{14,12},{1,3},{3,1},... | collective-permute-start | bytes 1572872 | tf_op jit(solution)/shard_map/ppermute | solution.py:222
  32.7 7.6 %all-to-all-done.got = bf16[4,256,1280]{2,1,0:T(8,128)(2,1)S(1)} async-done(((bf16[4,256,1280]{2,1,0:T(8,128)(2,1)}), bf16[4,256,1280]{2,1,0:T(8,128)(2,1)S(1)}, u32[]{:S(2)}, u32[]{:S(2)}) %all-to-all-start) | async-done | bytes 2621472 | tf_op jit(solution)/shard_map/all_to_all | solution.py:208
  40.4 0.0 copy-start.1
  40.4 5.1 %collective-permute-start.3 = (bf16[4,256,256]{2,1,0:T(8,128)(2,1)S(1)}, bf16[4,256,256]{2,1,0:T(8,128)(2,1)S(1)}, u32[]{:S(2)}, u32[]{:S(2)}) collective-permute-start(bf16[4,256,256]{2,1,0:T(8,128)(2,1)S(1)} %pack.1.mine), channel_id=1, source_target_pairs={{0,1},{1,0},{2,3},{3,2},{4,5},{5,4},{6,7},{7,6},{8,9},{9,8},{10,11... | collective-permute-start | bytes 1572872 | tf_op jit(solution)/shard_map/ppermute | solution.py:233
  45.5 0.7 own_grad.1.own
  46.2 0.0 collective-permute-done.4.after.far
  46.2 0.0 copy-done.1
  46.2 0.8 collective-permute-done.3.other
  47.0 0.7 weight_grad.1
  47.7 0.0 copy-start
  47.8 1.0 copy-done
  48.7 0.8 copy-done.3
  49.5 7.0 %all-to-all-start.1 = ((bf16[8,512,128]{2,1,0:T(8,128)(2,1)}), bf16[8,512,128]{2,1,0:T(8,128)(2,1)S(1)}, u32[]{:S(2)}, u32[]{:S(2)}) async-start(bf16[8,512,128]{2,1,0:T(8,128)(2,1)} %copy-done), calls=%async_computation.1 | async-start | bytes 2097152 | tf_op jit(solution)/shard_map/all_to_all | solution.py:281
  56.5 1.1 w_other.1
  57.6 4.7 %collective-permute-start.5 = (bf16[8,128,256]{2,1,0:T(8,128)(2,1)S(1)}, bf16[8,128,256]{2,1,0:T(8,128)(2,1)S(1)}, u32[]{:S(2)}, u32[]{:S(2)}) collective-permute-start(bf16[8,128,256]{2,1,0:T(8,128)(2,1)S(1)} %w_other.1), channel_id=1, source_target_pairs={{0,1},{1,0},{2,3},{3,2},{4,5},{5,4},{6,7},{7,6},{8,9},{9,8},{10,11... | collective-permute-start | bytes 1572872 | tf_op jit(solution)/shard_map/ppermute | solution.py:260
  62.3 1.5 %collective-permute-done.5.w_other = bf16[8,128,256]{2,1,0:T(8,128)(2,1)S(1)} collective-permute-done((bf16[8,128,256]{2,1,0:T(8,128)(2,1)S(1)}, bf16[8,128,256]{2,1,0:T(8,128)(2,1)S(1)}, u32[]{:S(2)}, u32[]{:S(2)}) %collective-permute-start.5) | collective-permute-done | bytes 524320 | tf_op jit(solution)/shard_map/ppermute | solution.py:260
  63.8 0.0 copy-done.2
  63.8 1.0 copy-done.4
  64.8 3.7 %input_grad.1 = (bf16[256,1024]{1,0:T(8,128)(2,1)}, bf16[256,1024]{1,0:T(8,128)(2,1)}, bf16[256,1024]{1,0:T(8,128)(2,1)}, bf16[256,1024]{1,0:T(8,128)(2,1)}, f32[8,128]{1,0:T(8,128)S(1)}) custom-call(bf16[4,256,256]{2,1,0:T(8,128)(2,1)S(1)} %copy-done.2, bf16[4,256,256]{2,1,0:T(8,128)(2,1)S(1)} %copy-done.4, ...), custom_call_target="tpu_custom_call" | custom-call | tf_op jit(solution)/shard_map/input_grad/pallas_call | solution.py:261
  68.6 5.3 %collective-permute-start.6 = (bf16[256,1024]{1,0:T(8,128)(2,1)}, bf16[256,1024]{1,0:T(8,128)(2,1)S(1)}, u32[]{:S(2)}, u32[]{:S(2)}) collective-permute-start(bf16[256,1024]{1,0:T(8,128)(2,1)} %get-tuple-element.14), channel_id=1, source_target_pairs={{0,0},{1,16},{16,1},{17,17},{32,32},{33,48},{48,33},{49,49},{2,2},... | collective-permute-start | bytes 1572872 | tf_op jit(solution)/shard_map/ppermute | solution.py:279
  73.9 1.9 %collective-permute-start.7 = (bf16[256,1024]{1,0:T(8,128)(2,1)}, bf16[256,1024]{1,0:T(8,128)(2,1)S(1)}, u32[]{:S(2)}, u32[]{:S(2)}) collective-permute-start(bf16[256,1024]{1,0:T(8,128)(2,1)} %get-tuple-element.15), channel_id=1, source_target_pairs={{0,16},{1,0},{16,17},{17,1},{32,48},{33,32},{48,49},{49,33},{2,18}... | collective-permute-start | bytes 1572872 | tf_op jit(solution)/shard_map/ppermute | solution.py:279
  75.9 2.8 %collective-permute-start.8 = (bf16[256,1024]{1,0:T(8,128)(2,1)}, bf16[256,1024]{1,0:T(8,128)(2,1)S(1)}, u32[]{:S(2)}, u32[]{:S(2)}) collective-permute-start(bf16[256,1024]{1,0:T(8,128)(2,1)} %get-tuple-element.16), channel_id=1, source_target_pairs={{0,32},{1,48},{16,33},{17,49},{32,0},{33,16},{48,1},{49,17},{2,34}... | collective-permute-start | bytes 1572872 | tf_op jit(solution)/shard_map/ppermute | solution.py:279
  78.7 3.0 %collective-permute-start.9 = (bf16[256,1024]{1,0:T(8,128)(2,1)}, bf16[256,1024]{1,0:T(8,128)(2,1)S(1)}, u32[]{:S(2)}, u32[]{:S(2)}) collective-permute-start(bf16[256,1024]{1,0:T(8,128)(2,1)} %get-tuple-element.17), channel_id=1, source_target_pairs={{0,48},{1,32},{16,49},{17,33},{32,16},{33,0},{48,17},{49,1},{2,50}... | collective-permute-start | bytes 1572872 | tf_op jit(solution)/shard_map/ppermute | solution.py:279
  81.7 1.9 %all-to-all-done.1.term = bf16[8,512,128]{2,1,0:T(8,128)(2,1)S(1)} async-done(((bf16[8,512,128]{2,1,0:T(8,128)(2,1)}), bf16[8,512,128]{2,1,0:T(8,128)(2,1)S(1)}, u32[]{:S(2)}, u32[]{:S(2)}) %all-to-all-start.1) | async-done | bytes 1048608 | tf_op jit(solution)/shard_map/all_to_all | solution.py:281
  83.6 0.8 sum_y.1
  84.4 17.0 %all-to-all-start.2 = ((bf16[12,2,24,128]{3,2,1,0:T(8,128)(2,1)}), bf16[12,2,24,128]{3,2,1,0:T(8,128)(2,1)S(1)}, u32[]{:S(2)}, u32[]{:S(2)}) async-start(bf16[12,2,24,128]{3,2,1,0:T(8,128)(2,1)} %sum_y.1), calls=%async_computation.2 | async-start | bytes 294912 | tf_op jit(solution)/shard_map/all_to_all | solution.py:290
  101.4 0.0 collective-permute-done.6.after0.r0
  101.4 0.0 collective-permute-done.7.after1.r1
  101.4 0.0 collective-permute-done.8.after2.r2
  101.4 0.0 collective-permute-done.9.after3.r3
  101.4 11.3 %all-to-all-done.2.term = bf16[12,2,24,128]{3,2,1,0:T(8,128)(2,1)S(1)} async-done(((bf16[12,2,24,128]{3,2,1,0:T(8,128)(2,1)}), bf16[12,2,24,128]{3,2,1,0:T(8,128)(2,1)S(1)}, u32[]{:S(2)}, u32[]{:S(2)}) %all-to-all-start.2) | async-done | bytes 147488 | tf_op jit(solution)/shard_map/all_to_all | solution.py:290
  112.8 0.7 sum_z.1
  113.4 3.6 %all-to-all-start.3 = ((bf16[12,2,24,128]{3,2,1,0:T(8,128)(2,1)}), bf16[12,2,24,128]{3,2,1,0:T(8,128)(2,1)S(1)}, u32[]{:S(2)}, u32[]{:S(2)}) async-start(bf16[12,2,24,128]{3,2,1,0:T(8,128)(2,1)} %sum_z.1), calls=%async_computation.3 | async-start | bytes 294912 | tf_op jit(solution)/shard_map/all_to_all | solution.py:312
  117.1 2.1 %placed.1 = (bf16[256,4096]{1,0:T(8,128)(2,1)}, f32[8,128]{1,0:T(8,128)S(1)}) custom-call(bf16[256,1024]{1,0:T(8,128)(2,1)S(1)} %collective-permute-done.6.after0.r0, bf16[256,1024]{1,0:T(8,128)(2,1)S(1)} %collective-permute-done.7.after1.r1, bf16[256,1024]{1,0:T(8,128)(2,1)S(1)} %collective-permute-done.8.after2.r2, ...), custom_call_target="tpu_custom_call" | custom-call | tf_op jit(solution)/shard_map/placed/pallas_call | solution.py:291
  119.1 8.7 %all-to-all-done.3.term = bf16[12,2,24,128]{3,2,1,0:T(8,128)(2,1)S(1)} async-done(((bf16[12,2,24,128]{3,2,1,0:T(8,128)(2,1)}), bf16[12,2,24,128]{3,2,1,0:T(8,128)(2,1)S(1)}, u32[]{:S(2)}, u32[]{:S(2)}) %all-to-all-start.3) | async-done | bytes 147488 | tf_op jit(solution)/shard_map/all_to_all | solution.py:312
  127.8 12.1 %all_to_all.25.term = bf16[4,12,24,128]{3,2,1,0:T(8,128)(2,1)S(1)} all-to-all(bf16[4,12,24,128]{3,2,1,0:T(8,128)(2,1)S(1)} %split.1), channel_id=1, replica_groups=mesh['z'=12,'xl'=2,'xh'=2,'y'=8,'t'=2] {'xl','t'}, dimensions={0} | all-to-all | bytes 589824 | tf_op jit(solution)/shard_map/all_to_all | solution.py:321
  140.0 0.9 turn.1
  (8 shorter events, 0.1 us)
Async XLA Ops:
  5.9 5.0 %copy-start.5 = (bf16[512,256]{1,0:T(8,128)(2,1)S(1)}, bf16[512,256]{1,0:T(8,128)(2,1)}, u32[]{:S(2)}) copy-start(bf16[512,256]{1,0:T(8,128)(2,1)} %weight.1) | copy-start | bytes 786436
  5.9 5.0 %copy-start.6 = (f32[8,128]{1,0:T(8,128)S(1)}, f32[8,128]{1,0:T(8,128)}, u32[]{:S(2)}) copy-start(f32[8,128]{1,0:T(8,128)} %get-tuple-element.12.after) | copy-start | bytes 12292
  5.9 34.4 %all-to-all-start = ((bf16[4,256,1280]{2,1,0:T(8,128)(2,1)}), bf16[4,256,1280]{2,1,0:T(8,128)(2,1)S(1)}, u32[]{:S(2)}, u32[]{:S(2)}) async-start(bf16[4,256,1280]{2,1,0:T(8,128)(2,1)} %get-tuple-element.11), calls=%async_computation | async-start | bytes 5242880 | tf_op jit(solution)/shard_map/all_to_all | solution.py:208
  10.9 11.8 %collective-permute-start.2 = (bf16[256,256]{1,0:T(8,128)(2,1)S(1)}, bf16[256,256]{1,0:T(8,128)(2,1)S(1)}, u32[]{:S(2)}, u32[]{:S(2)}) collective-permute-start(bf16[256,256]{1,0:T(8,128)(2,1)S(1)} %half_weight.1), channel_id=1, source_target_pairs={{0,12},{2,14},{4,8},{6,10},{8,4},{10,6},{12,0},{14,2},{1,13},{3,15... | collective-permute-start | bytes 393224 | tf_op jit(solution)/shard_map/ppermute | solution.py:220
  16.8 8.1 %collective-permute-start.1 = (bf16[256,256]{1,0:T(8,128)(2,1)S(1)}, bf16[256,256]{1,0:T(8,128)(2,1)S(1)}, u32[]{:S(2)}, u32[]{:S(2)}) collective-permute-start(bf16[256,256]{1,0:T(8,128)(2,1)S(1)} %half_weight.1), channel_id=1, source_target_pairs={{0,4},{2,6},{4,0},{6,2},{8,12},{10,14},{12,8},{14,10},{1,5},{3,7},... | collective-permute-start | bytes 393224 | tf_op jit(solution)/shard_map/ppermute | solution.py:220
  20.6 9.7 %collective-permute-start = (bf16[256,256]{1,0:T(8,128)(2,1)S(1)}, bf16[256,256]{1,0:T(8,128)(2,1)S(1)}, u32[]{:S(2)}, u32[]{:S(2)}) collective-permute-start(bf16[256,256]{1,0:T(8,128)(2,1)S(1)} %half_weight.1), channel_id=1, source_target_pairs={{0,8},{2,10},{4,12},{6,14},{8,0},{10,2},{12,4},{14,6},{1,9},{3,11}... | collective-permute-start | bytes 393224 | tf_op jit(solution)/shard_map/ppermute | solution.py:220
  30.4 15.8 %collective-permute-start.4 = (bf16[4,256,256]{2,1,0:T(8,128)(2,1)S(1)}, bf16[4,256,256]{2,1,0:T(8,128)(2,1)}, u32[]{:S(2)}, u32[]{:S(2)}) collective-permute-start(bf16[4,256,256]{2,1,0:T(8,128)(2,1)S(1)} %pad_maximum_fusion.after.near), channel_id=1, source_target_pairs={{0,2},{2,0},{4,6},{6,4},{8,10},{10,8},{12,14},{14,12},{1,3},{3,1},... | collective-permute-start | bytes 1572872 | tf_op jit(solution)/shard_map/ppermute | solution.py:222
  40.4 5.9 %copy-start.1 = (bf16[4,256,256]{2,1,0:T(8,128)(2,1)}, bf16[4,256,256]{2,1,0:T(8,128)(2,1)S(1)}, u32[]{:S(2)}) copy-start(bf16[4,256,256]{2,1,0:T(8,128)(2,1)S(1)} %pack.1.mine) | copy-start | bytes 1572868
  40.4 6.6 %collective-permute-start.3 = (bf16[4,256,256]{2,1,0:T(8,128)(2,1)S(1)}, bf16[4,256,256]{2,1,0:T(8,128)(2,1)S(1)}, u32[]{:S(2)}, u32[]{:S(2)}) collective-permute-start(bf16[4,256,256]{2,1,0:T(8,128)(2,1)S(1)} %pack.1.mine), channel_id=1, source_target_pairs={{0,1},{1,0},{2,3},{3,2},{4,5},{5,4},{6,7},{7,6},{8,9},{9,8},{10,11... | collective-permute-start | bytes 1572872 | tf_op jit(solution)/shard_map/ppermute | solution.py:233
  47.7 1.0 copy-start
  48.7 0.8 copy-start.3
  49.5 14.3 %copy-start.2 = (bf16[4,256,256]{2,1,0:T(8,128)(2,1)S(1)}, bf16[4,256,256]{2,1,0:T(8,128)(2,1)}, u32[]{:S(2)}) copy-start(bf16[4,256,256]{2,1,0:T(8,128)(2,1)} %copy-done.1) | copy-start | bytes 1572868
  49.5 34.1 %all-to-all-start.1 = ((bf16[8,512,128]{2,1,0:T(8,128)(2,1)}), bf16[8,512,128]{2,1,0:T(8,128)(2,1)S(1)}, u32[]{:S(2)}, u32[]{:S(2)}) async-start(bf16[8,512,128]{2,1,0:T(8,128)(2,1)} %copy-done), calls=%async_computation.1 | async-start | bytes 2097152 | tf_op jit(solution)/shard_map/all_to_all | solution.py:281
  57.6 6.2 %collective-permute-start.5 = (bf16[8,128,256]{2,1,0:T(8,128)(2,1)S(1)}, bf16[8,128,256]{2,1,0:T(8,128)(2,1)S(1)}, u32[]{:S(2)}, u32[]{:S(2)}) collective-permute-start(bf16[8,128,256]{2,1,0:T(8,128)(2,1)S(1)} %w_other.1), channel_id=1, source_target_pairs={{0,1},{1,0},{2,3},{3,2},{4,5},{5,4},{6,7},{7,6},{8,9},{9,8},{10,11... | collective-permute-start | bytes 1572872 | tf_op jit(solution)/shard_map/ppermute | solution.py:260
  63.8 1.0 copy-start.4
  68.6 32.8 %collective-permute-start.6 = (bf16[256,1024]{1,0:T(8,128)(2,1)}, bf16[256,1024]{1,0:T(8,128)(2,1)S(1)}, u32[]{:S(2)}, u32[]{:S(2)}) collective-permute-start(bf16[256,1024]{1,0:T(8,128)(2,1)} %get-tuple-element.14), channel_id=1, source_target_pairs={{0,0},{1,16},{16,1},{17,17},{32,32},{33,48},{48,33},{49,49},{2,2},... | collective-permute-start | bytes 1572872 | tf_op jit(solution)/shard_map/ppermute | solution.py:279
  73.9 27.5 %collective-permute-start.7 = (bf16[256,1024]{1,0:T(8,128)(2,1)}, bf16[256,1024]{1,0:T(8,128)(2,1)S(1)}, u32[]{:S(2)}, u32[]{:S(2)}) collective-permute-start(bf16[256,1024]{1,0:T(8,128)(2,1)} %get-tuple-element.15), channel_id=1, source_target_pairs={{0,16},{1,0},{16,17},{17,1},{32,48},{33,32},{48,49},{49,33},{2,18}... | collective-permute-start | bytes 1572872 | tf_op jit(solution)/shard_map/ppermute | solution.py:279
  75.9 25.6 %collective-permute-start.8 = (bf16[256,1024]{1,0:T(8,128)(2,1)}, bf16[256,1024]{1,0:T(8,128)(2,1)S(1)}, u32[]{:S(2)}, u32[]{:S(2)}) collective-permute-start(bf16[256,1024]{1,0:T(8,128)(2,1)} %get-tuple-element.16), channel_id=1, source_target_pairs={{0,32},{1,48},{16,33},{17,49},{32,0},{33,16},{48,1},{49,17},{2,34}... | collective-permute-start | bytes 1572872 | tf_op jit(solution)/shard_map/ppermute | solution.py:279
  78.7 22.8 %collective-permute-start.9 = (bf16[256,1024]{1,0:T(8,128)(2,1)}, bf16[256,1024]{1,0:T(8,128)(2,1)S(1)}, u32[]{:S(2)}, u32[]{:S(2)}) collective-permute-start(bf16[256,1024]{1,0:T(8,128)(2,1)} %get-tuple-element.17), channel_id=1, source_target_pairs={{0,48},{1,32},{16,49},{17,33},{32,16},{33,0},{48,17},{49,1},{2,50}... | collective-permute-start | bytes 1572872 | tf_op jit(solution)/shard_map/ppermute | solution.py:279
  84.4 28.4 %all-to-all-start.2 = ((bf16[12,2,24,128]{3,2,1,0:T(8,128)(2,1)}), bf16[12,2,24,128]{3,2,1,0:T(8,128)(2,1)S(1)}, u32[]{:S(2)}, u32[]{:S(2)}) async-start(bf16[12,2,24,128]{3,2,1,0:T(8,128)(2,1)} %sum_y.1), calls=%async_computation.2 | async-start | bytes 294912 | tf_op jit(solution)/shard_map/all_to_all | solution.py:290
  113.4 14.4 %all-to-all-start.3 = ((bf16[12,2,24,128]{3,2,1,0:T(8,128)(2,1)}), bf16[12,2,24,128]{3,2,1,0:T(8,128)(2,1)S(1)}, u32[]{:S(2)}, u32[]{:S(2)}) async-start(bf16[12,2,24,128]{3,2,1,0:T(8,128)(2,1)} %sum_z.1), calls=%async_computation.3 | async-start | bytes 294912 | tf_op jit(solution)/shard_map/all_to_all | solution.py:312

commit v4 on v3

--- a/solution.py
+++ b/solution.py
@@ -12,7 +12,7 @@
 TOK, D, HS, COLS = 256, 8192, 128, 256
 QUART = 128
 HALF = NY // 2
-STEPS = (0, 4, 2, 6)
+STEPS = (0, 6, 2, 4)
 TOKEN = jax.ShapeDtypeStruct((8, 128), jnp.float32)
 FEAT = NY * QUART
 KV = NT * COLS
@@ -94,38 +94,43 @@
         out[y, rest, :] = g[:, y * QUART : (y + 1) * QUART]
 
 
-def other_kernel(near, far, out):
+def other_kernel(mine, near, far, out):
+    out[: 4 * TOK, :] = mine[...].reshape(4 * TOK, COLS)
     rows = pl.ds(pl.multiple_of((1 - lax.axis_index("t")) * QUART, QUART), QUART)
-    for k in range(HALF):
-        out[k] = near[k, rows, :]
-        out[HALF + k] = far[k, rows, :]
-
-
-def input_kernel(mine, other, near, far, w_other, *outs):
+    for k in range(NY):
+        shard = near[k, rows, :] if k < HALF else far[k - HALF, rows, :]
+        out[4 * TOK + k * QUART : 4 * TOK + (k + 1) * QUART, :] = shard
+
+
+def input_kernel(mine, near, far, other, *outs):
     outs, token = outs[:4], outs[4]
     token[...] = jnp.zeros(TOKEN.shape, TOKEN.dtype)
-    xl, t, y = lax.axis_index("xl"), lax.axis_index("t"), lax.axis_index("y")
-    lhs = []
-    for r in range(4):
-        i = 2 * (xl ^ (r >> 1)) + (t ^ (r & 1))
-        lhs.append(jnp.concatenate([mine[i], other[i]], axis=1))
-    lhs = jnp.concatenate(lhs, axis=0)
+    xl, t = lax.axis_index("xl"), lax.axis_index("t")
     own = pl.ds(pl.multiple_of(t * QUART, QUART), QUART)
-    for half, weight in enumerate((near, far)):
+
+    def multiply(weight, h):
+        lhs = []
+        for r in range(4):
+            i = 2 * (xl ^ (r >> 1)) + (t ^ (r & 1))
+            rows = pl.ds(pl.multiple_of(i * TOK, TOK), TOK)
+            lhs.append(jnp.concatenate([mine[i], other[rows, :]], axis=1))
+        lhs = jnp.concatenate(lhs, axis=0)
         for j in range(0, HALF, 2):
+            at = 4 * TOK + (HALF * h + j) * QUART
             rhs = jnp.concatenate(
                 [
-                    jnp.concatenate([weight[k, own, :], w_other[HALF * half + k]], axis=1)
-                    for k in (j, j + 1)
+                    jnp.concatenate([weight[j + k, own, :] for k in range(2)], axis=0),
+                    other[at : at + 2 * QUART, :],
                 ],
-                axis=0,
+                axis=1,
             )
             p = lax.dot_general(lhs, rhs, (((1,), (1,)), ((), ())), preferred_element_type=F32)
             p = p.astype(BF16)
-            for k in (j, j + 1):
-                at = pl.ds(pl.multiple_of((y ^ STEPS[k] ^ half) * QUART, QUART), QUART)
-                for r, out in enumerate(outs):
-                    out[:, at] = p[r * TOK : (r + 1) * TOK, (k - j) * QUART : (k - j + 1) * QUART]
+            for r, out in enumerate(outs):
+                out[:, j * QUART : (j + 2) * QUART] = p[r * TOK : (r + 1) * TOK, :]
+
+    pl.when(pl.program_id(0) == 0)(functools.partial(multiply, near, 0))
+    pl.when(pl.program_id(0) == 1)(functools.partial(multiply, far, 1))
 
 
 def sum_y_kernel(term, after, out):
@@ -167,12 +172,13 @@
 
 def place_kernel(r0, r1, r2, r3, out, token):
     token[...] = jnp.zeros(TOKEN.shape, TOKEN.dtype)
-    mine = 2 * lax.axis_index("xl") + lax.axis_index("xh")
+    mine, y = 2 * lax.axis_index("xl") + lax.axis_index("xh"), lax.axis_index("y")
     for r, got in enumerate((r0, r1, r2, r3)):
         q = mine ^ r
-        for y in range(NY):
-            at = pl.ds(pl.multiple_of(y * 4 * QUART + q * QUART, QUART), QUART)
-            out[:, at] = got[:, y * QUART : (y + 1) * QUART]
+        for k in range(NY):
+            block = y ^ STEPS[k % HALF] ^ (k // HALF)
+            at = pl.ds(pl.multiple_of(block * 4 * QUART + q * QUART, QUART), QUART)
+            out[:, at] = got[:, k * QUART : (k + 1) * QUART]
 
 
 def whole(count):
@@ -186,7 +192,7 @@
 
 
 def per_device(activations, norm_gain, key_weight, key_grad, doc_lengths):
-    rows = 64
+    rows = 128
     blocks, prepared = pl.pallas_call(
         prep_kernel,
         grid=(TOK // rows,),
@@ -249,23 +255,26 @@
         name="weight_grad",
     )(got, other, term, far)
 
-    w_other = pl.pallas_call(
+    swapped = pl.pallas_call(
         other_kernel,
-        in_specs=whole(2),
-        out_specs=whole(1)[0],
-        out_shape=jax.ShapeDtypeStruct((NY, QUART, COLS), BF16),
-        compiler_params=PARAMS,
-        name="w_other",
-    )(near, far)
-    w_other = lax.ppermute(w_other, "t", [(0, 1), (1, 0)])
+        in_specs=whole(3),
+        out_specs=whole(1)[0],
+        out_shape=jax.ShapeDtypeStruct((4 * TOK + FEAT, COLS), BF16),
+        compiler_params=PARAMS,
+        name="to_other",
+    )(mine, near, far)
+    swapped = lax.ppermute(swapped, "t", [(0, 1), (1, 0)])
+    shards = pl.BlockSpec((4, TOK, COLS), lambda i: (0, 0, 0))
     *products, multiplied = pl.pallas_call(
         input_kernel,
-        in_specs=whole(5),
-        out_specs=whole(5),
+        grid=(2,),
+        in_specs=[shards] * 3 + [pl.BlockSpec((4 * TOK + FEAT, COLS), lambda i: (0, 0))],
+        out_specs=[pl.BlockSpec((TOK, FEAT // 2), lambda i: (0, i))] * 4
+        + [pl.BlockSpec(TOKEN.shape, lambda i: (0, 0))],
         out_shape=[jax.ShapeDtypeStruct((TOK, FEAT), BF16)] * 4 + [TOKEN],
         compiler_params=PARAMS,
         name="input_grad",
-    )(mine, other, near, far, w_other)
+    )(mine, near, far, swapped)
 
     returned = []
     for r in range(4):
@@ -288,6 +297,7 @@
         name="sum_y",
     )(term, multiplied)
     term = lax.all_to_all(term, "z", 0, 0, tiled=True)
+    rows = 64
     normed_grad, placed = pl.pallas_call(
         place_kernel,
         grid=(TOK // rows,),

time: 142 us -> 140 us (0.986)
  starting transfers between devices: 69.6 us -> 64.6 us
  waiting for transfers between devices: 39.3 us -> 44.2 us
    all_to_all x1, waiting for transfers between devices: 1.89 us -> 5.75 us  [per_device(): term = lax.all_to_all(term, 'y', 0, 0, tiled=True)]
    ppermute x3, waiting for transfers between devices: 7.56 us -> 10.3 us  [per_device(): lax.ppermute(half_weight, 'y', [(i, i ^ e) for i in range(NY)])]
    all_to_all x1, waiting for transfers between devices: 7.6 us -> 5.3 us  [per_device(): got = lax.all_to_all(blocks, ('xl', 'xh'), 0, 0, tiled=True)]
    ppermute x1, starting transfers between devices: 4.72 us -> 2.57 us  [per_device(): swapped = lax.ppermute(swapped, 't', [(0, 1), (1, 0)])]
    all_to_all x2, starting transfers between devices: 20.6 us -> 18.5 us  [per_device(): term = lax.all_to_all(term, 'z', 0, 0, tiled=True)]
where the time goes in v4:
time: 140 us; the launch traced here: 139 us
  starting transfers between devices  64.6 us (46%)
  waiting for transfers between devices  44.2 us (32%)
  Pallas kernels  15.6 us (11%)
  blocking collectives  12.1 us (9%)
  local copies, waits for them, and re-layouts  2.02 us (1%)
    all_to_all x2, waiting for transfers between devices, per_device(): term = lax.all_to_all(term, 'z', 0, 0, tiled=True)  19.9 us
    all_to_all x2, starting transfers between devices, per_device(): term = lax.all_to_all(term, 'z', 0, 0, tiled=True)  18.5 us
    ppermute x4, starting transfers between devices, per_device(): returned.append(lax.ppermute(products[r], ('xl', 'xh', 't'), pairs))  12.9 us
    all_to_all x1, blocking collectives, per_device(): term = lax.all_to_all(term, ('xl', 't'), 0, 0, tiled=True)  12.1 us
    ppermute x3, starting transfers between devices, per_device(): lax.ppermute(half_weight, 'y', [(i, i ^ e) for i in range(NY)])  11.8 us
    ppermute x3, waiting for transfers between devices, per_device(): lax.ppermute(half_weight, 'y', [(i, i ^ e) for i in range(NY)])  10.3 us
    all_to_all x1, starting transfers between devices, per_device(): term = lax.all_to_all(term, 'y', 0, 0, tiled=True)  6.82 us
    all_to_all x1, waiting for transfers between devices, per_device(): term = lax.all_to_all(term, 'y', 0, 0, tiled=True)  5.75 us
  transfers between devices with their start and end apart: 14, of which 8 were waited for; matrix products, arithmetic and copies ran while one was open for 0% of the time, Pallas kernels for 6%

profile of v4, /device:TPU:1, one launch (start us, length us, event | category | flops | bytes accessed | tf_op | source)
XLA Modules:
  0.0 139.4 jit_solution(4414030258112616375)
XLA Ops:
  0.6 4.8 %prep.1 = (bf16[4,256,1280]{2,1,0:T(8,128)(2,1)}, f32[8,128]{1,0:T(8,128)}) custom-call(s32[1,4]{1,0:T(1,128)} %doc.1, bf16[256,8192]{1,0:T(8,128)(2,1)} %act.1, f32[1,8192]{1,0:T(1,128)} %bitcast.9, bf16[256,256]{1,0:T(8,128)(2,1)} %key_grad.1), custom_call_target="tpu_custom_call" | custom-call | tf_op jit(solution)/shard_map/prep/pallas_call | solution.py:196
  5.4 0.0 copy-start.3
  5.4 0.0 copy-start.4
  5.4 5.0 %all-to-all-start = ((bf16[4,256,1280]{2,1,0:T(8,128)(2,1)}), bf16[4,256,1280]{2,1,0:T(8,128)(2,1)S(1)}, u32[]{:S(2)}, u32[]{:S(2)}) async-start(bf16[4,256,1280]{2,1,0:T(8,128)(2,1)} %get-tuple-element.11), calls=%async_computation | async-start | bytes 5242880 | tf_op jit(solution)/shard_map/all_to_all | solution.py:214
  10.4 0.0 copy-done.3
  10.4 0.0 copy-done.4
  10.4 7.5 %collective-permute-start.2 = (bf16[256,256]{1,0:T(8,128)(2,1)S(1)}, bf16[256,256]{1,0:T(8,128)(2,1)S(1)}, u32[]{:S(2)}, u32[]{:S(2)}) collective-permute-start(bf16[256,256]{1,0:T(8,128)(2,1)S(1)} %half_weight.1), channel_id=1, source_target_pairs={{0,8},{2,10},{4,12},{6,14},{8,0},{10,2},{12,4},{14,6},{1,9},{3,11}... | collective-permute-start | bytes 393224 | tf_op jit(solution)/shard_map/ppermute | solution.py:226
  17.9 2.4 %collective-permute-start.1 = (bf16[256,256]{1,0:T(8,128)(2,1)S(1)}, bf16[256,256]{1,0:T(8,128)(2,1)S(1)}, u32[]{:S(2)}, u32[]{:S(2)}) collective-permute-start(bf16[256,256]{1,0:T(8,128)(2,1)S(1)} %half_weight.1), channel_id=1, source_target_pairs={{0,4},{2,6},{4,0},{6,2},{8,12},{10,14},{12,8},{14,10},{1,5},{3,7},... | collective-permute-start | bytes 393224 | tf_op jit(solution)/shard_map/ppermute | solution.py:226
  20.3 1.9 %collective-permute-start = (bf16[256,256]{1,0:T(8,128)(2,1)S(1)}, bf16[256,256]{1,0:T(8,128)(2,1)S(1)}, u32[]{:S(2)}, u32[]{:S(2)}) collective-permute-start(bf16[256,256]{1,0:T(8,128)(2,1)S(1)} %half_weight.1), channel_id=1, source_target_pairs={{0,12},{2,14},{4,8},{6,10},{8,4},{10,6},{12,0},{14,2},{1,13},{3,15... | collective-permute-start | bytes 393224 | tf_op jit(solution)/shard_map/ppermute | solution.py:226
  22.2 0.0 collective-permute-done.2
  22.2 8.7 %collective-permute-done.1 = bf16[256,256]{1,0:T(8,128)(2,1)S(1)} collective-permute-done((bf16[256,256]{1,0:T(8,128)(2,1)S(1)}, bf16[256,256]{1,0:T(8,128)(2,1)S(1)}, u32[]{:S(2)}, u32[]{:S(2)}) %collective-permute-start.1) | collective-permute-done | bytes 131104 | tf_op jit(solution)/shard_map/ppermute | solution.py:226
  30.9 1.6 %collective-permute-done = bf16[256,256]{1,0:T(8,128)(2,1)S(1)} collective-permute-done((bf16[256,256]{1,0:T(8,128)(2,1)S(1)}, bf16[256,256]{1,0:T(8,128)(2,1)S(1)}, u32[]{:S(2)}, u32[]{:S(2)}) %collective-permute-start) | collective-permute-done | bytes 131104 | tf_op jit(solution)/shard_map/ppermute | solution.py:226
  32.5 0.1 pad_maximum_fusion.after.near
  32.6 1.9 %collective-permute-start.4 = (bf16[4,256,256]{2,1,0:T(8,128)(2,1)S(1)}, bf16[4,256,256]{2,1,0:T(8,128)(2,1)}, u32[]{:S(2)}, u32[]{:S(2)}) collective-permute-start(bf16[4,256,256]{2,1,0:T(8,128)(2,1)S(1)} %pad_maximum_fusion.after.near), channel_id=1, source_target_pairs={{0,2},{2,0},{4,6},{6,4},{8,10},{10,8},{12,14},{14,12},{1,3},{3,1},... | collective-permute-start | bytes 1572872 | tf_op jit(solution)/shard_map/ppermute | solution.py:228
  34.5 5.3 %all-to-all-done.got = bf16[4,256,1280]{2,1,0:T(8,128)(2,1)S(1)} async-done(((bf16[4,256,1280]{2,1,0:T(8,128)(2,1)}), bf16[4,256,1280]{2,1,0:T(8,128)(2,1)S(1)}, u32[]{:S(2)}, u32[]{:S(2)}) %all-to-all-start) | async-done | bytes 2621472 | tf_op jit(solution)/shard_map/all_to_all | solution.py:214
  39.8 0.0 copy-start
  39.9 5.1 %collective-permute-start.3 = (bf16[4,256,256]{2,1,0:T(8,128)(2,1)S(1)}, bf16[4,256,256]{2,1,0:T(8,128)(2,1)S(1)}, u32[]{:S(2)}, u32[]{:S(2)}) collective-permute-start(bf16[4,256,256]{2,1,0:T(8,128)(2,1)S(1)} %pack.1.mine), channel_id=1, source_target_pairs={{0,1},{1,0},{2,3},{3,2},{4,5},{5,4},{6,7},{7,6},{8,9},{9,8},{10,11... | collective-permute-start | bytes 1572872 | tf_op jit(solution)/shard_map/ppermute | solution.py:239
  45.0 0.7 own_grad.1.own
  45.7 0.0 collective-permute-done.4.after.far
  45.7 0.0 copy-done
  45.7 0.8 collective-permute-done.3.other
  46.5 0.7 weight_grad.1
  47.2 0.0 copy-start.2
  47.2 1.0 copy-done.2
  48.2 6.8 %all-to-all-start.1 = ((bf16[8,512,128]{2,1,0:T(8,128)(2,1)}), bf16[8,512,128]{2,1,0:T(8,128)(2,1)S(1)}, u32[]{:S(2)}, u32[]{:S(2)}) async-start(bf16[8,512,128]{2,1,0:T(8,128)(2,1)} %copy-done.2), calls=%async_computation.1 | async-start | bytes 2097152 | tf_op jit(solution)/shard_map/all_to_all | solution.py:290
  55.0 1.0 copy-done.1
  56.1 1.1 to_other.1
  57.2 2.6 %collective-permute-start.5 = (bf16[2048,256]{1,0:T(8,128)(2,1)S(1)}, bf16[2048,256]{1,0:T(8,128)(2,1)S(1)}, u32[]{:S(2)}, u32[]{:S(2)}) collective-permute-start(bf16[2048,256]{1,0:T(8,128)(2,1)S(1)} %to_other.1), channel_id=1, source_target_pairs={{0,1},{1,0},{2,3},{3,2},{4,5},{5,4},{6,7},{7,6},{8,9},{9,8},{10,11... | collective-permute-start | bytes 3145736 | tf_op jit(solution)/shard_map/ppermute | solution.py:266
  59.8 2.3 %collective-permute-done.5.other = bf16[2048,256]{1,0:T(8,128)(2,1)S(1)} collective-permute-done((bf16[2048,256]{1,0:T(8,128)(2,1)S(1)}, bf16[2048,256]{1,0:T(8,128)(2,1)S(1)}, u32[]{:S(2)}, u32[]{:S(2)}) %collective-permute-start.5) | collective-permute-done | bytes 1048608 | tf_op jit(solution)/shard_map/ppermute | solution.py:266
  62.0 3.6 %input_grad.1 = (bf16[256,1024]{1,0:T(8,128)(2,1)}, bf16[256,1024]{1,0:T(8,128)(2,1)}, bf16[256,1024]{1,0:T(8,128)(2,1)}, bf16[256,1024]{1,0:T(8,128)(2,1)}, f32[8,128]{1,0:T(8,128)S(1)}) custom-call(bf16[4,256,256]{2,1,0:T(8,128)(2,1)S(1)} %copy-done.1, bf16[4,256,256]{2,1,0:T(8,128)(2,1)S(1)} %pad_maximum_fusion.after.near, ...), custom_call_target="tpu_custom_call" | custom-call | tf_op jit(solution)/shard_map/input_grad/pallas_call | solution.py:268
  65.6 3.4 %collective-permute-start.6 = (bf16[256,1024]{1,0:T(8,128)(2,1)}, bf16[256,1024]{1,0:T(8,128)(2,1)S(1)}, u32[]{:S(2)}, u32[]{:S(2)}) collective-permute-start(bf16[256,1024]{1,0:T(8,128)(2,1)} %get-tuple-element.14), channel_id=1, source_target_pairs={{0,0},{1,16},{16,1},{17,17},{32,32},{33,48},{48,33},{49,49},{2,2},... | collective-permute-start | bytes 1572872 | tf_op jit(solution)/shard_map/ppermute | solution.py:288
  69.0 1.9 %collective-permute-start.7 = (bf16[256,1024]{1,0:T(8,128)(2,1)}, bf16[256,1024]{1,0:T(8,128)(2,1)S(1)}, u32[]{:S(2)}, u32[]{:S(2)}) collective-permute-start(bf16[256,1024]{1,0:T(8,128)(2,1)} %get-tuple-element.15), channel_id=1, source_target_pairs={{0,16},{1,0},{16,17},{17,1},{32,48},{33,32},{48,49},{49,33},{2,18}... | collective-permute-start | bytes 1572872 | tf_op jit(solution)/shard_map/ppermute | solution.py:288
  70.9 3.0 %collective-permute-start.8 = (bf16[256,1024]{1,0:T(8,128)(2,1)}, bf16[256,1024]{1,0:T(8,128)(2,1)S(1)}, u32[]{:S(2)}, u32[]{:S(2)}) collective-permute-start(bf16[256,1024]{1,0:T(8,128)(2,1)} %get-tuple-element.16), channel_id=1, source_target_pairs={{0,32},{1,48},{16,33},{17,49},{32,0},{33,16},{48,1},{49,17},{2,34}... | collective-permute-start | bytes 1572872 | tf_op jit(solution)/shard_map/ppermute | solution.py:288
  74.0 4.5 %collective-permute-start.9 = (bf16[256,1024]{1,0:T(8,128)(2,1)}, bf16[256,1024]{1,0:T(8,128)(2,1)S(1)}, u32[]{:S(2)}, u32[]{:S(2)}) collective-permute-start(bf16[256,1024]{1,0:T(8,128)(2,1)} %get-tuple-element.17), channel_id=1, source_target_pairs={{0,48},{1,32},{16,49},{17,33},{32,16},{33,0},{48,17},{49,1},{2,50}... | collective-permute-start | bytes 1572872 | tf_op jit(solution)/shard_map/ppermute | solution.py:288
  78.5 5.7 %all-to-all-done.1.term = bf16[8,512,128]{2,1,0:T(8,128)(2,1)S(1)} async-done(((bf16[8,512,128]{2,1,0:T(8,128)(2,1)}), bf16[8,512,128]{2,1,0:T(8,128)(2,1)S(1)}, u32[]{:S(2)}, u32[]{:S(2)}) %all-to-all-start.1) | async-done | bytes 1048608 | tf_op jit(solution)/shard_map/all_to_all | solution.py:290
  84.3 0.8 sum_y.1
  85.1 14.9 %all-to-all-start.2 = ((bf16[12,2,24,128]{3,2,1,0:T(8,128)(2,1)}), bf16[12,2,24,128]{3,2,1,0:T(8,128)(2,1)S(1)}, u32[]{:S(2)}, u32[]{:S(2)}) async-start(bf16[12,2,24,128]{3,2,1,0:T(8,128)(2,1)} %sum_y.1), calls=%async_computation.2 | async-start | bytes 294912 | tf_op jit(solution)/shard_map/all_to_all | solution.py:299
  99.9 0.0 collective-permute-done.6.after0.r0
  100.0 0.0 collective-permute-done.7.after1.r1
  100.0 0.0 collective-permute-done.8.after2.r2
  100.0 0.0 collective-permute-done.9.after3.r3
  100.0 11.3 %all-to-all-done.2.term = bf16[12,2,24,128]{3,2,1,0:T(8,128)(2,1)S(1)} async-done(((bf16[12,2,24,128]{3,2,1,0:T(8,128)(2,1)}), bf16[12,2,24,128]{3,2,1,0:T(8,128)(2,1)S(1)}, u32[]{:S(2)}, u32[]{:S(2)}) %all-to-all-start.2) | async-done | bytes 147488 | tf_op jit(solution)/shard_map/all_to_all | solution.py:299
  111.3 0.7 sum_z.1
  112.0 3.6 %all-to-all-start.3 = ((bf16[12,2,24,128]{3,2,1,0:T(8,128)(2,1)}), bf16[12,2,24,128]{3,2,1,0:T(8,128)(2,1)S(1)}, u32[]{:S(2)}, u32[]{:S(2)}) async-start(bf16[12,2,24,128]{3,2,1,0:T(8,128)(2,1)} %sum_z.1), calls=%async_computation.3 | async-start | bytes 294912 | tf_op jit(solution)/shard_map/all_to_all | solution.py:322
  115.6 2.1 %placed.1 = (bf16[256,4096]{1,0:T(8,128)(2,1)}, f32[8,128]{1,0:T(8,128)S(1)}) custom-call(bf16[256,1024]{1,0:T(8,128)(2,1)S(1)} %collective-permute-done.6.after0.r0, bf16[256,1024]{1,0:T(8,128)(2,1)S(1)} %collective-permute-done.7.after1.r1, bf16[256,1024]{1,0:T(8,128)(2,1)S(1)} %collective-permute-done.8.after2.r2, ...), custom_call_target="tpu_custom_call" | custom-call | tf_op jit(solution)/shard_map/placed/pallas_call | solution.py:301
  117.7 8.6 %all-to-all-done.3.term = bf16[12,2,24,128]{3,2,1,0:T(8,128)(2,1)S(1)} async-done(((bf16[12,2,24,128]{3,2,1,0:T(8,128)(2,1)}), bf16[12,2,24,128]{3,2,1,0:T(8,128)(2,1)S(1)}, u32[]{:S(2)}, u32[]{:S(2)}) %all-to-all-start.3) | async-done | bytes 147488 | tf_op jit(solution)/shard_map/all_to_all | solution.py:322
  126.4 12.1 %all_to_all.25.term = bf16[4,12,24,128]{3,2,1,0:T(8,128)(2,1)S(1)} all-to-all(bf16[4,12,24,128]{3,2,1,0:T(8,128)(2,1)S(1)} %split.1), channel_id=1, replica_groups=mesh['z'=12,'xl'=2,'xh'=2,'y'=8,'t'=2] {'xl','t'}, dimensions={0} | all-to-all | bytes 589824 | tf_op jit(solution)/shard_map/all_to_all | solution.py:331
  138.5 0.9 turn.1
  (4 shorter events, 0.1 us)
Async XLA Ops:
  5.4 5.0 %copy-start.3 = (bf16[512,256]{1,0:T(8,128)(2,1)S(1)}, bf16[512,256]{1,0:T(8,128)(2,1)}, u32[]{:S(2)}) copy-start(bf16[512,256]{1,0:T(8,128)(2,1)} %weight.1) | copy-start | bytes 786436
  5.4 5.0 %copy-start.4 = (f32[8,128]{1,0:T(8,128)S(1)}, f32[8,128]{1,0:T(8,128)}, u32[]{:S(2)}) copy-start(f32[8,128]{1,0:T(8,128)} %get-tuple-element.12.after) | copy-start | bytes 12292
  5.4 34.4 %all-to-all-start = ((bf16[4,256,1280]{2,1,0:T(8,128)(2,1)}), bf16[4,256,1280]{2,1,0:T(8,128)(2,1)S(1)}, u32[]{:S(2)}, u32[]{:S(2)}) async-start(bf16[4,256,1280]{2,1,0:T(8,128)(2,1)} %get-tuple-element.11), calls=%async_computation | async-start | bytes 5242880 | tf_op jit(solution)/shard_map/all_to_all | solution.py:214
  10.4 11.8 %collective-permute-start.2 = (bf16[256,256]{1,0:T(8,128)(2,1)S(1)}, bf16[256,256]{1,0:T(8,128)(2,1)S(1)}, u32[]{:S(2)}, u32[]{:S(2)}) collective-permute-start(bf16[256,256]{1,0:T(8,128)(2,1)S(1)} %half_weight.1), channel_id=1, source_target_pairs={{0,8},{2,10},{4,12},{6,14},{8,0},{10,2},{12,4},{14,6},{1,9},{3,11}... | collective-permute-start | bytes 393224 | tf_op jit(solution)/shard_map/ppermute | solution.py:226
  17.9 13.0 %collective-permute-start.1 = (bf16[256,256]{1,0:T(8,128)(2,1)S(1)}, bf16[256,256]{1,0:T(8,128)(2,1)S(1)}, u32[]{:S(2)}, u32[]{:S(2)}) collective-permute-start(bf16[256,256]{1,0:T(8,128)(2,1)S(1)} %half_weight.1), channel_id=1, source_target_pairs={{0,4},{2,6},{4,0},{6,2},{8,12},{10,14},{12,8},{14,10},{1,5},{3,7},... | collective-permute-start | bytes 393224 | tf_op jit(solution)/shard_map/ppermute | solution.py:226
  20.3 12.2 %collective-permute-start = (bf16[256,256]{1,0:T(8,128)(2,1)S(1)}, bf16[256,256]{1,0:T(8,128)(2,1)S(1)}, u32[]{:S(2)}, u32[]{:S(2)}) collective-permute-start(bf16[256,256]{1,0:T(8,128)(2,1)S(1)} %half_weight.1), channel_id=1, source_target_pairs={{0,12},{2,14},{4,8},{6,10},{8,4},{10,6},{12,0},{14,2},{1,13},{3,15... | collective-permute-start | bytes 393224 | tf_op jit(solution)/shard_map/ppermute | solution.py:226
  32.6 13.1 %collective-permute-start.4 = (bf16[4,256,256]{2,1,0:T(8,128)(2,1)S(1)}, bf16[4,256,256]{2,1,0:T(8,128)(2,1)}, u32[]{:S(2)}, u32[]{:S(2)}) collective-permute-start(bf16[4,256,256]{2,1,0:T(8,128)(2,1)S(1)} %pad_maximum_fusion.after.near), channel_id=1, source_target_pairs={{0,2},{2,0},{4,6},{6,4},{8,10},{10,8},{12,14},{14,12},{1,3},{3,1},... | collective-permute-start | bytes 1572872 | tf_op jit(solution)/shard_map/ppermute | solution.py:228
  39.8 5.9 %copy-start = (bf16[4,256,256]{2,1,0:T(8,128)(2,1)}, bf16[4,256,256]{2,1,0:T(8,128)(2,1)S(1)}, u32[]{:S(2)}) copy-start(bf16[4,256,256]{2,1,0:T(8,128)(2,1)S(1)} %pack.1.mine) | copy-start | bytes 1572868
  39.9 6.6 %collective-permute-start.3 = (bf16[4,256,256]{2,1,0:T(8,128)(2,1)S(1)}, bf16[4,256,256]{2,1,0:T(8,128)(2,1)S(1)}, u32[]{:S(2)}, u32[]{:S(2)}) collective-permute-start(bf16[4,256,256]{2,1,0:T(8,128)(2,1)S(1)} %pack.1.mine), channel_id=1, source_target_pairs={{0,1},{1,0},{2,3},{3,2},{4,5},{5,4},{6,7},{7,6},{8,9},{9,8},{10,11... | collective-permute-start | bytes 1572872 | tf_op jit(solution)/shard_map/ppermute | solution.py:239
  47.2 1.0 copy-start.2
  48.2 36.1 %all-to-all-start.1 = ((bf16[8,512,128]{2,1,0:T(8,128)(2,1)}), bf16[8,512,128]{2,1,0:T(8,128)(2,1)S(1)}, u32[]{:S(2)}, u32[]{:S(2)}) async-start(bf16[8,512,128]{2,1,0:T(8,128)(2,1)} %copy-done.2), calls=%async_computation.1 | async-start | bytes 2097152 | tf_op jit(solution)/shard_map/all_to_all | solution.py:290
  55.0 1.0 copy-start.1
  57.2 4.8 %collective-permute-start.5 = (bf16[2048,256]{1,0:T(8,128)(2,1)S(1)}, bf16[2048,256]{1,0:T(8,128)(2,1)S(1)}, u32[]{:S(2)}, u32[]{:S(2)}) collective-permute-start(bf16[2048,256]{1,0:T(8,128)(2,1)S(1)} %to_other.1), channel_id=1, source_target_pairs={{0,1},{1,0},{2,3},{3,2},{4,5},{5,4},{6,7},{7,6},{8,9},{9,8},{10,11... | collective-permute-start | bytes 3145736 | tf_op jit(solution)/shard_map/ppermute | solution.py:266
  65.6 34.4 %collective-permute-start.6 = (bf16[256,1024]{1,0:T(8,128)(2,1)}, bf16[256,1024]{1,0:T(8,128)(2,1)S(1)}, u32[]{:S(2)}, u32[]{:S(2)}) collective-permute-start(bf16[256,1024]{1,0:T(8,128)(2,1)} %get-tuple-element.14), channel_id=1, source_target_pairs={{0,0},{1,16},{16,1},{17,17},{32,32},{33,48},{48,33},{49,49},{2,2},... | collective-permute-start | bytes 1572872 | tf_op jit(solution)/shard_map/ppermute | solution.py:288
  69.0 31.0 %collective-permute-start.7 = (bf16[256,1024]{1,0:T(8,128)(2,1)}, bf16[256,1024]{1,0:T(8,128)(2,1)S(1)}, u32[]{:S(2)}, u32[]{:S(2)}) collective-permute-start(bf16[256,1024]{1,0:T(8,128)(2,1)} %get-tuple-element.15), channel_id=1, source_target_pairs={{0,16},{1,0},{16,17},{17,1},{32,48},{33,32},{48,49},{49,33},{2,18}... | collective-permute-start | bytes 1572872 | tf_op jit(solution)/shard_map/ppermute | solution.py:288
  70.9 29.0 %collective-permute-start.8 = (bf16[256,1024]{1,0:T(8,128)(2,1)}, bf16[256,1024]{1,0:T(8,128)(2,1)S(1)}, u32[]{:S(2)}, u32[]{:S(2)}) collective-permute-start(bf16[256,1024]{1,0:T(8,128)(2,1)} %get-tuple-element.16), channel_id=1, source_target_pairs={{0,32},{1,48},{16,33},{17,49},{32,0},{33,16},{48,1},{49,17},{2,34}... | collective-permute-start | bytes 1572872 | tf_op jit(solution)/shard_map/ppermute | solution.py:288
  74.0 26.0 %collective-permute-start.9 = (bf16[256,1024]{1,0:T(8,128)(2,1)}, bf16[256,1024]{1,0:T(8,128)(2,1)S(1)}, u32[]{:S(2)}, u32[]{:S(2)}) collective-permute-start(bf16[256,1024]{1,0:T(8,128)(2,1)} %get-tuple-element.17), channel_id=1, source_target_pairs={{0,48},{1,32},{16,49},{17,33},{32,16},{33,0},{48,17},{49,1},{2,50}... | collective-permute-start | bytes 1572872 | tf_op jit(solution)/shard_map/ppermute | solution.py:288
  85.1 26.2 %all-to-all-start.2 = ((bf16[12,2,24,128]{3,2,1,0:T(8,128)(2,1)}), bf16[12,2,24,128]{3,2,1,0:T(8,128)(2,1)S(1)}, u32[]{:S(2)}, u32[]{:S(2)}) async-start(bf16[12,2,24,128]{3,2,1,0:T(8,128)(2,1)} %sum_y.1), calls=%async_computation.2 | async-start | bytes 294912 | tf_op jit(solution)/shard_map/all_to_all | solution.py:299
  112.0 14.4 %all-to-all-start.3 = ((bf16[12,2,24,128]{3,2,1,0:T(8,128)(2,1)}), bf16[12,2,24,128]{3,2,1,0:T(8,128)(2,1)S(1)}, u32[]{:S(2)}, u32[]{:S(2)}) async-start(bf16[12,2,24,128]{3,2,1,0:T(8,128)(2,1)} %sum_z.1), calls=%async_computation.3 | async-start | bytes 294912 | tf_op jit(solution)/shard_map/all_to_all | solution.py:322

commit v5 on v4

--- a/solution.py
+++ b/solution.py
@@ -16,6 +16,8 @@
 TOKEN = jax.ShapeDtypeStruct((8, 128), jnp.float32)
 FEAT = NY * QUART
 KV = NT * COLS
+LAST_FIRST = [list(range(NY - 1, -1, -1))]
+ALONG_Z = [[(7 - p) % NZ for p in range(NZ)]]
 ZCOLS = 24
 BF16, F32 = jnp.bfloat16, jnp.float32
 
@@ -90,8 +92,9 @@
     rest = pl.ds(pl.multiple_of((1 - t) * COLS, COLS), COLS)
     g = product(other[...], got)
     for y in range(NY):
-        out[y, mine, :] = own[y]
-        out[y, rest, :] = g[:, y * QUART : (y + 1) * QUART]
+        place = NY - 1 - y
+        out[place, mine, :] = own[y]
+        out[place, rest, :] = g[:, y * QUART : (y + 1) * QUART]
 
 
 def other_kernel(mine, near, far, out):
@@ -287,7 +290,7 @@
         ]
         returned.append(lax.ppermute(products[r], ("xl", "xh", "t"), pairs))
 
-    term = lax.all_to_all(term, "y", 0, 0, tiled=True)
+    term = lax.all_to_all(term, "y", 0, 0, axis_index_groups=LAST_FIRST, tiled=True)
     term = pl.pallas_call(
         sum_y_kernel,
         in_specs=whole(1) + [pl.BlockSpec(memory_space=pl.ANY)],
@@ -296,7 +299,7 @@
         compiler_params=PARAMS,
         name="sum_y",
     )(term, multiplied)
-    term = lax.all_to_all(term, "z", 0, 0, tiled=True)
+    term = lax.all_to_all(term, "z", 0, 0, axis_index_groups=ALONG_Z, tiled=True)
     rows = 64
     normed_grad, placed = pl.pallas_call(
         place_kernel,
@@ -319,7 +322,7 @@
         compiler_params=PARAMS,
         name="sum_z",
     )(term, *returned)
-    term = lax.all_to_all(term, "z", 0, 0, tiled=True)
+    term = lax.all_to_all(term, "z", 0, 0, axis_index_groups=ALONG_Z, tiled=True)
     term = pl.pallas_call(
         split_kernel,
         in_specs=whole(1) + UNUSED,

time: 140 us -> 133 us (0.950); the launches traced: 139 us -> 131 us
  waiting for transfers between devices: 44.2 us -> 26.8 us
  starting transfers between devices: 64.6 us -> 75.2 us
  blocking collectives: 12.1 us -> 10.2 us
    all_to_all x3, waiting for transfers between devices: 25.7 us -> 8.2 us  [the longest x2 8.2 us: per_device(): lax.all_to_all(term, 'z', 0, 0, axis_index_groups=ALONG_Z, tiled=True)]
    all_to_all x3, starting transfers between devices: 25.3 us -> 35.6 us  [the longest x2 28.5 us: per_device(): lax.all_to_all(term, 'z', 0, 0, axis_index_groups=ALONG_Z, tiled=True)]
    all_to_all x1, blocking collectives: 12.1 us -> 10.2 us  [per_device(): term = lax.all_to_all(term, ('xl', 't'), 0, 0, tiled=True)]
  transfers between devices with their start and end apart: 14 -> 14, of which waited for: 8 -> 7; matrix products, arithmetic and copies ran while one was open for 0% -> 0% of each run, Pallas kernels for 6% -> 6%
where the time goes in v5:
time: 133 us; the launch traced here: 131 us
  starting transfers between devices  75.2 us (57%)
  waiting for transfers between devices  26.8 us (20%)
  Pallas kernels  15.5 us (12%)
  blocking collectives  10.2 us (8%)
  local copies, waits for them, and re-layouts  2.02 us (2%)
    all_to_all x2, starting transfers between devices, per_device(): lax.all_to_all(term, 'z', 0, 0, axis_index_groups=ALONG_Z, tiled=True)  28.5 us
    ppermute x4, starting transfers between devices, per_device(): returned.append(lax.ppermute(products[r], ('xl', 'xh', 't'), pairs))  12.9 us
    ppermute x3, starting transfers between devices, per_device(): lax.ppermute(half_weight, 'y', [(i, i ^ e) for i in range(NY)])  11.8 us
    ppermute x3, waiting for transfers between devices, per_device(): lax.ppermute(half_weight, 'y', [(i, i ^ e) for i in range(NY)])  10.3 us
    all_to_all x1, blocking collectives, per_device(): term = lax.all_to_all(term, ('xl', 't'), 0, 0, tiled=True)  10.2 us
    all_to_all x2, waiting for transfers between devices, per_device(): lax.all_to_all(term, 'z', 0, 0, axis_index_groups=ALONG_Z, tiled=True)  8.2 us
    all_to_all x1, starting transfers between devices, per_device(): lax.all_to_all(term, 'y', 0, 0, axis_index_groups=LAST_FIRST, tiled=True)  7.1 us
    all_to_all x1, waiting for transfers between devices, per_device(): got = lax.all_to_all(blocks, ('xl', 'xh'), 0, 0, tiled=True)  5.3 us
  transfers between devices with their start and end apart: 14, of which 7 were waited for; matrix products, arithmetic and copies ran while one was open for 0% of the time, Pallas kernels for 6%

profile of v5, /device:TPU:1, one launch (start us, length us, event | category | flops | bytes accessed | tf_op | source)
XLA Modules:
  0.0 130.6 jit_solution(1796651341179629636)
XLA Ops:
  0.6 4.8 %prep.1 = (bf16[4,256,1280]{2,1,0:T(8,128)(2,1)}, f32[8,128]{1,0:T(8,128)}) custom-call(s32[1,4]{1,0:T(1,128)} %doc.1, bf16[256,8192]{1,0:T(8,128)(2,1)} %act.1, f32[1,8192]{1,0:T(1,128)} %bitcast.9, bf16[256,256]{1,0:T(8,128)(2,1)} %key_grad.1), custom_call_target="tpu_custom_call" | custom-call | tf_op jit(solution)/shard_map/prep/pallas_call | solution.py:199
  5.4 0.0 copy-start.3
  5.4 0.0 copy-start.4
  5.4 5.0 %all-to-all-start = ((bf16[4,256,1280]{2,1,0:T(8,128)(2,1)}), bf16[4,256,1280]{2,1,0:T(8,128)(2,1)S(1)}, u32[]{:S(2)}, u32[]{:S(2)}) async-start(bf16[4,256,1280]{2,1,0:T(8,128)(2,1)} %get-tuple-element.11), calls=%async_computation | async-start | bytes 5242880 | tf_op jit(solution)/shard_map/all_to_all | solution.py:217
  10.4 0.0 copy-done.3
  10.4 0.0 copy-done.4
  10.4 7.5 %collective-permute-start.2 = (bf16[256,256]{1,0:T(8,128)(2,1)S(1)}, bf16[256,256]{1,0:T(8,128)(2,1)S(1)}, u32[]{:S(2)}, u32[]{:S(2)}) collective-permute-start(bf16[256,256]{1,0:T(8,128)(2,1)S(1)} %half_weight.1), channel_id=1, source_target_pairs={{0,8},{2,10},{4,12},{6,14},{8,0},{10,2},{12,4},{14,6},{1,9},{3,11}... | collective-permute-start | bytes 393224 | tf_op jit(solution)/shard_map/ppermute | solution.py:229
  17.9 2.4 %collective-permute-start.1 = (bf16[256,256]{1,0:T(8,128)(2,1)S(1)}, bf16[256,256]{1,0:T(8,128)(2,1)S(1)}, u32[]{:S(2)}, u32[]{:S(2)}) collective-permute-start(bf16[256,256]{1,0:T(8,128)(2,1)S(1)} %half_weight.1), channel_id=1, source_target_pairs={{0,4},{2,6},{4,0},{6,2},{8,12},{10,14},{12,8},{14,10},{1,5},{3,7},... | collective-permute-start | bytes 393224 | tf_op jit(solution)/shard_map/ppermute | solution.py:229
  20.3 1.9 %collective-permute-start = (bf16[256,256]{1,0:T(8,128)(2,1)S(1)}, bf16[256,256]{1,0:T(8,128)(2,1)S(1)}, u32[]{:S(2)}, u32[]{:S(2)}) collective-permute-start(bf16[256,256]{1,0:T(8,128)(2,1)S(1)} %half_weight.1), channel_id=1, source_target_pairs={{0,12},{2,14},{4,8},{6,10},{8,4},{10,6},{12,0},{14,2},{1,13},{3,15... | collective-permute-start | bytes 393224 | tf_op jit(solution)/shard_map/ppermute | solution.py:229
  22.2 0.0 collective-permute-done.2
  22.2 8.7 %collective-permute-done.1 = bf16[256,256]{1,0:T(8,128)(2,1)S(1)} collective-permute-done((bf16[256,256]{1,0:T(8,128)(2,1)S(1)}, bf16[256,256]{1,0:T(8,128)(2,1)S(1)}, u32[]{:S(2)}, u32[]{:S(2)}) %collective-permute-start.1) | collective-permute-done | bytes 131104 | tf_op jit(solution)/shard_map/ppermute | solution.py:229
  30.9 1.6 %collective-permute-done = bf16[256,256]{1,0:T(8,128)(2,1)S(1)} collective-permute-done((bf16[256,256]{1,0:T(8,128)(2,1)S(1)}, bf16[256,256]{1,0:T(8,128)(2,1)S(1)}, u32[]{:S(2)}, u32[]{:S(2)}) %collective-permute-start) | collective-permute-done | bytes 131104 | tf_op jit(solution)/shard_map/ppermute | solution.py:229
  32.5 0.1 pad_maximum_fusion.after.near
  32.6 1.9 %collective-permute-start.4 = (bf16[4,256,256]{2,1,0:T(8,128)(2,1)S(1)}, bf16[4,256,256]{2,1,0:T(8,128)(2,1)}, u32[]{:S(2)}, u32[]{:S(2)}) collective-permute-start(bf16[4,256,256]{2,1,0:T(8,128)(2,1)S(1)} %pad_maximum_fusion.after.near), channel_id=1, source_target_pairs={{0,2},{2,0},{4,6},{6,4},{8,10},{10,8},{12,14},{14,12},{1,3},{3,1},... | collective-permute-start | bytes 1572872 | tf_op jit(solution)/shard_map/ppermute | solution.py:231
  34.5 5.3 %all-to-all-done.got = bf16[4,256,1280]{2,1,0:T(8,128)(2,1)S(1)} async-done(((bf16[4,256,1280]{2,1,0:T(8,128)(2,1)}), bf16[4,256,1280]{2,1,0:T(8,128)(2,1)S(1)}, u32[]{:S(2)}, u32[]{:S(2)}) %all-to-all-start) | async-done | bytes 2621472 | tf_op jit(solution)/shard_map/all_to_all | solution.py:217
  39.8 0.0 copy-start
  39.9 5.1 %collective-permute-start.3 = (bf16[4,256,256]{2,1,0:T(8,128)(2,1)S(1)}, bf16[4,256,256]{2,1,0:T(8,128)(2,1)S(1)}, u32[]{:S(2)}, u32[]{:S(2)}) collective-permute-start(bf16[4,256,256]{2,1,0:T(8,128)(2,1)S(1)} %pack.1.mine), channel_id=1, source_target_pairs={{0,1},{1,0},{2,3},{3,2},{4,5},{5,4},{6,7},{7,6},{8,9},{9,8},{10,11... | collective-permute-start | bytes 1572872 | tf_op jit(solution)/shard_map/ppermute | solution.py:242
  45.0 0.7 own_grad.1.own
  45.7 0.0 collective-permute-done.4.after.far
  45.7 0.0 copy-done
  45.7 0.8 collective-permute-done.3.other
  46.5 0.7 weight_grad.1
  47.2 0.0 copy-start.2
  47.2 1.0 copy-done.2
  48.2 7.1 %all-to-all-start.1 = ((bf16[8,512,128]{2,1,0:T(8,128)(2,1)}), bf16[8,512,128]{2,1,0:T(8,128)(2,1)S(1)}, u32[]{:S(2)}, u32[]{:S(2)}) async-start(bf16[8,512,128]{2,1,0:T(8,128)(2,1)} %copy-done.2), calls=%async_computation.1 | async-start | bytes 2097152 | tf_op jit(solution)/shard_map/all_to_all | solution.py:293
  55.3 1.0 copy-done.1
  56.3 1.1 to_other.1
  57.5 2.8 %collective-permute-start.5 = (bf16[2048,256]{1,0:T(8,128)(2,1)S(1)}, bf16[2048,256]{1,0:T(8,128)(2,1)S(1)}, u32[]{:S(2)}, u32[]{:S(2)}) collective-permute-start(bf16[2048,256]{1,0:T(8,128)(2,1)S(1)} %to_other.1), channel_id=1, source_target_pairs={{0,1},{1,0},{2,3},{3,2},{4,5},{5,4},{6,7},{7,6},{8,9},{9,8},{10,11... | collective-permute-start | bytes 3145736 | tf_op jit(solution)/shard_map/ppermute | solution.py:269
  60.3 2.3 %collective-permute-done.5.other = bf16[2048,256]{1,0:T(8,128)(2,1)S(1)} collective-permute-done((bf16[2048,256]{1,0:T(8,128)(2,1)S(1)}, bf16[2048,256]{1,0:T(8,128)(2,1)S(1)}, u32[]{:S(2)}, u32[]{:S(2)}) %collective-permute-start.5) | collective-permute-done | bytes 1048608 | tf_op jit(solution)/shard_map/ppermute | solution.py:269
  62.6 3.6 %input_grad.1 = (bf16[256,1024]{1,0:T(8,128)(2,1)}, bf16[256,1024]{1,0:T(8,128)(2,1)}, bf16[256,1024]{1,0:T(8,128)(2,1)}, bf16[256,1024]{1,0:T(8,128)(2,1)}, f32[8,128]{1,0:T(8,128)S(1)}) custom-call(bf16[4,256,256]{2,1,0:T(8,128)(2,1)S(1)} %copy-done.1, bf16[4,256,256]{2,1,0:T(8,128)(2,1)S(1)} %pad_maximum_fusion.after.near, ...), custom_call_target="tpu_custom_call" | custom-call | tf_op jit(solution)/shard_map/input_grad/pallas_call | solution.py:271
  66.1 4.7 %collective-permute-start.6 = (bf16[256,1024]{1,0:T(8,128)(2,1)}, bf16[256,1024]{1,0:T(8,128)(2,1)S(1)}, u32[]{:S(2)}, u32[]{:S(2)}) collective-permute-start(bf16[256,1024]{1,0:T(8,128)(2,1)} %get-tuple-element.14), channel_id=1, source_target_pairs={{0,0},{1,16},{16,1},{17,17},{32,32},{33,48},{48,33},{49,49},{2,2},... | collective-permute-start | bytes 1572872 | tf_op jit(solution)/shard_map/ppermute | solution.py:291
  70.9 1.9 %collective-permute-start.7 = (bf16[256,1024]{1,0:T(8,128)(2,1)}, bf16[256,1024]{1,0:T(8,128)(2,1)S(1)}, u32[]{:S(2)}, u32[]{:S(2)}) collective-permute-start(bf16[256,1024]{1,0:T(8,128)(2,1)} %get-tuple-element.15), channel_id=1, source_target_pairs={{0,16},{1,0},{16,17},{17,1},{32,48},{33,32},{48,49},{49,33},{2,18}... | collective-permute-start | bytes 1572872 | tf_op jit(solution)/shard_map/ppermute | solution.py:291
  72.8 2.8 %collective-permute-start.8 = (bf16[256,1024]{1,0:T(8,128)(2,1)}, bf16[256,1024]{1,0:T(8,128)(2,1)S(1)}, u32[]{:S(2)}, u32[]{:S(2)}) collective-permute-start(bf16[256,1024]{1,0:T(8,128)(2,1)} %get-tuple-element.16), channel_id=1, source_target_pairs={{0,32},{1,48},{16,33},{17,49},{32,0},{33,16},{48,1},{49,17},{2,34}... | collective-permute-start | bytes 1572872 | tf_op jit(solution)/shard_map/ppermute | solution.py:291
  75.6 3.4 %collective-permute-start.9 = (bf16[256,1024]{1,0:T(8,128)(2,1)}, bf16[256,1024]{1,0:T(8,128)(2,1)S(1)}, u32[]{:S(2)}, u32[]{:S(2)}) collective-permute-start(bf16[256,1024]{1,0:T(8,128)(2,1)} %get-tuple-element.17), channel_id=1, source_target_pairs={{0,48},{1,32},{16,49},{17,33},{32,16},{33,0},{48,17},{49,1},{2,50}... | collective-permute-start | bytes 1572872 | tf_op jit(solution)/shard_map/ppermute | solution.py:291
  79.1 0.0 all-to-all-done.1.term
  79.1 0.8 sum_y.1
  79.9 18.8 %all-to-all-start.2 = ((bf16[12,2,24,128]{3,2,1,0:T(8,128)(2,1)}), bf16[12,2,24,128]{3,2,1,0:T(8,128)(2,1)S(1)}, u32[]{:S(2)}, u32[]{:S(2)}) async-start(bf16[12,2,24,128]{3,2,1,0:T(8,128)(2,1)} %sum_y.1), calls=%async_computation.2 | async-start | bytes 294912 | tf_op jit(solution)/shard_map/all_to_all | solution.py:302
  98.6 0.0 collective-permute-done.6.after0.r0
  98.7 0.0 collective-permute-done.7.after1.r1
  98.7 0.0 collective-permute-done.8.after2.r2
  98.7 0.0 collective-permute-done.9.after3.r3
  98.7 5.6 %all-to-all-done.2.term = bf16[12,2,24,128]{3,2,1,0:T(8,128)(2,1)S(1)} async-done(((bf16[12,2,24,128]{3,2,1,0:T(8,128)(2,1)}), bf16[12,2,24,128]{3,2,1,0:T(8,128)(2,1)S(1)}, u32[]{:S(2)}, u32[]{:S(2)}) %all-to-all-start.2) | async-done | bytes 147488 | tf_op jit(solution)/shard_map/all_to_all | solution.py:302
  104.2 0.7 sum_z.1
  104.9 9.7 %all-to-all-start.3 = ((bf16[12,2,24,128]{3,2,1,0:T(8,128)(2,1)}), bf16[12,2,24,128]{3,2,1,0:T(8,128)(2,1)S(1)}, u32[]{:S(2)}, u32[]{:S(2)}) async-start(bf16[12,2,24,128]{3,2,1,0:T(8,128)(2,1)} %sum_z.1), calls=%async_computation.3 | async-start | bytes 294912 | tf_op jit(solution)/shard_map/all_to_all | solution.py:325
  114.7 2.1 %placed.1 = (bf16[256,4096]{1,0:T(8,128)(2,1)}, f32[8,128]{1,0:T(8,128)S(1)}) custom-call(bf16[256,1024]{1,0:T(8,128)(2,1)S(1)} %collective-permute-done.6.after0.r0, bf16[256,1024]{1,0:T(8,128)(2,1)S(1)} %collective-permute-done.7.after1.r1, bf16[256,1024]{1,0:T(8,128)(2,1)S(1)} %collective-permute-done.8.after2.r2, ...), custom_call_target="tpu_custom_call" | custom-call | tf_op jit(solution)/shard_map/placed/pallas_call | solution.py:304
  116.7 2.7 %all-to-all-done.3.term = bf16[12,2,24,128]{3,2,1,0:T(8,128)(2,1)S(1)} async-done(((bf16[12,2,24,128]{3,2,1,0:T(8,128)(2,1)}), bf16[12,2,24,128]{3,2,1,0:T(8,128)(2,1)S(1)}, u32[]{:S(2)}, u32[]{:S(2)}) %all-to-all-start.3) | async-done | bytes 147488 | tf_op jit(solution)/shard_map/all_to_all | solution.py:325
  119.4 10.2 %all_to_all.25.term = bf16[4,12,24,128]{3,2,1,0:T(8,128)(2,1)S(1)} all-to-all(bf16[4,12,24,128]{3,2,1,0:T(8,128)(2,1)S(1)} %split.1), channel_id=1, replica_groups=mesh['z'=12,'xl'=2,'xh'=2,'y'=8,'t'=2] {'xl','t'}, dimensions={0} | all-to-all | bytes 589824 | tf_op jit(solution)/shard_map/all_to_all | solution.py:334
  129.6 0.9 turn.1
  (4 shorter events, 0.1 us)
Async XLA Ops:
  5.4 5.0 %copy-start.3 = (bf16[512,256]{1,0:T(8,128)(2,1)S(1)}, bf16[512,256]{1,0:T(8,128)(2,1)}, u32[]{:S(2)}) copy-start(bf16[512,256]{1,0:T(8,128)(2,1)} %weight.1) | copy-start | bytes 786436
  5.4 5.0 %copy-start.4 = (f32[8,128]{1,0:T(8,128)S(1)}, f32[8,128]{1,0:T(8,128)}, u32[]{:S(2)}) copy-start(f32[8,128]{1,0:T(8,128)} %get-tuple-element.12.after) | copy-start | bytes 12292
  5.4 34.4 %all-to-all-start = ((bf16[4,256,1280]{2,1,0:T(8,128)(2,1)}), bf16[4,256,1280]{2,1,0:T(8,128)(2,1)S(1)}, u32[]{:S(2)}, u32[]{:S(2)}) async-start(bf16[4,256,1280]{2,1,0:T(8,128)(2,1)} %get-tuple-element.11), calls=%async_computation | async-start | bytes 5242880 | tf_op jit(solution)/shard_map/all_to_all | solution.py:217
  10.4 11.8 %collective-permute-start.2 = (bf16[256,256]{1,0:T(8,128)(2,1)S(1)}, bf16[256,256]{1,0:T(8,128)(2,1)S(1)}, u32[]{:S(2)}, u32[]{:S(2)}) collective-permute-start(bf16[256,256]{1,0:T(8,128)(2,1)S(1)} %half_weight.1), channel_id=1, source_target_pairs={{0,8},{2,10},{4,12},{6,14},{8,0},{10,2},{12,4},{14,6},{1,9},{3,11}... | collective-permute-start | bytes 393224 | tf_op jit(solution)/shard_map/ppermute | solution.py:229
  17.9 13.0 %collective-permute-start.1 = (bf16[256,256]{1,0:T(8,128)(2,1)S(1)}, bf16[256,256]{1,0:T(8,128)(2,1)S(1)}, u32[]{:S(2)}, u32[]{:S(2)}) collective-permute-start(bf16[256,256]{1,0:T(8,128)(2,1)S(1)} %half_weight.1), channel_id=1, source_target_pairs={{0,4},{2,6},{4,0},{6,2},{8,12},{10,14},{12,8},{14,10},{1,5},{3,7},... | collective-permute-start | bytes 393224 | tf_op jit(solution)/shard_map/ppermute | solution.py:229
  20.3 12.2 %collective-permute-start = (bf16[256,256]{1,0:T(8,128)(2,1)S(1)}, bf16[256,256]{1,0:T(8,128)(2,1)S(1)}, u32[]{:S(2)}, u32[]{:S(2)}) collective-permute-start(bf16[256,256]{1,0:T(8,128)(2,1)S(1)} %half_weight.1), channel_id=1, source_target_pairs={{0,12},{2,14},{4,8},{6,10},{8,4},{10,6},{12,0},{14,2},{1,13},{3,15... | collective-permute-start | bytes 393224 | tf_op jit(solution)/shard_map/ppermute | solution.py:229
  32.6 13.1 %collective-permute-start.4 = (bf16[4,256,256]{2,1,0:T(8,128)(2,1)S(1)}, bf16[4,256,256]{2,1,0:T(8,128)(2,1)}, u32[]{:S(2)}, u32[]{:S(2)}) collective-permute-start(bf16[4,256,256]{2,1,0:T(8,128)(2,1)S(1)} %pad_maximum_fusion.after.near), channel_id=1, source_target_pairs={{0,2},{2,0},{4,6},{6,4},{8,10},{10,8},{12,14},{14,12},{1,3},{3,1},... | collective-permute-start | bytes 1572872 | tf_op jit(solution)/shard_map/ppermute | solution.py:231
  39.8 5.9 %copy-start = (bf16[4,256,256]{2,1,0:T(8,128)(2,1)}, bf16[4,256,256]{2,1,0:T(8,128)(2,1)S(1)}, u32[]{:S(2)}) copy-start(bf16[4,256,256]{2,1,0:T(8,128)(2,1)S(1)} %pack.1.mine) | copy-start | bytes 1572868
  39.9 6.6 %collective-permute-start.3 = (bf16[4,256,256]{2,1,0:T(8,128)(2,1)S(1)}, bf16[4,256,256]{2,1,0:T(8,128)(2,1)S(1)}, u32[]{:S(2)}, u32[]{:S(2)}) collective-permute-start(bf16[4,256,256]{2,1,0:T(8,128)(2,1)S(1)} %pack.1.mine), channel_id=1, source_target_pairs={{0,1},{1,0},{2,3},{3,2},{4,5},{5,4},{6,7},{7,6},{8,9},{9,8},{10,11... | collective-permute-start | bytes 1572872 | tf_op jit(solution)/shard_map/ppermute | solution.py:242
  47.2 1.0 copy-start.2
  48.2 30.9 %all-to-all-start.1 = ((bf16[8,512,128]{2,1,0:T(8,128)(2,1)}), bf16[8,512,128]{2,1,0:T(8,128)(2,1)S(1)}, u32[]{:S(2)}, u32[]{:S(2)}) async-start(bf16[8,512,128]{2,1,0:T(8,128)(2,1)} %copy-done.2), calls=%async_computation.1 | async-start | bytes 2097152 | tf_op jit(solution)/shard_map/all_to_all | solution.py:293
  55.3 1.0 copy-start.1
  57.5 5.1 %collective-permute-start.5 = (bf16[2048,256]{1,0:T(8,128)(2,1)S(1)}, bf16[2048,256]{1,0:T(8,128)(2,1)S(1)}, u32[]{:S(2)}, u32[]{:S(2)}) collective-permute-start(bf16[2048,256]{1,0:T(8,128)(2,1)S(1)} %to_other.1), channel_id=1, source_target_pairs={{0,1},{1,0},{2,3},{3,2},{4,5},{5,4},{6,7},{7,6},{8,9},{9,8},{10,11... | collective-permute-start | bytes 3145736 | tf_op jit(solution)/shard_map/ppermute | solution.py:269
  66.1 32.5 %collective-permute-start.6 = (bf16[256,1024]{1,0:T(8,128)(2,1)}, bf16[256,1024]{1,0:T(8,128)(2,1)S(1)}, u32[]{:S(2)}, u32[]{:S(2)}) collective-permute-start(bf16[256,1024]{1,0:T(8,128)(2,1)} %get-tuple-element.14), channel_id=1, source_target_pairs={{0,0},{1,16},{16,1},{17,17},{32,32},{33,48},{48,33},{49,49},{2,2},... | collective-permute-start | bytes 1572872 | tf_op jit(solution)/shard_map/ppermute | solution.py:291
  70.9 27.8 %collective-permute-start.7 = (bf16[256,1024]{1,0:T(8,128)(2,1)}, bf16[256,1024]{1,0:T(8,128)(2,1)S(1)}, u32[]{:S(2)}, u32[]{:S(2)}) collective-permute-start(bf16[256,1024]{1,0:T(8,128)(2,1)} %get-tuple-element.15), channel_id=1, source_target_pairs={{0,16},{1,0},{16,17},{17,1},{32,48},{33,32},{48,49},{49,33},{2,18}... | collective-permute-start | bytes 1572872 | tf_op jit(solution)/shard_map/ppermute | solution.py:291
  72.8 25.9 %collective-permute-start.8 = (bf16[256,1024]{1,0:T(8,128)(2,1)}, bf16[256,1024]{1,0:T(8,128)(2,1)S(1)}, u32[]{:S(2)}, u32[]{:S(2)}) collective-permute-start(bf16[256,1024]{1,0:T(8,128)(2,1)} %get-tuple-element.16), channel_id=1, source_target_pairs={{0,32},{1,48},{16,33},{17,49},{32,0},{33,16},{48,1},{49,17},{2,34}... | collective-permute-start | bytes 1572872 | tf_op jit(solution)/shard_map/ppermute | solution.py:291
  75.6 23.1 %collective-permute-start.9 = (bf16[256,1024]{1,0:T(8,128)(2,1)}, bf16[256,1024]{1,0:T(8,128)(2,1)S(1)}, u32[]{:S(2)}, u32[]{:S(2)}) collective-permute-start(bf16[256,1024]{1,0:T(8,128)(2,1)} %get-tuple-element.17), channel_id=1, source_target_pairs={{0,48},{1,32},{16,49},{17,33},{32,16},{33,0},{48,17},{49,1},{2,50}... | collective-permute-start | bytes 1572872 | tf_op jit(solution)/shard_map/ppermute | solution.py:291
  79.9 24.3 %all-to-all-start.2 = ((bf16[12,2,24,128]{3,2,1,0:T(8,128)(2,1)}), bf16[12,2,24,128]{3,2,1,0:T(8,128)(2,1)S(1)}, u32[]{:S(2)}, u32[]{:S(2)}) async-start(bf16[12,2,24,128]{3,2,1,0:T(8,128)(2,1)} %sum_y.1), calls=%async_computation.2 | async-start | bytes 294912 | tf_op jit(solution)/shard_map/all_to_all | solution.py:302
  104.9 14.5 %all-to-all-start.3 = ((bf16[12,2,24,128]{3,2,1,0:T(8,128)(2,1)}), bf16[12,2,24,128]{3,2,1,0:T(8,128)(2,1)S(1)}, u32[]{:S(2)}, u32[]{:S(2)}) async-start(bf16[12,2,24,128]{3,2,1,0:T(8,128)(2,1)} %sum_z.1), calls=%async_computation.3 | async-start | bytes 294912 | tf_op jit(solution)/shard_map/all_to_all | solution.py:325

commit v6 on v5

--- a/solution.py
+++ b/solution.py
@@ -16,7 +16,7 @@
 TOKEN = jax.ShapeDtypeStruct((8, 128), jnp.float32)
 FEAT = NY * QUART
 KV = NT * COLS
-LAST_FIRST = [list(range(NY - 1, -1, -1))]
+ALONG_Y = [[3, 2, 1, 7, 6, 0, 5, 4]]
 ALONG_Z = [[(7 - p) % NZ for p in range(NZ)]]
 ZCOLS = 24
 BF16, F32 = jnp.bfloat16, jnp.float32
@@ -92,7 +92,7 @@
     rest = pl.ds(pl.multiple_of((1 - t) * COLS, COLS), COLS)
     g = product(other[...], got)
     for y in range(NY):
-        place = NY - 1 - y
+        place = ALONG_Y[0].index(y)
         out[place, mine, :] = own[y]
         out[place, rest, :] = g[:, y * QUART : (y + 1) * QUART]
 
@@ -290,7 +290,7 @@
         ]
         returned.append(lax.ppermute(products[r], ("xl", "xh", "t"), pairs))
 
-    term = lax.all_to_all(term, "y", 0, 0, axis_index_groups=LAST_FIRST, tiled=True)
+    term = lax.all_to_all(term, "y", 0, 0, axis_index_groups=ALONG_Y, tiled=True)
     term = pl.pallas_call(
         sum_y_kernel,
         in_specs=whole(1) + [pl.BlockSpec(memory_space=pl.ANY)],

time: 133 us -> 134 us (level); the launches traced: 131 us -> 134 us
  waiting for transfers between devices: 26.8 us -> 29.1 us
    all_to_all x1, waiting for transfers between devices: 0.01 us -> 2.45 us  [per_device(): lax.all_to_all(term, 'y', 0, 0, axis_index_groups=ALONG_Y, tiled=True)]
  transfers between devices with their start and end apart: 14 -> 14, of which waited for: 7 -> 8; matrix products, arithmetic and copies ran while one was open for 0% -> 0% of each run, Pallas kernels for 6% -> 6%
where the time goes in v6:
time: 134 us
  starting transfers between devices  75.3 us (56%)
  waiting for transfers between devices  29.1 us (22%)
  Pallas kernels  15.5 us (12%)
  blocking collectives  10.7 us (8%)
  local copies, waits for them, and re-layouts  2.02 us (2%)
    all_to_all x2, starting transfers between devices, per_device(): lax.all_to_all(term, 'z', 0, 0, axis_index_groups=ALONG_Z, tiled=True)  28.3 us
    ppermute x4, starting transfers between devices, per_device(): returned.append(lax.ppermute(products[r], ('xl', 'xh', 't'), pairs))  12.9 us
    ppermute x3, starting transfers between devices, per_device(): lax.ppermute(half_weight, 'y', [(i, i ^ e) for i in range(NY)])  11.8 us
    all_to_all x1, blocking collectives, per_device(): term = lax.all_to_all(term, ('xl', 't'), 0, 0, tiled=True)  10.7 us
    ppermute x3, waiting for transfers between devices, per_device(): lax.ppermute(half_weight, 'y', [(i, i ^ e) for i in range(NY)])  10.3 us
    all_to_all x2, waiting for transfers between devices, per_device(): lax.all_to_all(term, 'z', 0, 0, axis_index_groups=ALONG_Z, tiled=True)  8.1 us
    all_to_all x1, starting transfers between devices, per_device(): lax.all_to_all(term, 'y', 0, 0, axis_index_groups=ALONG_Y, tiled=True)  7.45 us
    all_to_all x1, waiting for transfers between devices, per_device(): got = lax.all_to_all(blocks, ('xl', 'xh'), 0, 0, tiled=True)  5.3 us
  transfers between devices with their start and end apart: 14, of which 8 were waited for; matrix products, arithmetic and copies ran while one was open for 0% of the time, Pallas kernels for 6%

profile of v6, /device:TPU:1, one launch (start us, length us, event | category | flops | bytes accessed | tf_op | source)
XLA Modules:
  0.0 133.5 jit_solution(12298132279718254973)
XLA Ops:
  0.6 4.8 %prep.1 = (bf16[4,256,1280]{2,1,0:T(8,128)(2,1)}, f32[8,128]{1,0:T(8,128)}) custom-call(s32[1,4]{1,0:T(1,128)} %doc.1, bf16[256,8192]{1,0:T(8,128)(2,1)} %act.1, f32[1,8192]{1,0:T(1,128)} %bitcast.9, bf16[256,256]{1,0:T(8,128)(2,1)} %key_grad.1), custom_call_target="tpu_custom_call" | custom-call | tf_op jit(solution)/shard_map/prep/pallas_call | solution.py:199
  5.4 0.0 copy-start.3
  5.4 0.0 copy-start.4
  5.4 5.0 %all-to-all-start = ((bf16[4,256,1280]{2,1,0:T(8,128)(2,1)}), bf16[4,256,1280]{2,1,0:T(8,128)(2,1)S(1)}, u32[]{:S(2)}, u32[]{:S(2)}) async-start(bf16[4,256,1280]{2,1,0:T(8,128)(2,1)} %get-tuple-element.11), calls=%async_computation | async-start | bytes 5242880 | tf_op jit(solution)/shard_map/all_to_all | solution.py:217
  10.4 0.0 copy-done.3
  10.4 0.0 copy-done.4
  10.4 7.5 %collective-permute-start.2 = (bf16[256,256]{1,0:T(8,128)(2,1)S(1)}, bf16[256,256]{1,0:T(8,128)(2,1)S(1)}, u32[]{:S(2)}, u32[]{:S(2)}) collective-permute-start(bf16[256,256]{1,0:T(8,128)(2,1)S(1)} %half_weight.1), channel_id=1, source_target_pairs={{0,8},{2,10},{4,12},{6,14},{8,0},{10,2},{12,4},{14,6},{1,9},{3,11}... | collective-permute-start | bytes 393224 | tf_op jit(solution)/shard_map/ppermute | solution.py:229
  17.9 2.4 %collective-permute-start.1 = (bf16[256,256]{1,0:T(8,128)(2,1)S(1)}, bf16[256,256]{1,0:T(8,128)(2,1)S(1)}, u32[]{:S(2)}, u32[]{:S(2)}) collective-permute-start(bf16[256,256]{1,0:T(8,128)(2,1)S(1)} %half_weight.1), channel_id=1, source_target_pairs={{0,4},{2,6},{4,0},{6,2},{8,12},{10,14},{12,8},{14,10},{1,5},{3,7},... | collective-permute-start | bytes 393224 | tf_op jit(solution)/shard_map/ppermute | solution.py:229
  20.3 1.9 %collective-permute-start = (bf16[256,256]{1,0:T(8,128)(2,1)S(1)}, bf16[256,256]{1,0:T(8,128)(2,1)S(1)}, u32[]{:S(2)}, u32[]{:S(2)}) collective-permute-start(bf16[256,256]{1,0:T(8,128)(2,1)S(1)} %half_weight.1), channel_id=1, source_target_pairs={{0,12},{2,14},{4,8},{6,10},{8,4},{10,6},{12,0},{14,2},{1,13},{3,15... | collective-permute-start | bytes 393224 | tf_op jit(solution)/shard_map/ppermute | solution.py:229
  22.2 0.0 collective-permute-done.2
  22.2 8.7 %collective-permute-done.1 = bf16[256,256]{1,0:T(8,128)(2,1)S(1)} collective-permute-done((bf16[256,256]{1,0:T(8,128)(2,1)S(1)}, bf16[256,256]{1,0:T(8,128)(2,1)S(1)}, u32[]{:S(2)}, u32[]{:S(2)}) %collective-permute-start.1) | collective-permute-done | bytes 131104 | tf_op jit(solution)/shard_map/ppermute | solution.py:229
  30.9 1.6 %collective-permute-done = bf16[256,256]{1,0:T(8,128)(2,1)S(1)} collective-permute-done((bf16[256,256]{1,0:T(8,128)(2,1)S(1)}, bf16[256,256]{1,0:T(8,128)(2,1)S(1)}, u32[]{:S(2)}, u32[]{:S(2)}) %collective-permute-start) | collective-permute-done | bytes 131104 | tf_op jit(solution)/shard_map/ppermute | solution.py:229
  32.5 0.1 pad_maximum_fusion.after.near
  32.6 1.9 %collective-permute-start.4 = (bf16[4,256,256]{2,1,0:T(8,128)(2,1)S(1)}, bf16[4,256,256]{2,1,0:T(8,128)(2,1)}, u32[]{:S(2)}, u32[]{:S(2)}) collective-permute-start(bf16[4,256,256]{2,1,0:T(8,128)(2,1)S(1)} %pad_maximum_fusion.after.near), channel_id=1, source_target_pairs={{0,2},{2,0},{4,6},{6,4},{8,10},{10,8},{12,14},{14,12},{1,3},{3,1},... | collective-permute-start | bytes 1572872 | tf_op jit(solution)/shard_map/ppermute | solution.py:231
  34.5 5.3 %all-to-all-done.got = bf16[4,256,1280]{2,1,0:T(8,128)(2,1)S(1)} async-done(((bf16[4,256,1280]{2,1,0:T(8,128)(2,1)}), bf16[4,256,1280]{2,1,0:T(8,128)(2,1)S(1)}, u32[]{:S(2)}, u32[]{:S(2)}) %all-to-all-start) | async-done | bytes 2621472 | tf_op jit(solution)/shard_map/all_to_all | solution.py:217
  39.8 0.0 copy-start
  39.9 5.1 %collective-permute-start.3 = (bf16[4,256,256]{2,1,0:T(8,128)(2,1)S(1)}, bf16[4,256,256]{2,1,0:T(8,128)(2,1)S(1)}, u32[]{:S(2)}, u32[]{:S(2)}) collective-permute-start(bf16[4,256,256]{2,1,0:T(8,128)(2,1)S(1)} %pack.1.mine), channel_id=1, source_target_pairs={{0,1},{1,0},{2,3},{3,2},{4,5},{5,4},{6,7},{7,6},{8,9},{9,8},{10,11... | collective-permute-start | bytes 1572872 | tf_op jit(solution)/shard_map/ppermute | solution.py:242
  45.0 0.7 own_grad.1.own
  45.7 0.0 collective-permute-done.4.after.far
  45.7 0.0 copy-done
  45.7 0.8 collective-permute-done.3.other
  46.5 0.7 weight_grad.1
  47.2 0.0 copy-start.2
  47.2 1.0 copy-done.2
  48.2 7.5 %all-to-all-start.1 = ((bf16[8,512,128]{2,1,0:T(8,128)(2,1)}), bf16[8,512,128]{2,1,0:T(8,128)(2,1)S(1)}, u32[]{:S(2)}, u32[]{:S(2)}) async-start(bf16[8,512,128]{2,1,0:T(8,128)(2,1)} %copy-done.2), calls=%async_computation.1 | async-start | bytes 2097152 | tf_op jit(solution)/shard_map/all_to_all | solution.py:293
  55.7 1.0 copy-done.1
  56.7 1.1 to_other.1
  57.8 2.8 %collective-permute-start.5 = (bf16[2048,256]{1,0:T(8,128)(2,1)S(1)}, bf16[2048,256]{1,0:T(8,128)(2,1)S(1)}, u32[]{:S(2)}, u32[]{:S(2)}) collective-permute-start(bf16[2048,256]{1,0:T(8,128)(2,1)S(1)} %to_other.1), channel_id=1, source_target_pairs={{0,1},{1,0},{2,3},{3,2},{4,5},{5,4},{6,7},{7,6},{8,9},{9,8},{10,11... | collective-permute-start | bytes 3145736 | tf_op jit(solution)/shard_map/ppermute | solution.py:269
  60.6 2.3 %collective-permute-done.5.other = bf16[2048,256]{1,0:T(8,128)(2,1)S(1)} collective-permute-done((bf16[2048,256]{1,0:T(8,128)(2,1)S(1)}, bf16[2048,256]{1,0:T(8,128)(2,1)S(1)}, u32[]{:S(2)}, u32[]{:S(2)}) %collective-permute-start.5) | collective-permute-done | bytes 1048608 | tf_op jit(solution)/shard_map/ppermute | solution.py:269
  62.9 3.6 %input_grad.1 = (bf16[256,1024]{1,0:T(8,128)(2,1)}, bf16[256,1024]{1,0:T(8,128)(2,1)}, bf16[256,1024]{1,0:T(8,128)(2,1)}, bf16[256,1024]{1,0:T(8,128)(2,1)}, f32[8,128]{1,0:T(8,128)S(1)}) custom-call(bf16[4,256,256]{2,1,0:T(8,128)(2,1)S(1)} %copy-done.1, bf16[4,256,256]{2,1,0:T(8,128)(2,1)S(1)} %pad_maximum_fusion.after.near, ...), custom_call_target="tpu_custom_call" | custom-call | tf_op jit(solution)/shard_map/input_grad/pallas_call | solution.py:271
  66.5 4.6 %collective-permute-start.6 = (bf16[256,1024]{1,0:T(8,128)(2,1)}, bf16[256,1024]{1,0:T(8,128)(2,1)S(1)}, u32[]{:S(2)}, u32[]{:S(2)}) collective-permute-start(bf16[256,1024]{1,0:T(8,128)(2,1)} %get-tuple-element.14), channel_id=1, source_target_pairs={{0,0},{1,16},{16,1},{17,17},{32,32},{33,48},{48,33},{49,49},{2,2},... | collective-permute-start | bytes 1572872 | tf_op jit(solution)/shard_map/ppermute | solution.py:291
  71.0 1.9 %collective-permute-start.7 = (bf16[256,1024]{1,0:T(8,128)(2,1)}, bf16[256,1024]{1,0:T(8,128)(2,1)S(1)}, u32[]{:S(2)}, u32[]{:S(2)}) collective-permute-start(bf16[256,1024]{1,0:T(8,128)(2,1)} %get-tuple-element.15), channel_id=1, source_target_pairs={{0,16},{1,0},{16,17},{17,1},{32,48},{33,32},{48,49},{49,33},{2,18}... | collective-permute-start | bytes 1572872 | tf_op jit(solution)/shard_map/ppermute | solution.py:291
  73.0 2.8 %collective-permute-start.8 = (bf16[256,1024]{1,0:T(8,128)(2,1)}, bf16[256,1024]{1,0:T(8,128)(2,1)S(1)}, u32[]{:S(2)}, u32[]{:S(2)}) collective-permute-start(bf16[256,1024]{1,0:T(8,128)(2,1)} %get-tuple-element.16), channel_id=1, source_target_pairs={{0,32},{1,48},{16,33},{17,49},{32,0},{33,16},{48,1},{49,17},{2,34}... | collective-permute-start | bytes 1572872 | tf_op jit(solution)/shard_map/ppermute | solution.py:291
  75.8 3.6 %collective-permute-start.9 = (bf16[256,1024]{1,0:T(8,128)(2,1)}, bf16[256,1024]{1,0:T(8,128)(2,1)S(1)}, u32[]{:S(2)}, u32[]{:S(2)}) collective-permute-start(bf16[256,1024]{1,0:T(8,128)(2,1)} %get-tuple-element.17), channel_id=1, source_target_pairs={{0,48},{1,32},{16,49},{17,33},{32,16},{33,0},{48,17},{49,1},{2,50}... | collective-permute-start | bytes 1572872 | tf_op jit(solution)/shard_map/ppermute | solution.py:291
  79.4 2.4 %all-to-all-done.1.term = bf16[8,512,128]{2,1,0:T(8,128)(2,1)S(1)} async-done(((bf16[8,512,128]{2,1,0:T(8,128)(2,1)}), bf16[8,512,128]{2,1,0:T(8,128)(2,1)S(1)}, u32[]{:S(2)}, u32[]{:S(2)}) %all-to-all-start.1) | async-done | bytes 1048608 | tf_op jit(solution)/shard_map/all_to_all | solution.py:293
  81.9 0.8 sum_y.1
  82.7 18.8 %all-to-all-start.2 = ((bf16[12,2,24,128]{3,2,1,0:T(8,128)(2,1)}), bf16[12,2,24,128]{3,2,1,0:T(8,128)(2,1)S(1)}, u32[]{:S(2)}, u32[]{:S(2)}) async-start(bf16[12,2,24,128]{3,2,1,0:T(8,128)(2,1)} %sum_y.1), calls=%async_computation.2 | async-start | bytes 294912 | tf_op jit(solution)/shard_map/all_to_all | solution.py:302
  101.4 0.0 collective-permute-done.6.after0.r0
  101.4 0.0 collective-permute-done.7.after1.r1
  101.4 0.0 collective-permute-done.8.after2.r2
  101.4 0.0 collective-permute-done.9.after3.r3
  101.4 5.4 %all-to-all-done.2.term = bf16[12,2,24,128]{3,2,1,0:T(8,128)(2,1)S(1)} async-done(((bf16[12,2,24,128]{3,2,1,0:T(8,128)(2,1)}), bf16[12,2,24,128]{3,2,1,0:T(8,128)(2,1)S(1)}, u32[]{:S(2)}, u32[]{:S(2)}) %all-to-all-start.2) | async-done | bytes 147488 | tf_op jit(solution)/shard_map/all_to_all | solution.py:302
  106.8 0.7 sum_z.1
  107.5 9.5 %all-to-all-start.3 = ((bf16[12,2,24,128]{3,2,1,0:T(8,128)(2,1)}), bf16[12,2,24,128]{3,2,1,0:T(8,128)(2,1)S(1)}, u32[]{:S(2)}, u32[]{:S(2)}) async-start(bf16[12,2,24,128]{3,2,1,0:T(8,128)(2,1)} %sum_z.1), calls=%async_computation.3 | async-start | bytes 294912 | tf_op jit(solution)/shard_map/all_to_all | solution.py:325
  117.1 2.1 %placed.1 = (bf16[256,4096]{1,0:T(8,128)(2,1)}, f32[8,128]{1,0:T(8,128)S(1)}) custom-call(bf16[256,1024]{1,0:T(8,128)(2,1)S(1)} %collective-permute-done.6.after0.r0, bf16[256,1024]{1,0:T(8,128)(2,1)S(1)} %collective-permute-done.7.after1.r1, bf16[256,1024]{1,0:T(8,128)(2,1)S(1)} %collective-permute-done.8.after2.r2, ...), custom_call_target="tpu_custom_call" | custom-call | tf_op jit(solution)/shard_map/placed/pallas_call | solution.py:304
  119.2 2.7 %all-to-all-done.3.term = bf16[12,2,24,128]{3,2,1,0:T(8,128)(2,1)S(1)} async-done(((bf16[12,2,24,128]{3,2,1,0:T(8,128)(2,1)}), bf16[12,2,24,128]{3,2,1,0:T(8,128)(2,1)S(1)}, u32[]{:S(2)}, u32[]{:S(2)}) %all-to-all-start.3) | async-done | bytes 147488 | tf_op jit(solution)/shard_map/all_to_all | solution.py:325
  121.9 10.7 %all_to_all.25.term = bf16[4,12,24,128]{3,2,1,0:T(8,128)(2,1)S(1)} all-to-all(bf16[4,12,24,128]{3,2,1,0:T(8,128)(2,1)S(1)} %split.1), channel_id=1, replica_groups=mesh['z'=12,'xl'=2,'xh'=2,'y'=8,'t'=2] {'xl','t'}, dimensions={0} | all-to-all | bytes 589824 | tf_op jit(solution)/shard_map/all_to_all | solution.py:334
  132.6 0.9 turn.1
  (4 shorter events, 0.1 us)
Async XLA Ops:
  5.4 5.0 %copy-start.3 = (bf16[512,256]{1,0:T(8,128)(2,1)S(1)}, bf16[512,256]{1,0:T(8,128)(2,1)}, u32[]{:S(2)}) copy-start(bf16[512,256]{1,0:T(8,128)(2,1)} %weight.1) | copy-start | bytes 786436
  5.4 5.0 %copy-start.4 = (f32[8,128]{1,0:T(8,128)S(1)}, f32[8,128]{1,0:T(8,128)}, u32[]{:S(2)}) copy-start(f32[8,128]{1,0:T(8,128)} %get-tuple-element.12.after) | copy-start | bytes 12292
  5.4 34.4 %all-to-all-start = ((bf16[4,256,1280]{2,1,0:T(8,128)(2,1)}), bf16[4,256,1280]{2,1,0:T(8,128)(2,1)S(1)}, u32[]{:S(2)}, u32[]{:S(2)}) async-start(bf16[4,256,1280]{2,1,0:T(8,128)(2,1)} %get-tuple-element.11), calls=%async_computation | async-start | bytes 5242880 | tf_op jit(solution)/shard_map/all_to_all | solution.py:217
  10.4 11.8 %collective-permute-start.2 = (bf16[256,256]{1,0:T(8,128)(2,1)S(1)}, bf16[256,256]{1,0:T(8,128)(2,1)S(1)}, u32[]{:S(2)}, u32[]{:S(2)}) collective-permute-start(bf16[256,256]{1,0:T(8,128)(2,1)S(1)} %half_weight.1), channel_id=1, source_target_pairs={{0,8},{2,10},{4,12},{6,14},{8,0},{10,2},{12,4},{14,6},{1,9},{3,11}... | collective-permute-start | bytes 393224 | tf_op jit(solution)/shard_map/ppermute | solution.py:229
  17.9 13.0 %collective-permute-start.1 = (bf16[256,256]{1,0:T(8,128)(2,1)S(1)}, bf16[256,256]{1,0:T(8,128)(2,1)S(1)}, u32[]{:S(2)}, u32[]{:S(2)}) collective-permute-start(bf16[256,256]{1,0:T(8,128)(2,1)S(1)} %half_weight.1), channel_id=1, source_target_pairs={{0,4},{2,6},{4,0},{6,2},{8,12},{10,14},{12,8},{14,10},{1,5},{3,7},... | collective-permute-start | bytes 393224 | tf_op jit(solution)/shard_map/ppermute | solution.py:229
  20.3 12.2 %collective-permute-start = (bf16[256,256]{1,0:T(8,128)(2,1)S(1)}, bf16[256,256]{1,0:T(8,128)(2,1)S(1)}, u32[]{:S(2)}, u32[]{:S(2)}) collective-permute-start(bf16[256,256]{1,0:T(8,128)(2,1)S(1)} %half_weight.1), channel_id=1, source_target_pairs={{0,12},{2,14},{4,8},{6,10},{8,4},{10,6},{12,0},{14,2},{1,13},{3,15... | collective-permute-start | bytes 393224 | tf_op jit(solution)/shard_map/ppermute | solution.py:229
  32.6 13.1 %collective-permute-start.4 = (bf16[4,256,256]{2,1,0:T(8,128)(2,1)S(1)}, bf16[4,256,256]{2,1,0:T(8,128)(2,1)}, u32[]{:S(2)}, u32[]{:S(2)}) collective-permute-start(bf16[4,256,256]{2,1,0:T(8,128)(2,1)S(1)} %pad_maximum_fusion.after.near), channel_id=1, source_target_pairs={{0,2},{2,0},{4,6},{6,4},{8,10},{10,8},{12,14},{14,12},{1,3},{3,1},... | collective-permute-start | bytes 1572872 | tf_op jit(solution)/shard_map/ppermute | solution.py:231
  39.8 5.9 %copy-start = (bf16[4,256,256]{2,1,0:T(8,128)(2,1)}, bf16[4,256,256]{2,1,0:T(8,128)(2,1)S(1)}, u32[]{:S(2)}) copy-start(bf16[4,256,256]{2,1,0:T(8,128)(2,1)S(1)} %pack.1.mine) | copy-start | bytes 1572868
  39.9 6.6 %collective-permute-start.3 = (bf16[4,256,256]{2,1,0:T(8,128)(2,1)S(1)}, bf16[4,256,256]{2,1,0:T(8,128)(2,1)S(1)}, u32[]{:S(2)}, u32[]{:S(2)}) collective-permute-start(bf16[4,256,256]{2,1,0:T(8,128)(2,1)S(1)} %pack.1.mine), channel_id=1, source_target_pairs={{0,1},{1,0},{2,3},{3,2},{4,5},{5,4},{6,7},{7,6},{8,9},{9,8},{10,11... | collective-permute-start | bytes 1572872 | tf_op jit(solution)/shard_map/ppermute | solution.py:242
  47.2 1.0 copy-start.2
  48.2 33.7 %all-to-all-start.1 = ((bf16[8,512,128]{2,1,0:T(8,128)(2,1)}), bf16[8,512,128]{2,1,0:T(8,128)(2,1)S(1)}, u32[]{:S(2)}, u32[]{:S(2)}) async-start(bf16[8,512,128]{2,1,0:T(8,128)(2,1)} %copy-done.2), calls=%async_computation.1 | async-start | bytes 2097152 | tf_op jit(solution)/shard_map/all_to_all | solution.py:293
  55.6 1.0 copy-start.1
  57.8 5.1 %collective-permute-start.5 = (bf16[2048,256]{1,0:T(8,128)(2,1)S(1)}, bf16[2048,256]{1,0:T(8,128)(2,1)S(1)}, u32[]{:S(2)}, u32[]{:S(2)}) collective-permute-start(bf16[2048,256]{1,0:T(8,128)(2,1)S(1)} %to_other.1), channel_id=1, source_target_pairs={{0,1},{1,0},{2,3},{3,2},{4,5},{5,4},{6,7},{7,6},{8,9},{9,8},{10,11... | collective-permute-start | bytes 3145736 | tf_op jit(solution)/shard_map/ppermute | solution.py:269
  66.5 34.9 %collective-permute-start.6 = (bf16[256,1024]{1,0:T(8,128)(2,1)}, bf16[256,1024]{1,0:T(8,128)(2,1)S(1)}, u32[]{:S(2)}, u32[]{:S(2)}) collective-permute-start(bf16[256,1024]{1,0:T(8,128)(2,1)} %get-tuple-element.14), channel_id=1, source_target_pairs={{0,0},{1,16},{16,1},{17,17},{32,32},{33,48},{48,33},{49,49},{2,2},... | collective-permute-start | bytes 1572872 | tf_op jit(solution)/shard_map/ppermute | solution.py:291
  71.0 30.4 %collective-permute-start.7 = (bf16[256,1024]{1,0:T(8,128)(2,1)}, bf16[256,1024]{1,0:T(8,128)(2,1)S(1)}, u32[]{:S(2)}, u32[]{:S(2)}) collective-permute-start(bf16[256,1024]{1,0:T(8,128)(2,1)} %get-tuple-element.15), channel_id=1, source_target_pairs={{0,16},{1,0},{16,17},{17,1},{32,48},{33,32},{48,49},{49,33},{2,18}... | collective-permute-start | bytes 1572872 | tf_op jit(solution)/shard_map/ppermute | solution.py:291
  73.0 28.5 %collective-permute-start.8 = (bf16[256,1024]{1,0:T(8,128)(2,1)}, bf16[256,1024]{1,0:T(8,128)(2,1)S(1)}, u32[]{:S(2)}, u32[]{:S(2)}) collective-permute-start(bf16[256,1024]{1,0:T(8,128)(2,1)} %get-tuple-element.16), channel_id=1, source_target_pairs={{0,32},{1,48},{16,33},{17,49},{32,0},{33,16},{48,1},{49,17},{2,34}... | collective-permute-start | bytes 1572872 | tf_op jit(solution)/shard_map/ppermute | solution.py:291
  75.8 25.6 %collective-permute-start.9 = (bf16[256,1024]{1,0:T(8,128)(2,1)}, bf16[256,1024]{1,0:T(8,128)(2,1)S(1)}, u32[]{:S(2)}, u32[]{:S(2)}) collective-permute-start(bf16[256,1024]{1,0:T(8,128)(2,1)} %get-tuple-element.17), channel_id=1, source_target_pairs={{0,48},{1,32},{16,49},{17,33},{32,16},{33,0},{48,17},{49,1},{2,50}... | collective-permute-start | bytes 1572872 | tf_op jit(solution)/shard_map/ppermute | solution.py:291
  82.7 24.2 %all-to-all-start.2 = ((bf16[12,2,24,128]{3,2,1,0:T(8,128)(2,1)}), bf16[12,2,24,128]{3,2,1,0:T(8,128)(2,1)S(1)}, u32[]{:S(2)}, u32[]{:S(2)}) async-start(bf16[12,2,24,128]{3,2,1,0:T(8,128)(2,1)} %sum_y.1), calls=%async_computation.2 | async-start | bytes 294912 | tf_op jit(solution)/shard_map/all_to_all | solution.py:302
  107.5 14.3 %all-to-all-start.3 = ((bf16[12,2,24,128]{3,2,1,0:T(8,128)(2,1)}), bf16[12,2,24,128]{3,2,1,0:T(8,128)(2,1)S(1)}, u32[]{:S(2)}, u32[]{:S(2)}) async-start(bf16[12,2,24,128]{3,2,1,0:T(8,128)(2,1)} %sum_z.1), calls=%async_computation.3 | async-start | bytes 294912 | tf_op jit(solution)/shard_map/all_to_all | solution.py:325
